TPU v7x, 32 devices: a whole 2x2x4 slice. The times are simulated.
32 devices in a mesh: grp: 2 (over x), head: 8 (over z, y), ctx: 2 (over core).
Axes of the slice: x: 2, y: 2, z: 4, core: 2. Of those that a mesh axis runs over, the one named last changes fastest.
Arguments:
- x_seq: bfloat16 [4096, 4096], P(('grp', 'ctx', 'head')), parts along dimension 0, may hold values from -6 to 6
- dy_seq: bfloat16 [4096, 4096], P(('grp', 'ctx', 'head')), parts along dimension 0, may hold values from -0.59765625 to 0.59765625
- dt_seq: bfloat16 [4096, 64], P(('grp', 'ctx', 'head')), parts along dimension 0, may hold values from 0.5 to 2
- a_log: float32 [64], replicated, may hold values from -13 to -2.9
- b_seq: bfloat16 [4096, 8, 128], P(('grp', 'ctx', 'head')), parts along dimension 0, may hold values from -0.5 to 0.5
- c_seq: bfloat16 [4096, 8, 128], P(('grp', 'ctx', 'head')), parts along dimension 0, may hold values from -0.5 to 0.5
Outputs:
- dx_seq: bfloat16 [4096, 4096], P(('grp', 'ctx', 'head')), parts along dimension 0
- ddt_seq: bfloat16 [4096, 64], P(('grp', 'ctx', 'head')), parts along dimension 0
- db_seq: bfloat16 [4096, 8, 128], P(('grp', 'ctx', 'head')), parts along dimension 0
- dc_seq: bfloat16 [4096, 8, 128], P(('grp', 'ctx', 'head')), parts along dimension 0
There are 2 independent parts, one for each index of `grp`. A program takes and returns all parts, laid end to end along the dimension named above; an argument that names none is the same for every part. Nothing has to cross between parts.
All inputs are finite; a program needn't handle non-finite values.
Results may differ from a plain program's by a relative error of at most 0.001.
Values may be sent and summed in bfloat16 or wider, within the bound.
No kernel may reach another device: no remote copies, remote signals or barrier semaphores. Data moves between devices by JAX's collectives and lax.ppermute only.
A program may use at most 128 MiB of HBM per device.

v0:
```python
import jax
import jax.numpy as jnp
import numpy as np
from jax import lax
from jax.sharding import PartitionSpec as P

HEADS = 64
HEAD_DIM = 64
STATE = 128
GROUPS = 8
STRETCH = 256


highest = lax.Precision.HIGHEST


def carried_in(value, axis, join, neutral, backward):
    count, mine = (lax.axis_size(axis), lax.axis_index(axis))
    pieces = jax.tree.map(lambda part: lax.all_gather(part, axis), value)
    if backward:
        pieces = jax.tree.map(lambda part: part[::-1], pieces)
        mine = count - 1 - mine
    total = jax.tree.map(
        lambda part, zero: jnp.full_like(part, 0) + jnp.asarray(zero, part.dtype), value, neutral
    )

    def lap(position, total):
        longer = join(total, jax.tree.map(lambda part: part[position], pieces))
        return jax.tree.map(lambda new, old: jnp.where(position < mine, new, old), longer, total)

    return lax.fori_loop(0, count - 1, lap, total)


def stretch_local(x_head, dy_head, dt_head, b_head, c_head, decay_rate):
    dt_full = dt_head.astype(jnp.float32)
    cum_log = jnp.cumsum(dt_full * decay_rate, axis=1)
    end_log = cum_log[:, -1]
    to_end = jnp.exp(end_log[:, None] - cum_log)
    from_start = jnp.exp(cum_log)
    x_scaled = dt_full[..., None] * x_head.astype(jnp.float32)
    states_loc = jnp.einsum(
        "cqp,cqn->cpn", x_scaled * to_end[..., None], b_head.astype(jnp.float32), precision=highest
    )
    grads_loc = jnp.einsum(
        "cqp,cqn->cpn",
        dy_head.astype(jnp.float32) * from_start[..., None],
        c_head.astype(jnp.float32),
        precision=highest,
    )
    return (cum_log, states_loc, grads_loc)


def chains(end_log, states_loc, grads_loc):
    factor = jnp.exp(end_log)
    zero_state = jnp.zeros(states_loc.shape[1:], jnp.float32)

    def forward(carry, item):
        return (item[0] * carry + item[1], carry)

    def backward(carry, item):
        return (item[0] * carry + item[1], carry)

    state_out, state_in = lax.scan(forward, zero_state, (factor, states_loc))
    grad_out, grad_in = lax.scan(backward, zero_state, (factor, grads_loc), reverse=True)
    return (state_in, grad_in, state_out, grad_out)


def stretch_grads(x_head, dy_head, dt_head, b_head, c_head, decay_rate, cum_log, state_in, grad_in):
    dt_full = dt_head.astype(jnp.float32)
    x_wide = x_head.astype(jnp.float32)
    dy_wide = dy_head.astype(jnp.float32)
    b_wide = b_head.astype(jnp.float32)
    c_wide = c_head.astype(jnp.float32)
    x_scaled = dt_full[..., None] * x_wide
    end_log = cum_log[:, -1]
    to_end = jnp.exp(end_log[:, None] - cum_log)
    from_start = jnp.exp(cum_log)
    span = cum_log.shape[1]
    lower_mask = jnp.arange(span)[:, None] >= jnp.arange(span)[None, :]
    log_gap = cum_log[:, :, None] - cum_log[:, None, :]
    decay_mat = jnp.where(lower_mask, jnp.exp(jnp.minimum(log_gap, 0.0)), 0.0)
    k_one = (
        jnp.einsum("cip,cjp->cij", dy_head, x_head, preferred_element_type=jnp.float32)
        * dt_full[:, None, :]
    )
    k_two = jnp.einsum("cin,cjn->cij", c_head, b_head, preferred_element_type=jnp.float32)
    a_one = decay_mat * k_one
    a_two = decay_mat * k_two
    b_state = jnp.einsum("cin,cpn->cip", b_wide, grad_in, precision=highest)
    c_state = jnp.einsum("cin,cpn->cip", c_wide, state_in, precision=highest)
    dxbar = (
        jnp.einsum("cki,ckp->cip", a_two, dy_wide, precision=highest) + to_end[..., None] * b_state
    )
    dcol = from_start[..., None] * jnp.einsum("cip,cpn->cin", dy_wide, state_in, precision=highest)
    dcol = dcol + jnp.einsum("cij,cjn->cin", a_one, b_wide, precision=highest)
    drow = jnp.einsum("cki,ckn->cin", a_one, c_wide, precision=highest)
    drow = drow + to_end[..., None] * jnp.einsum(
        "cip,cpn->cin", x_scaled, grad_in, precision=highest
    )
    box_terms = a_one * k_two
    col_sums = jnp.sum(box_terms, axis=1)
    row_sums = jnp.sum(box_terms, axis=2)
    box_sum = jnp.cumsum(col_sums, axis=1) - jnp.cumsum(row_sums, axis=1) + row_sums
    later_terms = from_start * jnp.sum(dy_wide * c_state, axis=-1)
    early_terms = to_end * jnp.sum(x_scaled * b_state, axis=-1)
    suffix_sum = jnp.flip(jnp.cumsum(jnp.flip(later_terms, 1), axis=1), 1)
    head_sum = jnp.cumsum(early_terms, axis=1)
    corner = jnp.exp(end_log) * jnp.sum(grad_in * state_in, axis=(1, 2))
    dlog_step = (
        box_sum + suffix_sum + head_sum + corner[:, None] - jnp.sum(dxbar * x_scaled, axis=-1)
    )
    grad_dt = jnp.sum(dxbar * x_wide, axis=-1) + decay_rate * dlog_step
    return (dt_full[..., None] * dxbar, grad_dt, drow, dcol)


def combine(earlier, later):
    return (earlier[0] * later[0], later[0][:, None, None] * earlier[1] + later[1])


def on_device(x_seq, dy_seq, dt_seq, a_log, b_seq, c_seq):
    tokens_here = x_seq.shape[0]
    head_count = lax.axis_size("head")
    per_device = HEADS // head_count
    group_here = max(GROUPS // head_count, 1)
    copies = max(head_count // GROUPS, 1)
    b_spread = jnp.repeat(b_seq, copies, axis=1)
    c_spread = jnp.repeat(c_seq, copies, axis=1)
    x_loc, dy_loc, dt_loc, b_loc, c_loc = (
        lax.all_to_all(x_seq, "head", split_axis=1, concat_axis=0, tiled=True),
        lax.all_to_all(dy_seq, "head", split_axis=1, concat_axis=0, tiled=True),
        lax.all_to_all(dt_seq, "head", split_axis=1, concat_axis=0, tiled=True),
        lax.all_to_all(b_spread, "head", split_axis=1, concat_axis=0, tiled=True),
        lax.all_to_all(c_spread, "head", split_axis=1, concat_axis=0, tiled=True),
    )
    segment = x_loc.shape[0]
    count = segment // STRETCH
    first_head = lax.axis_index("head") * per_device
    rates = -jnp.exp(lax.dynamic_slice_in_dim(a_log, first_head, per_device))
    x_heads = x_loc.reshape(count, STRETCH, per_device, HEAD_DIM).transpose(2, 0, 1, 3)
    dy_heads = dy_loc.reshape(count, STRETCH, per_device, HEAD_DIM).transpose(2, 0, 1, 3)
    dt_heads = dt_loc.reshape(count, STRETCH, per_device).transpose(2, 0, 1)
    pick = np.array(
        [member * group_here // per_device for member in range(per_device)], dtype=np.int32
    )
    b_groups = b_loc.reshape(count, STRETCH, group_here, STATE).transpose(2, 0, 1, 3)
    c_groups = c_loc.reshape(count, STRETCH, group_here, STATE).transpose(2, 0, 1, 3)
    b_heads = jnp.take(b_groups, pick, axis=0)
    c_heads = jnp.take(c_groups, pick, axis=0)
    cum_log, states_loc, grads_loc = jax.vmap(stretch_local)(
        x_heads, dy_heads, dt_heads, b_heads, c_heads, rates
    )
    end_log = cum_log[:, :, -1]
    state_zero, grad_zero, state_out, grad_out = jax.vmap(chains)(end_log, states_loc, grads_loc)
    running = jnp.cumsum(end_log, axis=1)
    total_log = running[:, -1]
    through = jnp.exp(total_log)
    before = jnp.exp(running - end_log)
    after = jnp.exp(total_log[:, None] - running)
    blank = jnp.zeros_like(state_out)
    units = jnp.ones_like(through)
    state_dev = carried_in((through, state_out), "ctx", combine, (units, blank), False)[1]
    grad_dev = carried_in((through, grad_out), "ctx", combine, (units, blank), True)[1]
    state_in = state_zero + before[..., None, None] * state_dev[:, None]
    grad_in = grad_zero + after[..., None, None] * grad_dev[:, None]

    def per_head(item):
        return stretch_grads(*item)

    dx_h, ddt_h, db_h, dc_h = lax.map(
        per_head, (x_heads, dy_heads, dt_heads, b_heads, c_heads, rates, cum_log, state_in, grad_in)
    )
    dx_local = (
        dx_h.transpose(1, 2, 0, 3).reshape(segment, per_device * HEAD_DIM).astype(jnp.bfloat16)
    )
    ddt_local = ddt_h.transpose(1, 2, 0).reshape(segment, per_device).astype(jnp.bfloat16)
    inner = per_device // group_here
    db_group = (
        db_h.reshape(group_here, inner, count, STRETCH, STATE)
        .sum(1)
        .transpose(1, 2, 0, 3)
        .reshape(segment, group_here, STATE)
        .astype(jnp.bfloat16)
    )
    dc_group = (
        dc_h.reshape(group_here, inner, count, STRETCH, STATE)
        .sum(1)
        .transpose(1, 2, 0, 3)
        .reshape(segment, group_here, STATE)
        .astype(jnp.bfloat16)
    )
    dx_back, ddt_back = (
        lax.all_to_all(dx_local, "head", split_axis=0, concat_axis=1, tiled=True),
        lax.all_to_all(ddt_local, "head", split_axis=0, concat_axis=1, tiled=True),
    )
    db_wide, dc_wide = (
        lax.all_to_all(db_group, "head", split_axis=0, concat_axis=1, tiled=True),
        lax.all_to_all(dc_group, "head", split_axis=0, concat_axis=1, tiled=True),
    )
    db_total = db_wide.astype(jnp.float32).reshape(tokens_here, GROUPS, copies, STATE).sum(2)
    dc_total = dc_wide.astype(jnp.float32).reshape(tokens_here, GROUPS, copies, STATE).sum(2)
    return (dx_back, ddt_back, db_total.astype(jnp.bfloat16), dc_total.astype(jnp.bfloat16))


def solution(mesh):
    in_specs = (
        P(("grp", "ctx", "head"), None),
        P(("grp", "ctx", "head"), None),
        P(("grp", "ctx", "head"), None),
        P(),
        P(("grp", "ctx", "head"), None, None),
        P(("grp", "ctx", "head"), None, None),
    )
    out_specs = (
        P(("grp", "ctx", "head"), None),
        P(("grp", "ctx", "head"), None),
        P(("grp", "ctx", "head"), None, None),
        P(("grp", "ctx", "head"), None, None),
    )
    return jax.shard_map(
        on_device, mesh=mesh, in_specs=in_specs, out_specs=out_specs, check_vma=False
    )
```

profile of v0, /device:TPU:0, one launch (start us, length us, event | category | flops | bytes accessed | tf_op | source)
XLA Modules:
  0.0 413.8 jit_solution(3703721364513627049)
XLA Ops:
  0.6 7.3 %all-to-all-start = ((bf16[128,8,8]{0,2,1:T(8,128)(2,1)}), bf16[128,8,8]{0,2,1:T(8,128)(2,1)S(1)}, u32[]{:S(2)}, u32[]{:S(2)}) async-start(bf16[128,8,8]{0,2,1:T(8,128)(2,1)} %bitcast.356), calls=%async_computation | async-start | bytes 32768 | tf_op jit(solution)/shard_map/all_to_all | solution.py:131
  9.6 4.9 %all-to-all-done = bf16[128,8,8]{0,2,1:T(8,128)(2,1)S(1)} async-done(((bf16[128,8,8]{0,2,1:T(8,128)(2,1)}), bf16[128,8,8]{0,2,1:T(8,128)(2,1)S(1)}, u32[]{:S(2)}, u32[]{:S(2)}) %all-to-all-start) | async-done | bytes 16416 | tf_op jit(solution)/shard_map/all_to_all | solution.py:131
  14.5 3.4 all-to-all-start.2
  20.4 5.7 %all-to-all-done.2 = bf16[128,8,128]{2,0,1:T(8,128)(2,1)S(1)} async-done(((bf16[128,8,128]{2,0,1:T(8,128)(2,1)}), bf16[128,8,128]{2,0,1:T(8,128)(2,1)S(1)}, u32[]{:S(2)}, u32[]{:S(2)}) %all-to-all-start.2) | async-done | bytes 262176 | tf_op jit(solution)/shard_map/all_to_all | solution.py:132
  26.1 3.7 all-to-all-start.4
  36.5 17.2 %all-to-all-done.4 = bf16[128,8,512]{0,2,1:T(8,128)(2,1)S(1)} async-done(((bf16[128,8,512]{0,2,1:T(8,128)(2,1)}), bf16[128,8,512]{0,2,1:T(8,128)(2,1)S(1)}, u32[]{:S(2)}, u32[]{:S(2)}) %all-to-all-start.4) | async-done | bytes 1048608 | tf_op jit(solution)/shard_map/all_to_all | solution.py:129
  53.7 3.6 all-to-all-start.3
  62.0 2.5 reshape.275
  67.6 15.2 %all-to-all-done.3 = bf16[128,8,512]{0,2,1:T(8,128)(2,1)S(1)} async-done(((bf16[128,8,512]{0,2,1:T(8,128)(2,1)}), bf16[128,8,512]{0,2,1:T(8,128)(2,1)S(1)}, u32[]{:S(2)}, u32[]{:S(2)}) %all-to-all-start.3) | async-done | bytes 1048608 | tf_op jit(solution)/shard_map/all_to_all | solution.py:130
  82.8 3.4 all-to-all-start.1
  87.4 3.4 while.58
  95.3 3.0 convert_multiply_fusion.3
  98.3 3.0 fusion.65
  102.5 3.4 while.57
  106.0 2.5 all-gather.1
  113.4 230.8 %while.56 = (s32[]{:T(128)}, bf16[8,4,256,64]{2,3,1,0:T(8,128)(2,1)}, bf16[8,4,256]{2,1,0:T(4,128)(2,1)}, f32[8,4,256,128]{3,2,1,0:T(8,128)}, f32[8,4,256,128]{3...) while((s32[]{:T(128)}, ...), condition=%wide.region_23.25_spmd, body=%wide.region_7.24_spmd.sunk | while | flops 1515330560 | bytes 15286049 | solution.py:169
  122.5 2.8 fusion.124
  151.3 2.8 fusion.124
  180.2 2.8 fusion.124
  209.1 2.8 fusion.124
  237.9 2.8 fusion.124
  266.8 2.8 fusion.124
  295.6 2.8 fusion.124
  324.5 2.8 fusion.124
  345.5 6.0 %all-to-all-start.6 = ((bf16[8,128,8]{1,2,0:T(8,128)(2,1)}), bf16[8,128,8]{1,2,0:T(8,128)(2,1)S(1)}, u32[]{:S(2)}, u32[]{:S(2)}) async-start(bf16[8,128,8]{1,2,0:T(8,128)(2,1)} %copy.187), calls=%async_computation.6 | async-start | bytes 32768 | tf_op jit(solution)/shard_map/all_to_all | solution.py:193
  358.1 4.0 all-to-all-start.7
  362.0 2.5 reduce_sum.94
  366.2 4.5 %all-to-all-done.7 = bf16[8,2,8192]{2,1,0:T(2,128)(2,1)S(1)} async-done(((bf16[8,2,8192]{2,1,0:T(2,128)(2,1)}), bf16[8,2,8192]{2,1,0:T(2,128)(2,1)S(1)}, u32[]{:S(2)}, u32[]{:S(2)}) %all-to-all-start.7) | async-done | bytes 262176 | tf_op jit(solution)/shard_map/all_to_all | solution.py:196
  370.7 3.6 all-to-all-start.8
  376.7 6.1 %all-to-all-done.8 = bf16[8,2,8192]{2,1,0:T(2,128)(2,1)S(1)} async-done(((bf16[8,2,8192]{2,1,0:T(2,128)(2,1)}), bf16[8,2,8192]{2,1,0:T(2,128)(2,1)S(1)}, u32[]{:S(2)}, u32[]{:S(2)}) %all-to-all-start.8) | async-done | bytes 262176 | tf_op jit(solution)/shard_map/all_to_all | solution.py:197
  382.8 3.6 all-to-all-start.5
  388.8 23.1 %all-to-all-done.5 = bf16[8,128,512]{1,2,0:T(8,128)(2,1)S(1)} async-done(((bf16[8,128,512]{1,2,0:T(8,128)(2,1)}), bf16[8,128,512]{1,2,0:T(8,128)(2,1)S(1)}, u32[]{:S(2)}, u32[]{:S(2)}) %all-to-all-start.5) | async-done | bytes 1048608 | tf_op jit(solution)/shard_map/all_to_all | solution.py:192
  (553 shorter events, 260.2 us)
Async XLA Ops:
  0.6 13.9 %all-to-all-start = ((bf16[128,8,8]{0,2,1:T(8,128)(2,1)}), bf16[128,8,8]{0,2,1:T(8,128)(2,1)S(1)}, u32[]{:S(2)}, u32[]{:S(2)}) async-start(bf16[128,8,8]{0,2,1:T(8,128)(2,1)} %bitcast.356), calls=%async_computation | async-start | bytes 32768 | tf_op jit(solution)/shard_map/all_to_all | solution.py:131
  14.5 11.6 %all-to-all-start.2 = ((bf16[128,8,128]{2,0,1:T(8,128)(2,1)}), bf16[128,8,128]{2,0,1:T(8,128)(2,1)S(1)}, u32[]{:S(2)}, u32[]{:S(2)}) async-start(bf16[128,8,128]{2,0,1:T(8,128)(2,1)} %copy.167), calls=%async_computation.2 | async-start | bytes 524288 | tf_op jit(solution)/shard_map/all_to_all | solution.py:132
  17.9 11.9 %copy-start.5 = (bf16[128,4096]{1,0:T(8,128)(2,1)S(1)}, bf16[128,4096]{1,0:T(8,128)(2,1)}, u32[]{:S(2)}) copy-start(bf16[128,4096]{1,0:T(8,128)(2,1)} %param.16) | copy-start | bytes 3145732
  26.1 5.1 %copy-start.7 = (bf16[128,8,128]{2,1,0:T(8,128)(2,1)S(1)}, bf16[128,8,128]{2,1,0:T(8,128)(2,1)}, u32[]{:S(2)}) copy-start(bf16[128,8,128]{2,1,0:T(8,128)(2,1)} %param.20) | copy-start | bytes 786436
  26.1 5.8 %copy-start.10 = (u32[32]{0:T(128)S(1)}, u32[32]{0:T(128)}, u32[]{:S(2)}) copy-start(u32[32]{0:T(128)} %constant.138) | copy-start | bytes 388
  26.1 7.1 %copy-start.9 = (f32[64]{0:T(128)S(1)}, f32[64]{0:T(128)}, u32[]{:S(2)}) copy-start(f32[64]{0:T(128)} %param.18) | copy-start | bytes 772
  26.1 27.6 %all-to-all-start.4 = ((bf16[128,8,512]{0,2,1:T(8,128)(2,1)}), bf16[128,8,512]{0,2,1:T(8,128)(2,1)S(1)}, u32[]{:S(2)}, u32[]{:S(2)}) async-start(bf16[128,8,512]{0,2,1:T(8,128)(2,1)} %bitcast.45), calls=%async_computation.4 | async-start | bytes 2097152 | tf_op jit(solution)/shard_map/all_to_all | solution.py:129
  33.3 0.7 copy-start.8
  53.7 29.1 %all-to-all-start.3 = ((bf16[128,8,512]{0,2,1:T(8,128)(2,1)}), bf16[128,8,512]{0,2,1:T(8,128)(2,1)S(1)}, u32[]{:S(2)}, u32[]{:S(2)}) async-start(bf16[128,8,512]{0,2,1:T(8,128)(2,1)} %bitcast.332), calls=%async_computation.3 | async-start | bytes 2097152 | tf_op jit(solution)/shard_map/all_to_all | solution.py:130
  82.8 15.5 %all-to-all-start.1 = ((bf16[128,8,128]{2,0,1:T(8,128)(2,1)}), bf16[128,8,128]{2,0,1:T(8,128)(2,1)S(1)}, u32[]{:S(2)}, u32[]{:S(2)}) async-start(bf16[128,8,128]{2,0,1:T(8,128)(2,1)} %copy.166), calls=%async_computation.1 | async-start | bytes 524288 | tf_op jit(solution)/shard_map/all_to_all | solution.py:133
  98.3 4.2 %copy-start.2 = (bf16[128,8,128]{2,0,1:T(8,128)(2,1)}, bf16[128,8,128]{2,0,1:T(8,128)(2,1)S(1)}, u32[]{:S(2)}) copy-start(bf16[128,8,128]{2,0,1:T(8,128)(2,1)S(1)} %all-to-all-done.1) | copy-start | bytes 786436
  102.5 5.9 %copy-start.4 = (f32[16,64,128]{2,1,0:T(8,128)S(1)}, f32[16,64,128]{2,1,0:T(8,128)}, u32[]{:S(2)}) copy-start(f32[16,64,128]{2,1,0:T(8,128)} %all-gather.2) | copy-start | bytes 1572868
  102.5 6.0 %copy-start = (f32[4,8,64,128]{3,2,1,0:T(8,128)S(1)}, f32[4,8,64,128]{3,2,1,0:T(8,128)}, u32[]{:S(2)}) copy-start(f32[4,8,64,128]{3,2,1,0:T(8,128)} %get-tuple-element.250) | copy-start | bytes 3145732
  106.0 3.9 copy-start.1
  109.9 1.6 copy-start.3
  345.5 12.5 %all-to-all-start.6 = ((bf16[8,128,8]{1,2,0:T(8,128)(2,1)}), bf16[8,128,8]{1,2,0:T(8,128)(2,1)S(1)}, u32[]{:S(2)}, u32[]{:S(2)}) async-start(bf16[8,128,8]{1,2,0:T(8,128)(2,1)} %copy.187), calls=%async_computation.6 | async-start | bytes 32768 | tf_op jit(solution)/shard_map/all_to_all | solution.py:193
  358.1 12.6 %all-to-all-start.7 = ((bf16[8,2,8192]{2,1,0:T(2,128)(2,1)}), bf16[8,2,8192]{2,1,0:T(2,128)(2,1)S(1)}, u32[]{:S(2)}, u32[]{:S(2)}) async-start(bf16[8,2,8192]{2,1,0:T(2,128)(2,1)} %reshape.334), calls=%async_computation.7 | async-start | bytes 524288 | tf_op jit(solution)/shard_map/all_to_all | solution.py:196
  362.0 12.3 %copy-start.6 = (bf16[8,4,256,64]{2,3,1,0:T(8,128)(2,1)S(1)}, bf16[8,4,256,64]{2,3,1,0:T(8,128)(2,1)}, u32[]{:S(2)}) copy-start(bf16[8,4,256,64]{2,3,1,0:T(8,128)(2,1)} %get-tuple-element.252) | copy-start | bytes 3145732
  370.7 12.1 %all-to-all-start.8 = ((bf16[8,2,8192]{2,1,0:T(2,128)(2,1)}), bf16[8,2,8192]{2,1,0:T(2,128)(2,1)S(1)}, u32[]{:S(2)}, u32[]{:S(2)}) async-start(bf16[8,2,8192]{2,1,0:T(2,128)(2,1)} %reshape.336), calls=%async_computation.8 | async-start | bytes 524288 | tf_op jit(solution)/shard_map/all_to_all | solution.py:197
  382.8 29.1 %all-to-all-start.5 = ((bf16[8,128,512]{1,2,0:T(8,128)(2,1)}), bf16[8,128,512]{1,2,0:T(8,128)(2,1)S(1)}, u32[]{:S(2)}, u32[]{:S(2)}) async-start(bf16[8,128,512]{1,2,0:T(8,128)(2,1)} %copy.186), calls=%async_computation.5 | async-start | bytes 2097152 | tf_op jit(solution)/shard_map/all_to_all | solution.py:192
where the time goes:
time: 417 us; the launch traced here: 414 us
  matrix products  114 us (27%)
  other arithmetic  102 us (24%)
  waiting for transfers between devices  78.9 us (19%)
  local copies, waits for them, and re-layouts  70.6 us (17%)
  starting transfers between devices  38.4 us (9%)
  blocking collectives  7.24 us (2%)
    another operation x70, other arithmetic  42.3 us
    all_to_all x1, waiting for transfers between devices, on_device(): lax.all_to_all(dx_local, 'head', split_axis=0, concat_axis=1, tiled=True)  23.1 us
    dot_general x8, matrix products, stretch_grads(): drow = jnp.einsum('cki,ckn->cin', a_one, c_wide, precision=highest)  22.4 us
    another operation x133, local copies, waits for them, and re-layouts  20.1 us
    dynamic_slice x32, local copies, waits for them, and re-layouts, on_device(): lax.map(per_head, (x_heads, dy_heads, dt_heads, b_heads, c_heads, rates,...  18.6 us
    all_to_all x1, waiting for transfers between devices, on_device(): lax.all_to_all(x_seq, 'head', split_axis=1, concat_axis=0, tiled=True)  17.2 us
    dot_general x8, matrix products, stretch_grads(): jnp.einsum('cip,cpn->cin', x_scaled, grad_in, precision=highest)  16.1 us
    dynamic_update_slice x8, other arithmetic, on_device(): lax.map(per_head, (x_heads, dy_heads, dt_heads, b_heads, c_heads, rates,...  15.3 us
  transfers between devices with their start and end apart: 9, of which 8 were waited for; matrix products, arithmetic and copies ran while one was open for 10% of the time, Pallas kernels for 0%

commit v1 on v0

v1 whole, which is shorter than its diff:
```python
import functools

import jax
import jax.numpy as jnp
from jax import lax
from jax.experimental import pallas as pl
from jax.experimental.pallas import tpu as pltpu
from jax.sharding import PartitionSpec as P

HEADS = 64
HEAD_DIM = 64
STATE = 128
GROUPS = 8
LANES = 128
ROWS = 8
DT_ROWS = 16
LOG2E = 1.4426950408889634
F32 = jnp.float32
BF16 = jnp.bfloat16


def split2(value):
    hi = value.astype(BF16)
    return hi, (value - hi.astype(F32)).astype(BF16)


def split3(value):
    hi = value.astype(BF16)
    rest = value - hi.astype(F32)
    mid = rest.astype(BF16)
    return hi, mid, (rest - mid.astype(F32)).astype(BF16)


def dot(a, b):
    return lax.dot_general(a, b, (((1,), (0,)), ((), ())), preferred_element_type=F32)


def dot_nt(a, b):
    return lax.dot_general(a, b, (((1,), (1,)), ((), ())), preferred_element_type=F32)


def dot_tn(a, b):
    return lax.dot_general(a, b, (((0,), (0,)), ((), ())), preferred_element_type=F32)


def cat(parts, axis):
    return jnp.concatenate(parts, axis=axis)


def upper(size, strict):
    row = lax.broadcasted_iota(jnp.int32, (size, size), 0)
    col = lax.broadcasted_iota(jnp.int32, (size, size), 1)
    return row < col if strict else row <= col


def cumulate(rows, strict):
    tri = upper(rows.shape[1], strict).astype(F32).astype(BF16)
    sums = dot(cat([part.astype(F32) for part in split3(rows)], 0).astype(BF16), tri)
    return sums[:ROWS] + sums[ROWS : 2 * ROWS] + sums[2 * ROWS :]


def spread_matrix(terms, width):
    row = lax.broadcasted_iota(jnp.int32, (terms * ROWS, width), 0)
    col = lax.broadcasted_iota(jnp.int32, (terms * ROWS, width), 1)
    return (row % ROWS == col // HEAD_DIM).astype(F32).astype(BF16)


def spread(cols, width):
    hi, lo = split2(cols)
    return dot(cat([hi.astype(F32), lo.astype(F32)], 1).astype(BF16), spread_matrix(2, width))


def steps_of(buf, first, rate):
    dt = buf[0, first : first + DT_ROWS, :].astype(F32)[:ROWS]
    return dt, cumulate(dt * rate, False)


def wide(buf, first, blocks, tokens):
    return cat([buf[0, first + i * tokens : first + (i + 1) * tokens, :] for i in range(blocks)], 1)


def states_kernel(blocks, tokens, width, flag_ref, rate_ref, buf_s, buf_g, s_ref, g_ref, before_ref, after_ref, send_ref, s_now, g_now, s_log, g_log):
    step, last = pl.program_id(0), pl.num_programs(0) - 1
    rate = rate_ref[...]
    b_row, c_row, dt_row = 2 * blocks * tokens, (2 * blocks + 1) * tokens, (2 * blocks + 2) * tokens

    @pl.when(step == 0)
    def _():
        s_now[...] = jnp.zeros_like(s_now)
        g_now[...] = jnp.zeros_like(g_now)
        s_log[...] = jnp.full_like(s_log, flag_ref[0])
        g_log[...] = jnp.full_like(g_log, flag_ref[1])

    dt, cum = steps_of(buf_s, dt_row, rate)
    end = cum[:, tokens - 1 :]
    cols = jnp.transpose(cat([dt * jnp.exp(end - cum), jnp.broadcast_to(jnp.exp(end), dt.shape)], 0))
    scale = spread(cols[:, :ROWS], width)
    through = spread(cols[:ROWS, ROWS:], width)
    hi, lo = split2(scale * wide(buf_s, 0, blocks, tokens).astype(F32))
    b_here = buf_s[0, b_row : b_row + tokens, :]
    s_ref[0] = s_now[...]
    before_ref[0] = s_log[...]
    s_now[...] = through[:1] * s_now[...] + dot_tn(cat([b_here, b_here], 0), cat([hi, lo], 0))
    s_log[...] = through * s_log[...]

    dt, cum = steps_of(buf_g, dt_row, rate)
    end = cum[:, tokens - 1 :]
    cols = jnp.transpose(cat([jnp.exp(cum), jnp.broadcast_to(jnp.exp(end), dt.shape)], 0))
    scale = spread(cols[:, :ROWS], width)
    through = spread(cols[:ROWS, ROWS:], width)
    hi, lo = split2(scale * wide(buf_g, blocks * tokens, blocks, tokens).astype(F32))
    c_here = buf_g[0, c_row : c_row + tokens, :]
    g_ref[0] = g_now[...]
    after_ref[0] = g_log[...]
    g_now[...] = through[:1] * g_now[...] + dot_tn(cat([c_here, c_here], 0), cat([hi, lo], 0))
    g_log[...] = through * g_log[...]

    @pl.when(step == last)
    def _():
        send_ref[...] = jnp.where(flag_ref[0] > 0.5, g_now[...], s_now[...])


def inner_kernel(blocks, tokens, width, rate_ref, buf, dxbar_ref, row_ref, db_ref, dc_ref):
    b_row, c_row, dt_row = 2 * blocks * tokens, (2 * blocks + 1) * tokens, (2 * blocks + 2) * tokens
    dt, cum = steps_of(buf, dt_row, rate_ref[...])
    cum = cum * LOG2E
    cols = jnp.transpose(cat([cum, dt], 0))
    dt_wide = spread(cols[:, ROWS:], width)
    b_here, c_here = buf[0, b_row : b_row + tokens, :], buf[0, c_row : c_row + tokens, :]
    k_two = dot_nt(b_here, c_here)
    mask = upper(tokens, False)
    left = lax.broadcasted_iota(jnp.int32, (tokens, LANES), 1) < HEAD_DIM
    none = jnp.zeros((tokens, LANES), F32)
    one_sum = jnp.zeros((tokens, tokens), F32)
    rows = []
    for block in range(blocks):
        x_here = buf[0, block * tokens : (block + 1) * tokens, :].astype(F32)
        dy_here = buf[0, (blocks + block) * tokens : (blocks + block + 1) * tokens, :]
        dy_f32 = dy_here.astype(F32)
        scaled = x_here * dt_wide[:, block * LANES : (block + 1) * LANES]
        hi = scaled.astype(BF16).astype(F32)
        lo = scaled - hi
        pair = cat(
            [
                cat([jnp.where(left, hi, none), jnp.where(left, lo, none)], 1),
                cat([jnp.where(left, none, hi), jnp.where(left, none, lo)], 1),
            ],
            0,
        ).astype(BF16)
        k_one = dot_nt(pair, cat([dy_here, dy_here], 1))
        tops, bottoms = [], []
        for side in range(2):
            head = 2 * block + side
            gap = jnp.where(mask, cum[head : head + 1, :] - cols[:, head : head + 1], -1e30)
            decay = jnp.exp2(gap)
            a_one = decay * k_one[side * tokens : (side + 1) * tokens]
            a_two = decay * k_two
            one_sum = one_sum + a_one
            rows.append(jnp.sum(a_one * k_two, axis=0, keepdims=True))
            hi_two, lo_two = split2(a_two)
            tops.append(hi_two)
            bottoms.append(lo_two)
        sides = cat([jnp.where(left, dy_f32, none), jnp.where(left, none, dy_f32)], 0).astype(BF16)
        both = dot(cat([cat(tops, 1), cat(bottoms, 1)], 0), sides)
        dxbar_ref[0, :, block * LANES : (block + 1) * LANES] = both[:tokens] + both[tokens:]
    if len(rows) < ROWS:
        rows.append(jnp.zeros((ROWS - len(rows), tokens), F32))
    row_ref[0] = cat(rows, 0)
    db_ref[0] = dot(cat(list(split2(one_sum)), 1), cat([c_here, c_here], 0))
    dc_ref[0] = dot(cat(list(split2(jnp.transpose(one_sum))), 1), cat([b_here, b_here], 0))


def outer_kernel(blocks, tokens, width, rate_ref, buf, state0, grad0, before, after, carried, dxbar_in, row_in, db_in, dc_in, out):
    b_row, c_row, dt_row = 2 * blocks * tokens, (2 * blocks + 1) * tokens, (2 * blocks + 2) * tokens
    rate = rate_ref[...]
    dt, cum = steps_of(buf, dt_row, rate)
    end = cum[:, tokens - 1 :]
    to_end, from_start = jnp.exp(end - cum), jnp.exp(cum)
    cols = jnp.transpose(cat([dt, to_end, from_start], 0))
    dt_wide = spread(cols[:, :ROWS], width)
    end_wide = spread(cols[:, ROWS : 2 * ROWS], width)
    start_wide = spread(cols[:, 2 * ROWS : 3 * ROWS], width)
    x_here = wide(buf, 0, blocks, tokens).astype(F32)
    dy_here = wide(buf, blocks * tokens, blocks, tokens).astype(F32)
    b_here, c_here = buf[0, b_row : b_row + tokens, :], buf[0, c_row : c_row + tokens, :]
    state = state0[0] + before[0, :1] * carried[...]
    grad = grad0[0] + after[0, :1] * carried[...]
    s_hi, s_lo = split2(state)
    g_hi, g_lo = split2(grad)
    b_grad = dot(cat([b_here, b_here], 1), cat([g_hi, g_lo], 0))
    c_state = dot(cat([c_here, c_here], 1), cat([s_hi, s_lo], 0))
    dxbar = dxbar_in[0] + end_wide * b_grad
    dx = (dt_wide * dxbar).astype(BF16)
    for block in range(blocks):
        out[0, block * tokens : (block + 1) * tokens, :] = dx[:, block * LANES : (block + 1) * LANES]
    u_hi, u_lo = split2(end_wide * (dt_wide * x_here))
    v_hi, v_lo = split2(start_wide * dy_here)
    db = db_in[0] + (dot_nt(u_hi, g_hi) + (dot_nt(u_hi, g_lo) + dot_nt(u_lo, g_hi)))
    dc = dc_in[0] + (dot_nt(v_hi, s_hi) + (dot_nt(v_hi, s_lo) + dot_nt(v_lo, s_hi)))
    out[0, blocks * tokens : (blocks + 1) * tokens, :] = db.astype(BF16)
    out[0, (blocks + 1) * tokens : (blocks + 2) * tokens, :] = dc.astype(BF16)
    both = grad * state
    corner = both[:ROWS]
    for i in range(1, STATE // ROWS):
        corner = corner + both[i * ROWS : (i + 1) * ROWS]
    parts = split3(cat([dxbar * x_here, dy_here * c_state, corner], 0))
    picker = spread_matrix(2, width)
    sums = dot_nt(picker, parts[0]) + (dot_nt(picker, parts[1]) + dot_nt(picker, parts[2]))
    along = sums[:ROWS, :tokens]
    later = from_start * sums[:ROWS, tokens : 2 * tokens]
    corner = jnp.sum(sums[:ROWS, 2 * tokens :], axis=1, keepdims=True)
    flow = dt * along - row_in[0] - later
    dlog = jnp.exp(end) * corner + jnp.sum(later, axis=1, keepdims=True) + cumulate(flow, True)
    ddt = along + rate * dlog
    out[0, (blocks + 2) * tokens : (blocks + 2) * tokens + DT_ROWS, :] = cat([ddt, jnp.zeros_like(ddt)], 0).astype(BF16)


def on_device(x_seq, dy_seq, dt_seq, a_log, b_seq, c_seq):
    tokens = x_seq.shape[0]
    count = lax.axis_size("head")
    heads = HEADS // count
    width = heads * HEAD_DIM
    blocks = width // LANES
    copies = count // GROUPS
    rows_in = (2 * blocks + 2) * tokens + DT_ROWS
    rows_out = (blocks + 2) * tokens + DT_ROWS

    def by_owner(value):
        return value.reshape(tokens, count, blocks, LANES).transpose(1, 2, 0, 3).reshape(count, blocks * tokens, LANES)

    def by_group(value):
        return jnp.repeat(value.transpose(1, 0, 2), copies, axis=0)

    dt_rows = jnp.pad(dt_seq.T.reshape(count, heads, tokens), ((0, 0), (0, DT_ROWS - heads), (0, 0)))
    sent = cat([by_owner(x_seq), by_owner(dy_seq), by_group(b_seq), by_group(c_seq), dt_rows], 1)
    buf = lax.all_to_all(sent, "head", split_axis=0, concat_axis=0, tiled=True)

    rates = -jnp.exp(lax.dynamic_slice_in_dim(a_log, lax.axis_index("head") * heads, heads))
    rate = jnp.broadcast_to(jnp.pad(rates, (0, ROWS - heads))[:, None], (ROWS, LANES))
    second = lax.axis_index("ctx").astype(F32)
    flags = jnp.stack([second, 1.0 - second])

    def whole(*shape):
        return pl.BlockSpec(shape, lambda k: (0,) * len(shape))

    def at(*shape):
        return pl.BlockSpec((1,) + shape, lambda k: (k, 0, 0))

    def back(*shape):
        return pl.BlockSpec((1,) + shape, lambda k: (count - 1 - k, 0, 0))

    def f32(*shape):
        return jax.ShapeDtypeStruct(shape, F32)

    params = pltpu.CompilerParams(vmem_limit_bytes=40 * 1024 * 1024)
    state0, grad0, before, after, send = pl.pallas_call(
        functools.partial(states_kernel, blocks, tokens, width),
        grid=(count,),
        in_specs=[pl.BlockSpec(memory_space=pltpu.SMEM), whole(ROWS, LANES), at(rows_in, LANES), back(rows_in, LANES)],
        out_specs=[at(STATE, width), back(STATE, width), at(ROWS, width), back(ROWS, width), whole(STATE, width)],
        out_shape=[f32(count, STATE, width), f32(count, STATE, width), f32(count, ROWS, width), f32(count, ROWS, width), f32(STATE, width)],
        scratch_shapes=[pltpu.VMEM((STATE, width), F32), pltpu.VMEM((STATE, width), F32), pltpu.VMEM((ROWS, width), F32), pltpu.VMEM((ROWS, width), F32)],
        compiler_params=params,
        name="states",
    )(flags, rate, buf, buf)
    carried = lax.ppermute(send, "ctx", [(0, 1), (1, 0)])
    dxbar, row_sums, db_in, dc_in = pl.pallas_call(
        functools.partial(inner_kernel, blocks, tokens, width),
        grid=(count,),
        in_specs=[whole(ROWS, LANES), at(rows_in, LANES)],
        out_specs=[at(tokens, width), at(ROWS, tokens), at(tokens, STATE), at(tokens, STATE)],
        out_shape=[f32(count, tokens, width), f32(count, ROWS, tokens), f32(count, tokens, STATE), f32(count, tokens, STATE)],
        compiler_params=params,
        cost_estimate=pl.CostEstimate(flops=2_000_000_000, bytes_accessed=6_000_000, transcendentals=1_000_000),
        name="inner",
    )(rate, buf)
    out = pl.pallas_call(
        functools.partial(outer_kernel, blocks, tokens, width),
        grid=(count,),
        in_specs=[
            whole(ROWS, LANES),
            at(rows_in, LANES),
            at(STATE, width),
            at(STATE, width),
            at(ROWS, width),
            at(ROWS, width),
            whole(STATE, width),
            at(tokens, width),
            at(ROWS, tokens),
            at(tokens, STATE),
            at(tokens, STATE),
        ],
        out_specs=at(rows_out, LANES),
        out_shape=jax.ShapeDtypeStruct((count, rows_out, LANES), BF16),
        compiler_params=params,
        name="outer",
    )(rate, buf, state0, grad0, before, after, carried, dxbar, row_sums, db_in, dc_in)

    home = lax.all_to_all(out, "head", split_axis=0, concat_axis=0, tiled=True)
    dx = home[:, : blocks * tokens].reshape(count, blocks, tokens, LANES).transpose(2, 0, 1, 3).reshape(tokens, HEADS * HEAD_DIM)

    def total(first):
        part = home[:, first : first + tokens]
        if copies > 1:
            part = part.astype(F32).reshape(GROUPS, copies, tokens, STATE).sum(1).astype(BF16)
        return part.transpose(1, 0, 2)

    db = total(blocks * tokens)
    dc = total((blocks + 1) * tokens)
    first = (blocks + 2) * tokens
    ddt = home[:, first : first + heads].reshape(HEADS, tokens).T
    return dx, ddt, db, dc


def solution(mesh):
    spec2 = P(("grp", "ctx", "head"), None)
    spec3 = P(("grp", "ctx", "head"), None, None)
    return jax.shard_map(
        on_device,
        mesh=mesh,
        in_specs=(spec2, spec2, spec2, P(), spec3, spec3),
        out_specs=(spec2, spec2, spec3, spec3),
        check_vma=False,
    )
```

time: 417 us -> 154 us (0.37)
  matrix products: 114 us -> 0 us
  other arithmetic: 102 us -> 0.15 us
  local copies, waits for them, and re-layouts: 70.6 us -> 13 us
  blocking collectives: 7.24 us -> 42.5 us
  starting transfers between devices: 38.4 us -> 7.48 us
  Pallas kernels: 0 us -> 30 us
  waiting for transfers between devices: 78.9 us -> 60 us
    dot_general x74 -> x0, matrix products: 114 us -> none  [the longest x8 22.4 us: stretch_grads(): drow = jnp.einsum('cki,ckn->cin', a_one, c_wide, precision=highest)]
    all_to_all x0 -> x1, blocking collectives: none -> 42.5 us  [on_device(): home = lax.all_to_all(out, 'head', split_axis=0, concat_axis=0, tiled=True)]
    another operation x71 -> x1, other arithmetic: 42.4 us -> 0.07 us  [on_device(): flags = jnp.stack([second, 1.0 - second])]
    all_to_all x9 -> x1, starting transfers between devices: 38.4 us -> 7.41 us  [on_device(): buf = lax.all_to_all(sent, 'head', split_axis=0, concat_axis=0, tiled=True)]
    pallas_call x0 -> x3, Pallas kernels: none -> 30 us  [the longest x1 11.2 us: on_device(): pl.pallas_call(functools.partial(states_kernel, blocks, tokens, width), g...]
    dynamic_update_slice x16 -> x0, other arithmetic: 21.1 us -> none  [the longest x8 15.3 us: on_device(): lax.map(per_head, (x_heads, dy_heads, dt_heads, b_heads, c_heads, rates,...]
    another operation x133 -> x0, local copies, waits for them, and re-layouts: 20.1 us -> none
    all_to_all x9 -> x1, waiting for transfers between devices: 78.9 us -> 60 us  [on_device(): buf = lax.all_to_all(sent, 'head', split_axis=0, concat_axis=0, tiled=True)]
  transfers between devices with their start and end apart: 9 -> 2, of which waited for: 8 -> 1; matrix products, arithmetic and copies ran while one was open for 10% -> 0% of each run, Pallas kernels for 0% -> 6%
where the time goes in v1:
time: 154 us
  waiting for transfers between devices  60 us (39%)
  blocking collectives  42.5 us (28%)
  Pallas kernels  30 us (19%)
  local copies, waits for them, and re-layouts  13 us (8%)
  starting transfers between devices  7.48 us (5%)
    all_to_all x1, waiting for transfers between devices, on_device(): buf = lax.all_to_all(sent, 'head', split_axis=0, concat_axis=0, tiled=True)  60 us
    all_to_all x1, blocking collectives, on_device(): home = lax.all_to_all(out, 'head', split_axis=0, concat_axis=0, tiled=True)  42.5 us
    pallas_call x1, Pallas kernels, on_device(): pl.pallas_call(functools.partial(states_kernel, blocks, tokens, width), g...  11.2 us
    pallas_call x1, Pallas kernels, on_device(): pl.pallas_call(functools.partial(outer_kernel, blocks, tokens, width), gr...  10.3 us
    pallas_call x1, Pallas kernels, on_device(): pl.pallas_call(functools.partial(inner_kernel, blocks, tokens, width), gr...  8.53 us
    all_to_all x1, starting transfers between devices, on_device(): buf = lax.all_to_all(sent, 'head', split_axis=0, concat_axis=0, tiled=True)  7.41 us
    unnamed x16, local copies, waits for them, and re-layouts  5.7 us
    reshape x4, local copies, waits for them, and re-layouts, by_owner(): value.reshape(tokens, count, blocks, LANES).transpose(1, 2, 0, 3)  3.46 us
  transfers between devices with their start and end apart: 2, of which 1 were waited for; matrix products, arithmetic and copies ran while one was open for 0% of the time, Pallas kernels for 6%

profile of v1, /device:TPU:0, one launch (start us, length us, event | category | flops | bytes accessed | tf_op | source)
XLA Modules:
  0.0 153.9 jit_solution(12946435811094496500)
XLA Ops:
  0.6 0.0 copy-start
  0.6 1.9 %reshape.33 = bf16[128,8,4,128]{3,2,1,0:T(4,128)(2,1)S(1)} reshape(bf16[128,4096]{1,0:T(8,128)(2,1)} %param.6) | data formatting | bytes 2097152 | tf_op jit(solution)/shard_map/reshape | solution.py:229
  2.5 0.4 copy.10
  2.9 0.0 copy-done
  3.0 0.8 reshape.35
  3.7 0.0 copy-start.1
  3.7 0.4 copy.11
  4.2 0.0 copy-start.2
  4.2 0.0 copy-start.3
  4.2 1.2 constant_dynamic-update-slice_fusion.1
  5.4 1.2 constant_dynamic-update-slice_fusion
  6.6 0.0 copy-done.1
  6.6 0.8 bitcast_dynamic-update-slice_fusion.1
  7.3 0.8 bitcast_dynamic-update-slice_fusion
  8.1 0.6 pad_dynamic-update-slice_fusion
  8.7 7.4 %all-to-all-start = ((bf16[8,1296,128]{2,1,0:T(8,128)(2,1)}), bf16[8,1296,128]{2,1,0:T(8,128)(2,1)S(1)}, u32[]{:S(2)}, u32[]{:S(2)}) async-start(bf16[8,1296,128]{2,1,0:T(8,128)(2,1)} %pad_dynamic-update-slice_fusion), calls=%async_computation | async-start | bytes 5308416 | tf_op jit(solution)/shard_map/all_to_all | solution.py:236
  16.1 0.1 pad_maximum_fusion.flag_ref
  16.2 0.1 exponential_negate_fusion
  16.3 60.0 %all-to-all-done.buf_s.buf_g.buf = bf16[8,1296,128]{2,1,0:T(8,128)(2,1)S(1)} async-done(((bf16[8,1296,128]{2,1,0:T(8,128)(2,1)}), bf16[8,1296,128]{2,1,0:T(8,128)(2,1)S(1)}, u32[]{:S(2)}, u32[]{:S(2)}) %all-to-all-start) | async-done | bytes 2654240 | tf_op jit(solution)/shard_map/all_to_all | solution.py:236
  76.3 0.1 broadcast_in_dim.2.rate_ref
  76.4 11.2 %states.1 = (f32[8,128,512]{2,1,0:T(8,128)S(1)}, f32[8,128,512]{2,1,0:T(8,128)S(1)}, f32[8,8,512]{2,1,0:T(8,128)S(1)}, f32[8,8,512]{2,1,0:T(8,128)S(1)}, f32[128,512]{1,0:T(8,128)S(1)}) custom-call(f32[2]{0:T(128)S(1)} %pad_maximum_fusion.flag_ref, f32[8,128]{1,0:T(8,128)S(1)} %broadcast_in_dim.2.rate_ref, ...), custom_call_target="tpu_custom_call" | custom-call | tf_op jit(solution)/shard_map/states/pallas_call | solution.py:256
  87.6 0.1 collective-permute-start
  87.7 8.5 %inner.1 = (f32[8,128,512]{2,1,0:T(8,128)S(1)}, f32[8,8,128]{2,1,0:T(8,128)S(1)}, f32[8,128,128]{2,1,0:T(8,128)S(1)}, f32[8,128,128]{2,1,0:T(8,128)S(1)}) custom-call(f32[8,128]{1,0:T(8,128)S(1)} %broadcast_in_dim.2.rate_ref, bf16[8,1296,128]{2,1,0:T(8,128)(2,1)S(1)} %all-to-all-done.buf_s.buf_g.buf), custom_call_target="tpu_custom_call" | custom-call | flops 2000000000 | bytes 6000000 | tf_op jit(solution)/shard_map/inner/pallas_call | solution.py:267
  96.2 0.0 collective-permute-done.carried
  96.2 10.3 %outer.1 = bf16[8,784,128]{2,1,0:T(8,128)(2,1)S(1)} custom-call(f32[8,128]{1,0:T(8,128)S(1)} %broadcast_in_dim.2.rate_ref, bf16[8,1296,128]{2,1,0:T(8,128)(2,1)S(1)} %all-to-all-done.buf_s.buf_g.buf, f32[8,128,512]{2,1,0:T(8,128)S(1)} %get-tuple-element.13.state0, f32[8,128,512]{2,1,0:T(8,128)S(1)} %get-tuple-element.14.grad0, ...), custom_call_target="tpu_custom_call" | custom-call | tf_op jit(solution)/shard_map/outer/pallas_call | solution.py:277
  106.5 42.5 %all_to_all.10 = bf16[8,784,128]{2,1,0:T(8,128)(2,1)S(1)} all-to-all(bf16[8,784,128]{2,1,0:T(8,128)(2,1)S(1)} %outer.1), channel_id=1, replica_groups=mesh['grp'=2,'head'=8,'ctx'=2] {'head'}, dimensions={0} | all-to-all | bytes 3211264 | tf_op jit(solution)/shard_map/all_to_all | solution.py:299
  149.0 0.1 slice.16
  149.1 0.8 copy.14
  149.9 1.6 %reshape.39 = bf16[128,4096]{1,0:T(8,128)(2,1)} reshape(bf16[128,8,4,128]{3,2,1,0:T(4,128)(2,1)S(1)} %copy.14) | data formatting | bytes 2097152 | tf_op jit(solution)/shard_map/reshape | solution.py:300
  151.6 0.9 copy.16
  152.5 0.9 copy.15
  153.3 0.6 slice_bitcast_fusion.2
  (5 shorter events, 0.1 us)
Async XLA Ops:
  0.6 2.3 %copy-start = (bf16[128,4096]{1,0:T(8,128)(2,1)S(1)}, bf16[128,4096]{1,0:T(8,128)(2,1)}, u32[]{:S(2)}) copy-start(bf16[128,4096]{1,0:T(8,128)(2,1)} %param.7) | copy-start | bytes 3145732
  3.7 2.8 %copy-start.1 = (bf16[128,8,128]{2,1,0:T(8,128)(2,1)S(1)}, bf16[128,8,128]{2,1,0:T(8,128)(2,1)}, u32[]{:S(2)}) copy-start(bf16[128,8,128]{2,1,0:T(8,128)(2,1)} %param.10) | copy-start | bytes 786436
  4.2 3.2 %copy-start.2 = (bf16[128,8,128]{2,1,0:T(8,128)(2,1)S(1)}, bf16[128,8,128]{2,1,0:T(8,128)(2,1)}, u32[]{:S(2)}) copy-start(bf16[128,8,128]{2,1,0:T(8,128)(2,1)} %param.11) | copy-start | bytes 786436
  4.2 3.9 %copy-start.3 = (bf16[128,64]{0,1:T(8,128)(2,1)S(1)}, bf16[128,64]{0,1:T(8,128)(2,1)}, u32[]{:S(2)}) copy-start(bf16[128,64]{0,1:T(8,128)(2,1)} %param.8) | copy-start | bytes 49156
  8.7 7.5 %copy-start.4 = (f32[64]{0:T(128)S(1)}, f32[64]{0:T(128)}, u32[]{:S(2)}) copy-start(f32[64]{0:T(128)} %param.9) | copy-start | bytes 772
  8.7 67.6 %all-to-all-start = ((bf16[8,1296,128]{2,1,0:T(8,128)(2,1)}), bf16[8,1296,128]{2,1,0:T(8,128)(2,1)S(1)}, u32[]{:S(2)}, u32[]{:S(2)}) async-start(bf16[8,1296,128]{2,1,0:T(8,128)(2,1)} %pad_dynamic-update-slice_fusion), calls=%async_computation | async-start | bytes 5308416 | tf_op jit(solution)/shard_map/all_to_all | solution.py:236
  87.6 8.6 %collective-permute-start = (f32[128,512]{1,0:T(8,128)S(1)}, f32[128,512]{1,0:T(8,128)S(1)}, u32[]{:S(2)}, u32[]{:S(2)}) collective-permute-start(f32[128,512]{1,0:T(8,128)S(1)} %get-tuple-element.17), channel_id=1, source_target_pairs={{0,1},{1,0},{2,3},{3,2},{4,5},{5,4},{6,7},{7,6},{8,9},{9,8},{10,11... | collective-permute-start | bytes 786440 | tf_op jit(solution)/shard_map/ppermute | solution.py:266

commit v2 on v1

v2 whole, which is shorter than its diff:
```python
import functools
from typing import NamedTuple

import jax
import jax.numpy as jnp
from jax import lax
from jax.experimental import pallas as pl
from jax.experimental.pallas import tpu as pltpu
from jax.sharding import PartitionSpec as P

HEADS = 64
HEAD_DIM = 64
STATE = 128
GROUPS = 8
LANES = 128
ROWS = 8
TILE = 16
LOG2E = 1.4426950408889634
F32 = jnp.float32
BF16 = jnp.bfloat16
PIECES = 1


def split2(value):
    hi = value.astype(BF16)
    return hi, (value - hi.astype(F32)).astype(BF16)


def split3(value):
    hi = value.astype(BF16)
    rest = value - hi.astype(F32)
    mid = rest.astype(BF16)
    return hi, mid, (rest - mid.astype(F32)).astype(BF16)


def dot(a, b):
    return lax.dot_general(a, b, (((1,), (0,)), ((), ())), preferred_element_type=F32)


def dot_nt(a, b):
    return lax.dot_general(a, b, (((1,), (1,)), ((), ())), preferred_element_type=F32)


def dot_tn(a, b):
    return lax.dot_general(a, b, (((0,), (0,)), ((), ())), preferred_element_type=F32)


def cat(parts, axis):
    return jnp.concatenate(parts, axis=axis)


def upper(size, strict):
    row = lax.broadcasted_iota(jnp.int32, (size, size), 0)
    col = lax.broadcasted_iota(jnp.int32, (size, size), 1)
    return row < col if strict else row <= col


def cumulate(rows, strict):
    tri = upper(rows.shape[1], strict).astype(F32).astype(BF16)
    sums = dot(cat([part.astype(F32) for part in split3(rows)], 0).astype(BF16), tri)
    return sums[:ROWS] + sums[ROWS : 2 * ROWS] + sums[2 * ROWS :]


def spread_matrix(terms, width):
    row = lax.broadcasted_iota(jnp.int32, (terms * ROWS, width), 0)
    col = lax.broadcasted_iota(jnp.int32, (terms * ROWS, width), 1)
    return (row % ROWS == col // HEAD_DIM).astype(F32).astype(BF16)


def spread(cols, width):
    hi, lo = split2(cols)
    return dot(cat([hi.astype(F32), lo.astype(F32)], 1).astype(BF16), spread_matrix(2, width))


class Place(NamedTuple):
    tokens: int
    blocks: int
    piece: int
    last: bool
    shared: bool
    bc: int
    dt: int
    dt_rows: int

    @property
    def width(self):
        return self.blocks * LANES

    def x(self, buf):
        return [buf[i * self.tokens : (i + 1) * self.tokens, :] for i in range(self.blocks)]

    def dy(self, buf):
        return [buf[i * self.tokens : (i + 1) * self.tokens, :] for i in range(self.blocks, 2 * self.blocks)]

    def b(self, buf):
        return buf[self.bc : self.bc + self.tokens, :]

    def c(self, buf):
        return buf[self.bc + self.tokens : self.bc + 2 * self.tokens, :]

    def steps(self, buf, rate):
        dt = buf[self.dt : self.dt + self.dt_rows, :].astype(F32)[self.piece * ROWS : (self.piece + 1) * ROWS]
        return dt, cumulate(dt * rate, False)


def states_kernel(place, flag_ref, rate_ref, *refs):
    bufs, refs = (refs[:2] * 2, refs[2:]) if place.shared else (refs[:4], refs[4:])
    xy_s, xy_g, bc_s, bc_g = bufs
    s_ref, g_ref, before_ref, after_ref, send_ref, now, log = refs
    step, last = pl.program_id(0), pl.num_programs(0) - 1
    rate, width, tokens = rate_ref[...], place.width, place.tokens

    @pl.when(step == 0)
    def _():
        now[...] = jnp.zeros_like(now)
        log[...] = jnp.ones_like(log)

    for seg in range(2):
        xy, bc = xy_s.at[seg, 0], bc_s.at[seg, 0]
        dt, cum = place.steps(bc, rate)
        end = cum[:, tokens - 1 :]
        cols = jnp.transpose(cat([dt * jnp.exp(end - cum), jnp.broadcast_to(jnp.exp(end), dt.shape)], 0))
        scale = spread(cols[:, :ROWS], width)
        through = spread(cols[:ROWS, ROWS:], width)
        hi, lo = split2(scale * cat(place.x(xy), 1).astype(F32))
        b_here = place.b(bc)
        s_ref[seg, 0] = now[seg]
        before_ref[seg, 0] = log[seg]
        now[seg] = through[:1] * now[seg] + dot_tn(cat([b_here, b_here], 0), cat([hi, lo], 0))
        log[seg] = through * log[seg]

        xy, bc = xy_g.at[seg, 0], bc_g.at[seg, 0]
        dt, cum = place.steps(bc, rate)
        end = cum[:, tokens - 1 :]
        cols = jnp.transpose(cat([jnp.exp(cum), jnp.broadcast_to(jnp.exp(end), dt.shape)], 0))
        scale = spread(cols[:, :ROWS], width)
        through = spread(cols[:ROWS, ROWS:], width)
        hi, lo = split2(scale * cat(place.dy(xy), 1).astype(F32))
        c_here = place.c(bc)
        g_ref[seg, 0] = now[2 + seg]
        after_ref[seg, 0] = log[2 + seg]
        now[2 + seg] = through[:1] * now[2 + seg] + dot_tn(cat([c_here, c_here], 0), cat([hi, lo], 0))
        log[2 + seg] = through * log[2 + seg]

    @pl.when(step == last)
    def _():
        front = flag_ref[0] > 0.5
        send_ref[:STATE] = now[0]
        send_ref[STATE : 2 * STATE] = jnp.where(front, now[1], now[2])
        send_ref[2 * STATE : 3 * STATE] = now[3]
        send_ref[3 * STATE :] = jnp.where(front, log[1], log[0])


def inner_kernel(place, rate_ref, *refs):
    refs = refs[:1] + refs if place.shared else refs
    xy_ref, bc_ref, dxbar_ref, row_ref, db_ref, dc_ref = refs
    xy, bc, tokens, width = xy_ref.at[0, 0], bc_ref.at[0, 0], place.tokens, place.width
    dt, cum = place.steps(bc, rate_ref[...])
    cum = cum * LOG2E
    cols = jnp.transpose(cat([cum, dt], 0))
    dt_wide = spread(cols[:, ROWS:], width)
    b_here, c_here = place.b(bc), place.c(bc)
    k_two = dot_nt(b_here, c_here)
    mask = upper(tokens, False)
    left = lax.broadcasted_iota(jnp.int32, (tokens, LANES), 1) < HEAD_DIM
    none = jnp.zeros((tokens, LANES), F32)
    one_sum = jnp.zeros((tokens, tokens), F32)
    rows = []
    for block, (x_here, dy_here) in enumerate(zip(place.x(xy), place.dy(xy))):
        dy_f32 = dy_here.astype(F32)
        scaled = x_here.astype(F32) * dt_wide[:, block * LANES : (block + 1) * LANES]
        hi = scaled.astype(BF16).astype(F32)
        lo = scaled - hi
        pair = cat(
            [
                cat([jnp.where(left, hi, none), jnp.where(left, lo, none)], 1),
                cat([jnp.where(left, none, hi), jnp.where(left, none, lo)], 1),
            ],
            0,
        ).astype(BF16)
        k_one = dot_nt(pair, cat([dy_here, dy_here], 1))
        tops, bottoms = [], []
        for side in range(2):
            head = 2 * block + side
            gap = jnp.where(mask, cum[head : head + 1, :] - cols[:, head : head + 1], -1e30)
            decay = jnp.exp2(gap)
            a_one = decay * k_one[side * tokens : (side + 1) * tokens]
            a_two = decay * k_two
            one_sum = one_sum + a_one
            rows.append(jnp.sum(a_one * k_two, axis=0, keepdims=True))
            hi_two, lo_two = split2(a_two)
            tops.append(hi_two)
            bottoms.append(lo_two)
        sides = cat([jnp.where(left, dy_f32, none), jnp.where(left, none, dy_f32)], 0).astype(BF16)
        both = dot(cat([cat(tops, 1), cat(bottoms, 1)], 0), sides)
        dxbar_ref[0, 0, :, block * LANES : (block + 1) * LANES] = both[:tokens] + both[tokens:]
    if len(rows) < ROWS:
        rows.append(jnp.zeros((ROWS - len(rows), tokens), F32))
    row_ref[0, 0] = cat(rows, 0)
    db_ref[0, 0] = dot(cat(list(split2(one_sum)), 1), cat([c_here, c_here], 0))
    dc_ref[0, 0] = dot(cat(list(split2(jnp.transpose(one_sum))), 1), cat([b_here, b_here], 0))


def outer_kernel(place, flag_ref, rate_ref, *refs):
    refs = refs[:1] + refs if place.shared else refs
    xy_ref, bc_ref, state0, grad0, before, after, sent, got, dxbar_in, row_in, db_in, dc_in, *refs = refs
    if place.piece > 0:
        db_old, dc_old, *refs = refs
    out, *refs = refs
    if not place.last:
        db_new, dc_new, *refs = refs
    (carried,) = refs
    xy, bc, tokens, width = xy_ref.at[0, 0], bc_ref.at[0, 0], place.tokens, place.width
    seg = pl.program_id(0)

    @pl.when((seg == 0) & (pl.program_id(1) == 0))
    def _():
        front = flag_ref[0] > 0.5
        sent0, sent2 = sent[:STATE], sent[2 * STATE : 3 * STATE]
        got0, got1, got2 = got[:STATE], got[STATE : 2 * STATE], got[2 * STATE : 3 * STATE]
        mine, other = sent[3 * STATE : 3 * STATE + 1], got[3 * STATE : 3 * STATE + 1]
        far = got1 + other * (jnp.where(front, sent2, sent0) + mine * jnp.where(front, got2, got0))
        near = jnp.where(front, got0, got2) + other * jnp.where(front, sent0, sent2)
        none = jnp.zeros_like(far)
        carried[0] = jnp.where(front, none, got0)
        carried[1] = jnp.where(front, near, far)
        carried[2] = jnp.where(front, far, near)
        carried[3] = jnp.where(front, got2, none)

    rate = rate_ref[...]
    dt, cum = place.steps(bc, rate)
    end = cum[:, tokens - 1 :]
    to_end, from_start = jnp.exp(end - cum), jnp.exp(cum)
    cols = jnp.transpose(cat([dt, to_end, from_start], 0))
    dt_wide = spread(cols[:, :ROWS], width)
    end_wide = spread(cols[:, ROWS : 2 * ROWS], width)
    start_wide = spread(cols[:, 2 * ROWS : 3 * ROWS], width)
    x_here = cat(place.x(xy), 1).astype(F32)
    dy_here = cat(place.dy(xy), 1).astype(F32)
    b_here, c_here = place.b(bc), place.c(bc)
    state = state0[0, 0] + before[0, 0, :1] * carried[seg]
    grad = grad0[0, 0] + after[0, 0, :1] * carried[2 + seg]
    s_hi, s_lo = split2(state)
    g_hi, g_lo = split2(grad)
    b_grad = dot(cat([b_here, b_here], 1), cat([g_hi, g_lo], 0))
    c_state = dot(cat([c_here, c_here], 1), cat([s_hi, s_lo], 0))
    dxbar = dxbar_in[0, 0] + end_wide * b_grad
    dx = (dt_wide * dxbar).astype(BF16)
    for block in range(place.blocks):
        out[0, 0, block * tokens : (block + 1) * tokens, :] = dx[:, block * LANES : (block + 1) * LANES]
    u_hi, u_lo = split2(end_wide * (dt_wide * x_here))
    v_hi, v_lo = split2(start_wide * dy_here)
    db = db_in[0, 0] + (dot_nt(u_hi, g_hi) + (dot_nt(u_hi, g_lo) + dot_nt(u_lo, g_hi)))
    dc = dc_in[0, 0] + (dot_nt(v_hi, s_hi) + (dot_nt(v_hi, s_lo) + dot_nt(v_lo, s_hi)))
    if place.piece > 0:
        db, dc = db + db_old[0, 0], dc + dc_old[0, 0]
    first = place.blocks * tokens
    if place.last:
        out[0, 0, first : first + tokens, :] = db.astype(BF16)
        out[0, 0, first + tokens : first + 2 * tokens, :] = dc.astype(BF16)
        first = first + 2 * tokens
    else:
        db_new[0, 0], dc_new[0, 0] = db, dc
    both = grad * state
    corner = both[:ROWS]
    for i in range(1, STATE // ROWS):
        corner = corner + both[i * ROWS : (i + 1) * ROWS]
    parts = split3(cat([dxbar * x_here, dy_here * c_state, corner], 0))
    picker = spread_matrix(2, width)
    sums = dot_nt(picker, parts[0]) + (dot_nt(picker, parts[1]) + dot_nt(picker, parts[2]))
    along = sums[:ROWS, :tokens]
    later = from_start * sums[:ROWS, tokens : 2 * tokens]
    corner = jnp.sum(sums[:ROWS, 2 * tokens :], axis=1, keepdims=True)
    flow = dt * along - row_in[0, 0] - later
    dlog = jnp.exp(end) * corner + jnp.sum(later, axis=1, keepdims=True) + cumulate(flow, True)
    ddt = along + rate * dlog
    out[0, 0, first : first + TILE, :] = cat([ddt, jnp.zeros_like(ddt)], 0).astype(BF16)


def on_device(x_seq, dy_seq, dt_seq, a_log, b_seq, c_seq):
    tokens = x_seq.shape[0]
    half = lax.axis_size("lo")
    count = 2 * half
    heads = HEADS // count
    width = heads * HEAD_DIM
    copies = count // GROUPS
    pieces = PIECES if width % (PIECES * LANES) == 0 else 1
    blocks = width // LANES // pieces
    piece_heads = heads // pieces
    dt_rows = -(-pieces * ROWS // TILE) * TILE
    member = lax.axis_index(("ctx", "lo"))
    front = 1.0 - lax.axis_index("hi").astype(F32)
    flags = jnp.stack([front, 1.0 - front])

    def swap(value):
        return lax.all_to_all(value, ("ctx", "lo"), split_axis=0, concat_axis=0, tiled=True)

    def by_owner(value):
        parts = value.reshape(tokens, count, pieces, blocks, LANES).transpose(2, 1, 3, 0, 4)
        return parts.reshape(pieces, count, blocks * tokens, LANES)

    def by_group(value):
        return jnp.repeat(value.transpose(1, 0, 2), copies, axis=0)

    def padded(value, rows):
        return jnp.pad(value, ((0, 0),) * (value.ndim - 2) + ((0, rows - value.shape[-2]), (0, 0)))

    dt_sent = padded(dt_seq.T.reshape(count, pieces, piece_heads, tokens), ROWS).reshape(count, pieces * ROWS, tokens)
    x_sent, dy_sent = by_owner(x_seq), by_owner(dy_seq)
    rates = -jnp.exp(lax.dynamic_slice_in_dim(a_log, member * heads, heads)).reshape(pieces, piece_heads)
    rates = jnp.broadcast_to(jnp.pad(rates, ((0, 0), (0, ROWS - piece_heads)))[:, :, None], (pieces, ROWS, LANES))

    def f32(*shape):
        return jax.ShapeDtypeStruct((2, half) + shape, F32)

    smem = pl.BlockSpec(memory_space=pltpu.SMEM)
    params = pltpu.CompilerParams(vmem_limit_bytes=40 * 1024 * 1024)

    def whole(*shape):
        return pl.BlockSpec(shape, lambda *k: (0,) * len(shape))

    def at(*shape):
        return pl.BlockSpec((1, 1) + shape, lambda s, k: (s, k) + (0,) * len(shape))

    homes = []
    shared_buf = db_old = dc_old = None
    for piece in range(pieces):
        sent = [x_sent[piece], dy_sent[piece]]
        if piece == 0:
            sent += [by_group(b_seq), by_group(c_seq), padded(dt_sent, dt_rows)]
        buf = swap(cat(sent, 1)).reshape(2, half, -1, LANES)
        shared_buf = buf if piece == 0 else shared_buf
        place = Place(tokens, blocks, piece, piece == pieces - 1, piece == 0, 2 * blocks * tokens, (2 * blocks + 2) * tokens, dt_rows)
        bufs = [buf] if place.shared else [buf, shared_buf]
        rate, wide = rates[piece], place.width

        def both(*shape):
            return pl.BlockSpec((2, 1) + shape, lambda k: (0, k) + (0,) * len(shape))

        def back(*shape):
            return pl.BlockSpec((2, 1) + shape, lambda k: (0, half - 1 - k) + (0,) * len(shape))

        total = (3 * STATE + ROWS, wide)
        state0, grad0, before, after, send = pl.pallas_call(
            functools.partial(states_kernel, place),
            grid=(half,),
            in_specs=[smem, whole(ROWS, LANES)] + [spec(*b.shape[2:]) for b in bufs for spec in (both, back)],
            out_specs=[both(STATE, wide), back(STATE, wide), both(ROWS, wide), back(ROWS, wide), whole(*total)],
            out_shape=[f32(STATE, wide), f32(STATE, wide), f32(ROWS, wide), f32(ROWS, wide), jax.ShapeDtypeStruct(total, F32)],
            scratch_shapes=[pltpu.VMEM((4, STATE, wide), F32), pltpu.VMEM((4, ROWS, wide), F32)],
            compiler_params=params,
            name="states",
        )(flags, rate, *[b for b in bufs for _ in range(2)])
        got = lax.ppermute(send, "hi", [(0, 1), (1, 0)])
        buf_specs = [at(*b.shape[2:]) for b in bufs]
        dxbar, row_sums, db_in, dc_in = pl.pallas_call(
            functools.partial(inner_kernel, place),
            grid=(2, half),
            in_specs=[whole(ROWS, LANES)] + buf_specs,
            out_specs=[at(tokens, wide), at(ROWS, tokens), at(tokens, STATE), at(tokens, STATE)],
            out_shape=[f32(tokens, wide), f32(ROWS, tokens), f32(tokens, STATE), f32(tokens, STATE)],
            compiler_params=params,
            cost_estimate=pl.CostEstimate(flops=2_000_000_000, bytes_accessed=6_000_000, transcendentals=1_000_000),
            name="inner",
        )(rate, *bufs)
        rows_out = blocks * tokens + (2 * tokens if place.last else 0) + TILE
        old = [] if piece == 0 else [db_old, dc_old]
        new = [] if place.last else [f32(tokens, STATE)] * 2
        out, *olds = pl.pallas_call(
            functools.partial(outer_kernel, place),
            grid=(2, half),
            in_specs=[smem, whole(ROWS, LANES)]
            + buf_specs
            + [at(STATE, wide), at(STATE, wide), at(ROWS, wide), at(ROWS, wide), whole(*total), whole(*total)]
            + [at(tokens, wide), at(ROWS, tokens), at(tokens, STATE), at(tokens, STATE)]
            + [at(tokens, STATE) for _ in old],
            out_specs=[at(rows_out, LANES)] + [at(tokens, STATE) for _ in new],
            out_shape=[jax.ShapeDtypeStruct((2, half, rows_out, LANES), BF16)] + new,
            scratch_shapes=[pltpu.VMEM((4, STATE, wide), F32)],
            compiler_params=params,
            name="outer",
        )(flags, rate, *bufs, state0, grad0, before, after, send, got, dxbar, row_sums, db_in, dc_in, *old)
        if olds:
            db_old, dc_old = olds
        homes.append(swap(out.reshape(count, rows_out, LANES)))

    def columns(home):
        return home[:, : blocks * tokens].reshape(count, blocks, tokens, LANES)

    dx = cat([columns(home) for home in homes], 1).transpose(2, 0, 1, 3).reshape(tokens, HEADS * HEAD_DIM)
    steps = [home[:, -TILE:][:, :piece_heads] for home in homes]
    ddt = cat(steps, 1).reshape(HEADS, tokens).T

    def summed(first):
        part = homes[-1][:, first : first + tokens]
        if copies > 1:
            part = part.astype(F32).reshape(GROUPS, copies, tokens, STATE).sum(1).astype(BF16)
        return part.transpose(1, 0, 2)

    return dx, ddt, summed(blocks * tokens), summed((blocks + 1) * tokens)


def solution(mesh):
    parts, head, ctx = (mesh.shape[name] for name in ("grp", "head", "ctx"))
    split = jax.sharding.Mesh(mesh.devices.reshape(parts, 2, head // 2, ctx), ("grp", "hi", "lo", "ctx"))
    spec = P(("grp", "ctx", "hi", "lo"))
    return jax.shard_map(
        on_device,
        mesh=split,
        in_specs=(spec, spec, spec, P(), spec, spec),
        out_specs=(spec, spec, spec, spec),
        check_vma=False,
    )
```

time: 154 us -> 135 us (0.88)
  blocking collectives: 42.5 us -> 23.7 us
    all_to_all x1, waiting for transfers between devices: 60 us -> 31.9 us  [swap(): lax.all_to_all(value, ('ctx', 'lo'), split_axis=0, concat_axis=0, tiled=T...]
    ppermute x1, waiting for transfers between devices: 0.01 us -> 26.9 us  [on_device(): got = lax.ppermute(send, 'hi', [(0, 1), (1, 0)])]
    all_to_all x1, blocking collectives: 42.5 us -> 23.7 us  [swap(): lax.all_to_all(value, ('ctx', 'lo'), split_axis=0, concat_axis=0, tiled=T...]
    ppermute x1, starting transfers between devices: 0.07 us -> 2.66 us  [on_device(): got = lax.ppermute(send, 'hi', [(0, 1), (1, 0)])]
    all_to_all x1, starting transfers between devices: 7.41 us -> 5.39 us  [swap(): lax.all_to_all(value, ('ctx', 'lo'), split_axis=0, concat_axis=0, tiled=T...]
    reshape x5 -> x3, local copies, waits for them, and re-layouts: 5.07 us -> 4.25 us  [the longest x2 2.64 us: by_owner(): value.reshape(tokens, count, pieces, blocks, LANES).transpose(2, 1, 3, 0, 4)]
  transfers between devices with their start and end apart: 2 -> 2, of which waited for: 1 -> 2; matrix products, arithmetic and copies ran while one was open for 0% -> 0% of each run, Pallas kernels for 6% -> 6%
where the time goes in v2:
time: 135 us
  waiting for transfers between devices  58.8 us (44%)
  Pallas kernels  30.6 us (23%)
  blocking collectives  23.7 us (18%)
  local copies, waits for them, and re-layouts  13 us (10%)
  starting transfers between devices  8.04 us (6%)
    all_to_all x1, waiting for transfers between devices, swap(): lax.all_to_all(value, ('ctx', 'lo'), split_axis=0, concat_axis=0, tiled=T...  31.9 us
    ppermute x1, waiting for transfers between devices, on_device(): got = lax.ppermute(send, 'hi', [(0, 1), (1, 0)])  26.9 us
    all_to_all x1, blocking collectives, swap(): lax.all_to_all(value, ('ctx', 'lo'), split_axis=0, concat_axis=0, tiled=T...  23.7 us
    pallas_call x1, Pallas kernels, on_device(): pl.pallas_call(functools.partial(outer_kernel, place), grid=(2, half), in...  11.2 us
    pallas_call x1, Pallas kernels, on_device(): pl.pallas_call(functools.partial(states_kernel, place), grid=(half,), in_...  10.9 us
    pallas_call x1, Pallas kernels, on_device(): pl.pallas_call(functools.partial(inner_kernel, place), grid=(2, half), in...  8.51 us
    unnamed x16, local copies, waits for them, and re-layouts  5.7 us
    all_to_all x1, starting transfers between devices, swap(): lax.all_to_all(value, ('ctx', 'lo'), split_axis=0, concat_axis=0, tiled=T...  5.39 us
  transfers between devices with their start and end apart: 2, of which 2 were waited for; matrix products, arithmetic and copies ran while one was open for 0% of the time, Pallas kernels for 6%

profile of v2, /device:TPU:0, one launch (start us, length us, event | category | flops | bytes accessed | tf_op | source)
XLA Modules:
  0.0 135.0 jit_solution(16147523509479979437)
XLA Ops:
  0.6 0.0 copy-start
  0.6 1.9 %reshape.40 = bf16[128,8,1,4,128]{4,3,1,0,2:T(4,128)(2,1)S(1)} reshape(bf16[128,4096]{1,0:T(8,128)(2,1)} %param.6) | data formatting | bytes 2097152 | tf_op jit(solution)/shard_map/reshape | solution.py:299
  2.5 0.4 copy.16
  2.9 0.0 copy-done
  3.0 0.8 reshape.41
  3.7 0.0 copy-start.1
  3.7 0.4 copy.17
  4.2 0.0 copy-start.2
  4.2 0.0 copy-start.3
  4.2 1.2 constant_dynamic-update-slice_fusion.1
  5.4 1.2 constant_dynamic-update-slice_fusion
  6.6 0.0 copy-done.1
  6.6 0.8 copy_dynamic-update-slice_fusion.1
  7.3 0.8 copy_dynamic-update-slice_fusion
  8.1 0.6 pad_dynamic-update-slice_fusion
  8.7 5.4 %all-to-all-start = ((bf16[8,1296,128]{2,1,0:T(8,128)(2,1)}), bf16[8,1296,128]{2,1,0:T(8,128)(2,1)S(1)}, u32[]{:S(2)}, u32[]{:S(2)}) async-start(bf16[8,1296,128]{2,1,0:T(8,128)(2,1)} %pad_dynamic-update-slice_fusion), calls=%async_computation | async-start | bytes 5308416 | tf_op jit(solution)/shard_map/all_to_all | solution.py:296
  14.1 0.1 pad_maximum_fusion.flag_ref
  14.2 0.1 exponential_negate_fusion
  14.3 31.9 %all-to-all-done = bf16[8,1296,128]{2,1,0:T(8,128)(2,1)S(1)} async-done(((bf16[8,1296,128]{2,1,0:T(8,128)(2,1)}), bf16[8,1296,128]{2,1,0:T(8,128)(2,1)S(1)}, u32[]{:S(2)}, u32[]{:S(2)}) %all-to-all-start) | async-done | bytes 2654240 | tf_op jit(solution)/shard_map/all_to_all | solution.py:296
  46.2 0.1 squeeze.3.rate_ref
  46.3 10.9 %states.1 = (f32[2,4,128,512]{3,2,1,0:T(8,128)S(1)}, f32[2,4,128,512]{3,2,1,0:T(8,128)S(1)}, f32[2,4,8,512]{3,2,1,0:T(8,128)S(1)}, f32[2,4,8,512]{3,2,1,0:T(8,128)S(1)}, f32[392,512]{1,0:T(8,128)S(1)}) custom-call(f32[2]{0:T(128)S(1)} %pad_maximum_fusion.flag_ref, f32[8,128]{1,0:T(8,128)S(1)} %squeeze.3.rate_ref, bf16[2,4,1296,128]{3,2,1,0:T(8,128)(2,1)S(1)} %bitcast.24, ...), custom_call_target="tpu_custom_call" | custom-call | tf_op jit(solution)/shard_map/states/pallas_call | solution.py:344
  57.1 2.7 %collective-permute-start = (f32[392,512]{1,0:T(8,128)S(1)}, f32[392,512]{1,0:T(8,128)S(1)}, u32[]{:S(2)}, u32[]{:S(2)}) collective-permute-start(f32[392,512]{1,0:T(8,128)S(1)} %get-tuple-element.17.refs_5_), channel_id=1, source_target_pairs={{0,8},{8,0},{1,9},{9,1},{2,10},{10,2},{3,11},{11,3},{4,12},{12,4},... | collective-permute-start | bytes 2408456 | tf_op jit(solution)/shard_map/ppermute | solution.py:354
  59.8 8.5 %inner.1 = (f32[2,4,128,512]{3,2,1,0:T(8,128)S(1)}, f32[2,4,8,128]{3,2,1,0:T(8,128)S(1)}, f32[2,4,128,128]{3,2,1,0:T(8,128)S(1)}, f32[2,4,128,128]{3,2,1,0:T(8,128)S(1)}) custom-call(f32[8,128]{1,0:T(8,128)S(1)} %squeeze.3.rate_ref, bf16[2,4,1296,128]{3,2,1,0:T(8,128)(2,1)S(1)} %bitcast.26), custom_call_target="tpu_custom_call" | custom-call | flops 2000000000 | bytes 6000000 | tf_op jit(solution)/shard_map/inner/pallas_call | solution.py:356
  68.3 26.9 %collective-permute-done.refs_6_ = f32[392,512]{1,0:T(8,128)S(1)} collective-permute-done((f32[392,512]{1,0:T(8,128)S(1)}, f32[392,512]{1,0:T(8,128)S(1)}, u32[]{:S(2)}, u32[]{:S(2)}) %collective-permute-start) | collective-permute-done | bytes 802848 | tf_op jit(solution)/shard_map/ppermute | solution.py:354
  95.2 11.2 %outer.1 = bf16[2,4,784,128]{3,2,1,0:T(8,128)(2,1)S(1)} custom-call(f32[2]{0:T(128)S(1)} %pad_maximum_fusion.flag_ref, f32[8,128]{1,0:T(8,128)S(1)} %squeeze.3.rate_ref, bf16[2,4,1296,128]{3,2,1,0:T(8,128)(2,1)S(1)} %bitcast.27, f32[2,4,128,512]{3,2,1,0:T(8,128)S(1)} %get-tuple-element.13.refs_1_, f32[2,4,128,512]{3,2,1,0:T(8,128)S(1)} %get-tuple-element.14.refs_2_, ...), custom_call_target="tpu_custom_call" | custom-call | tf_op jit(solution)/shard_map/outer/pallas_call | solution.py:369
  106.4 23.7 %all_to_all.10 = bf16[8,784,128]{2,1,0:T(8,128)(2,1)S(1)} all-to-all(bf16[8,784,128]{2,1,0:T(8,128)(2,1)S(1)} %bitcast.28), channel_id=1, replica_groups=mesh['grp'=2,'hi'=2,'lo'=4,'ctx'=2] {'ctx','lo'}, dimensions={0} | all-to-all | bytes 3211264 | tf_op jit(solution)/shard_map/all_to_all | solution.py:296
  130.1 0.1 slice.18
  130.2 0.8 copy.20
  131.0 1.6 %reshape.46 = bf16[128,4096]{1,0:T(8,128)(2,1)} reshape(bf16[128,8,4,128]{3,2,1,0:T(4,128)(2,1)S(1)} %copy.20) | data formatting | bytes 2097152 | tf_op jit(solution)/shard_map/reshape | solution.py:390
  132.7 0.9 copy.22
  133.5 0.9 copy.21
  134.4 0.6 slice_bitcast_fusion.2
  (5 shorter events, 0.1 us)
Async XLA Ops:
  0.6 2.3 %copy-start = (bf16[128,4096]{1,0:T(8,128)(2,1)S(1)}, bf16[128,4096]{1,0:T(8,128)(2,1)}, u32[]{:S(2)}) copy-start(bf16[128,4096]{1,0:T(8,128)(2,1)} %param.7) | copy-start | bytes 3145732
  3.7 2.8 %copy-start.1 = (bf16[128,8,128]{2,1,0:T(8,128)(2,1)S(1)}, bf16[128,8,128]{2,1,0:T(8,128)(2,1)}, u32[]{:S(2)}) copy-start(bf16[128,8,128]{2,1,0:T(8,128)(2,1)} %param.10) | copy-start | bytes 786436
  4.2 3.2 %copy-start.2 = (bf16[128,8,128]{2,1,0:T(8,128)(2,1)S(1)}, bf16[128,8,128]{2,1,0:T(8,128)(2,1)}, u32[]{:S(2)}) copy-start(bf16[128,8,128]{2,1,0:T(8,128)(2,1)} %param.11) | copy-start | bytes 786436
  4.2 3.9 %copy-start.3 = (bf16[128,64]{0,1:T(8,128)(2,1)S(1)}, bf16[128,64]{0,1:T(8,128)(2,1)}, u32[]{:S(2)}) copy-start(bf16[128,64]{0,1:T(8,128)(2,1)} %param.8) | copy-start | bytes 49156
  8.7 5.5 %copy-start.4 = (f32[64]{0:T(128)S(1)}, f32[64]{0:T(128)}, u32[]{:S(2)}) copy-start(f32[64]{0:T(128)} %param.9) | copy-start | bytes 772
  8.7 37.5 %all-to-all-start = ((bf16[8,1296,128]{2,1,0:T(8,128)(2,1)}), bf16[8,1296,128]{2,1,0:T(8,128)(2,1)S(1)}, u32[]{:S(2)}, u32[]{:S(2)}) async-start(bf16[8,1296,128]{2,1,0:T(8,128)(2,1)} %pad_dynamic-update-slice_fusion), calls=%async_computation | async-start | bytes 5308416 | tf_op jit(solution)/shard_map/all_to_all | solution.py:296
  57.1 38.1 %collective-permute-start = (f32[392,512]{1,0:T(8,128)S(1)}, f32[392,512]{1,0:T(8,128)S(1)}, u32[]{:S(2)}, u32[]{:S(2)}) collective-permute-start(f32[392,512]{1,0:T(8,128)S(1)} %get-tuple-element.17.refs_5_), channel_id=1, source_target_pairs={{0,8},{8,0},{1,9},{9,1},{2,10},{10,2},{3,11},{11,3},{4,12},{12,4},... | collective-permute-start | bytes 2408456 | tf_op jit(solution)/shard_map/ppermute | solution.py:354

commit v3 on v1

v3 whole, which is shorter than its diff:
```python
import functools
from typing import NamedTuple

import jax
import jax.numpy as jnp
from jax import lax
from jax.experimental import pallas as pl
from jax.experimental.pallas import tpu as pltpu
from jax.sharding import PartitionSpec as P

HEADS = 64
HEAD_DIM = 64
STATE = 128
GROUPS = 8
LANES = 128
ROWS = 8
TILE = 16
LOG2E = 1.4426950408889634
CODE_SPAN = 250.0
F32 = jnp.float32
BF16 = jnp.bfloat16


def split2(value):
    hi = value.astype(BF16)
    return hi, (value - hi.astype(F32)).astype(BF16)


def split3(value):
    hi = value.astype(BF16)
    rest = value - hi.astype(F32)
    mid = rest.astype(BF16)
    return hi, mid, (rest - mid.astype(F32)).astype(BF16)


def dot(a, b):
    return lax.dot_general(a, b, (((1,), (0,)), ((), ())), preferred_element_type=F32)


def dot_nt(a, b):
    return lax.dot_general(a, b, (((1,), (1,)), ((), ())), preferred_element_type=F32)


def dot_tn(a, b):
    return lax.dot_general(a, b, (((0,), (0,)), ((), ())), preferred_element_type=F32)


def cat(parts, axis):
    return jnp.concatenate(parts, axis=axis)


def upper(size, strict):
    row = lax.broadcasted_iota(jnp.int32, (size, size), 0)
    col = lax.broadcasted_iota(jnp.int32, (size, size), 1)
    return row < col if strict else row <= col


def cumulate(rows, strict):
    tri = upper(rows.shape[1], strict).astype(F32).astype(BF16)
    sums = dot(cat([part.astype(F32) for part in split3(rows)], 0).astype(BF16), tri)
    size = rows.shape[0]
    return sums[:size] + sums[size : 2 * size] + sums[2 * size :]


def spread_matrix(terms, width):
    row = lax.broadcasted_iota(jnp.int32, (terms * ROWS, width), 0)
    col = lax.broadcasted_iota(jnp.int32, (terms * ROWS, width), 1)
    return (row % ROWS == col // HEAD_DIM).astype(F32).astype(BF16)


def spread_rows(rows, width):
    return dot_tn(rows, spread_matrix(2, width))


def two_terms(rows):
    hi, lo = split2(rows)
    return cat([hi.astype(F32), lo.astype(F32)], 0).astype(BF16)


def spread(cols, width):
    hi, lo = split2(cols)
    return dot(cat([hi.astype(F32), lo.astype(F32)], 1).astype(BF16), spread_matrix(2, width))


class Place(NamedTuple):
    tokens: int
    blocks: int

    @property
    def width(self):
        return self.blocks * LANES

    @property
    def b_row(self):
        return 2 * self.blocks * self.tokens

    @property
    def dt_row(self):
        return self.b_row + 2 * self.tokens

    @property
    def rows_in(self):
        return self.dt_row + TILE

    @property
    def rows_out(self):
        return (self.blocks + 2) * self.tokens + TILE

    def x(self, buf):
        return [buf[i * self.tokens : (i + 1) * self.tokens, :] for i in range(self.blocks)]

    def dy(self, buf):
        return [buf[i * self.tokens : (i + 1) * self.tokens, :] for i in range(self.blocks, 2 * self.blocks)]

    def b(self, buf):
        return buf[self.b_row : self.b_row + self.tokens, :]

    def c(self, buf):
        return buf[self.b_row + self.tokens : self.b_row + 2 * self.tokens, :]

    def dt(self, buf):
        return buf[self.dt_row : self.dt_row + TILE, :].astype(F32)[:ROWS]

    def steps(self, buf, rate):
        dt = self.dt(buf)
        return dt, cumulate(dt * rate, False)


def pack_kernel(place, count, copies, x_hbm, dy_hbm, b_hbm, c_hbm, dt_hbm, out, x_ref, dy_ref, b_ref, c_ref, dt_ref, b_wide, c_wide, dt_wide, sems):
    tokens, blocks, width = place.tokens, place.blocks, place.width
    heads = HEADS // count
    parts = [(b_hbm, b_ref), (c_hbm, c_ref), (dt_hbm, dt_ref), (x_hbm, x_ref), (dy_hbm, dy_ref)]
    moves = [pltpu.make_async_copy(source, target, sems.at[i]) for i, (source, target) in enumerate(parts)]
    for move in moves:
        move.start()
    for move in moves[:3]:
        move.wait()
    b_wide[...] = b_ref[...].astype(F32).reshape(b_wide.shape)
    c_wide[...] = c_ref[...].astype(F32).reshape(c_wide.shape)
    dt_wide[...] = dt_ref[...].astype(F32)
    for dest in range(count):
        mine = pl.ds(dest // copies, tokens, stride=GROUPS)
        out[dest, place.b_row : place.b_row + tokens, :] = b_wide[mine, :].astype(BF16)
        out[dest, place.b_row + tokens : place.dt_row, :] = c_wide[mine, :].astype(BF16)
        dt = dt_wide[dest * heads : (dest + 1) * heads, :]
        out[dest, place.dt_row :, :] = cat([dt, jnp.zeros((TILE - heads, tokens), F32)], 0).astype(BF16)
    for move, ref, first in ((moves[3], x_ref, 0), (moves[4], dy_ref, blocks * tokens)):
        move.wait()
        for dest in range(count):
            for i in range(blocks):
                at = dest * width + i * LANES
                out[dest, first + i * tokens : first + (i + 1) * tokens, :] = ref[:, at : at + LANES]


def unpack_kernel(place, count, copies, home, dx_hbm, ddt_hbm, db_hbm, dc_hbm, dx_ref, db_ref, dc_ref, ddt_ref, db_wide, dc_wide, ddt_wide, sems):
    tokens, blocks, width = place.tokens, place.blocks, place.width
    heads = HEADS // count
    moves = []
    step = max(count // 4, 1)
    for source in range(count):
        for i in range(blocks):
            at = source * width + i * LANES
            dx_ref[:, at : at + LANES] = home[source, i * tokens : (i + 1) * tokens, :]
        if (source + 1) % step == 0:
            columns = slice((source + 1 - step) * width, (source + 1) * width)
            moves.append(pltpu.make_async_copy(dx_ref.at[:, columns], dx_hbm.at[:, columns], sems.at[len(moves)]))
            moves[-1].start()
    first = blocks * tokens
    for to, at in ((db_wide, first), (dc_wide, first + tokens)):
        for group in range(GROUPS):
            part = home[group * copies, at : at + tokens, :].astype(F32)
            for copy in range(1, copies):
                part = part + home[group * copies + copy, at : at + tokens, :].astype(F32)
            to[pl.ds(group, tokens, stride=GROUPS), :] = part
    for source in range(count):
        ddt_wide[source * heads : (source + 1) * heads, :] = home[source, first + 2 * tokens :, :].astype(F32)[:heads]
    db_ref[...] = db_wide[...].reshape(db_ref.shape).astype(BF16)
    dc_ref[...] = dc_wide[...].reshape(dc_ref.shape).astype(BF16)
    ddt_ref[...] = ddt_wide[...].astype(BF16)
    for source, target in ((db_ref, db_hbm), (dc_ref, dc_hbm), (ddt_ref, ddt_hbm)):
        moves.append(pltpu.make_async_copy(source, target, sems.at[len(moves)]))
        moves[-1].start()
    for move in moves:
        move.wait()


def segment_decays(place, bufs, rate):
    dts = [place.dt(buf) for buf in bufs]
    cums = cumulate(cat([dt * rate for dt in dts], 0), False)
    cums = [cums[i * ROWS : (i + 1) * ROWS] for i in range(len(bufs))]
    starts, start = [], jnp.zeros((ROWS, 1), F32)
    for cum in cums:
        starts.append(start + cum)
        start = start + cum[:, place.tokens - 1 :]
    return dts, [start - one for one in starts], starts, start


def encode(value, scale):
    size = jnp.exp2(jnp.abs(value) * (CODE_SPAN / scale) - CODE_SPAN / 2)
    return jnp.where(value < 0.0, -size, size).astype(BF16)


def decode(code, scale):
    code = code.astype(F32)
    size = (jnp.log(jnp.abs(code)) * LOG2E + CODE_SPAN / 2) * (scale / CODE_SPAN)
    return jnp.where(code < 0.0, -size, size)


def totals_kernel(place, flag_ref, rate_ref, buf, u_ref, v_ref, own_ref, send_ref, now, log):
    seg, width = pl.program_id(0), place.width
    chunks = [buf.at[0, i] for i in range(buf.shape[1])]
    dts, ends, starts, total = segment_decays(place, chunks, rate_ref[...])
    x_hi, x_lo, dy_hi, dy_lo, b_all, c_all = [], [], [], [], [], []
    for i, chunk in enumerate(chunks):
        to_end, from_start = two_terms(dts[i] * jnp.exp(ends[i])), two_terms(jnp.exp(starts[i]))
        u_ref[0, i], v_ref[0, i] = to_end, from_start
        hi, lo = split2(spread_rows(to_end, width) * cat(place.x(chunk), 1).astype(F32))
        x_hi.append(hi)
        x_lo.append(lo)
        hi, lo = split2(spread_rows(from_start, width) * cat(place.dy(chunk), 1).astype(F32))
        dy_hi.append(hi)
        dy_lo.append(lo)
        b_all.append(place.b(chunk))
        c_all.append(place.c(chunk))
    b_turned = jnp.transpose(cat(b_all, 0).astype(F32)).astype(BF16)
    c_turned = jnp.transpose(cat(c_all, 0).astype(F32)).astype(BF16)
    now[seg] = dot(b_turned, cat(x_hi, 0)) + dot(b_turned, cat(x_lo, 0))
    now[2 + seg] = dot(c_turned, cat(dy_hi, 0)) + dot(c_turned, cat(dy_lo, 0))
    log[seg] = spread_rows(two_terms(jnp.broadcast_to(jnp.exp(total), (ROWS, LANES))), width)[:ROWS]

    @pl.when(seg == 1)
    def _():
        front = flag_ref[0] > 0.5
        values = [now[0], jnp.where(front, now[1], now[2]), now[3]]
        tops = [jnp.maximum(jnp.max(jnp.abs(value), axis=0, keepdims=True), 1e-30) for value in values]
        scales = [(top * 1.01).astype(BF16).astype(F32) for top in tops]
        for i, (value, scale) in enumerate(zip(values, scales)):
            send_ref[i * STATE : (i + 1) * STATE] = encode(value, scale)
        logs = [part.astype(F32) for i in range(2) for part in split2(log[i, :1])]
        notes = cat(scales + logs + [jnp.zeros((TILE - 7, width), F32)], 0)
        send_ref[3 * STATE :] = notes.astype(BF16)
        own_ref[:STATE] = values[0]
        own_ref[STATE : 2 * STATE] = values[2]
        own_ref[2 * STATE :] = cat([log[0], log[1]], 0)


def head_sums(values, width):
    hi, lo = split2(values)
    picker = spread_matrix(2, width)
    return (dot_nt(picker, hi) + dot_nt(picker, lo))[:ROWS]


def fold(value):
    total = value[:ROWS]
    for i in range(1, value.shape[0] // ROWS):
        total = total + value[i * ROWS : (i + 1) * ROWS]
    return total


def middle_kernel(place, rate_ref, buf, dx_ref, ddt_ref, db_ref, dc_ref):
    tokens, width, blocks = place.tokens, place.width, place.blocks
    rate = rate_ref[...]
    chunks = [buf.at[0, i] for i in range(buf.shape[1])]
    dts = [place.dt(chunk) for chunk in chunks]
    cums = cumulate(cat([dt * rate for dt in dts], 0), False)
    cums = [cums[i * ROWS : (i + 1) * ROWS] for i in range(len(chunks))]
    ends = [cum[:, tokens - 1 :] for cum in cums]
    starts = [jnp.exp(cum) for cum in cums]

    scaled, us, vs, end_wides, dt_wides, adds_s, adds_g, through = [], [], [], [], [], [], [], []
    for i, chunk in enumerate(chunks):
        dt_wide = spread_rows(two_terms(dts[i]), width)
        end_wide = spread_rows(two_terms(jnp.exp(ends[i] - cums[i])), width)
        start_wide = spread_rows(two_terms(starts[i]), width)
        xbar = dt_wide * cat(place.x(chunk), 1).astype(F32)
        u, v = split2(end_wide * xbar), split2(start_wide * cat(place.dy(chunk), 1).astype(F32))
        b_here, c_here = place.b(chunk), place.c(chunk)
        adds_s.append(dot_tn(cat([b_here, b_here], 0), cat(list(u), 0)))
        adds_g.append(dot_tn(cat([c_here, c_here], 0), cat(list(v), 0)))
        through.append(start_wide[tokens - 1 :, :])
        scaled.append(xbar)
        us.append(u)
        vs.append(v)
        end_wides.append(end_wide)
        dt_wides.append(dt_wide)
    states, grads = [jnp.zeros((STATE, width), F32)], [jnp.zeros((STATE, width), F32)]
    for i in range(len(chunks) - 1):
        states.append(through[i] * states[-1] + adds_s[i])
        grads.append(through[-1 - i] * grads[-1] + adds_g[-1 - i])
    grads = grads[::-1]
    corners = head_sums(cat([fold(through[i] * (states[i] * grads[i])) for i in range(len(chunks))], 0), width)

    mask = upper(tokens, False)
    left = lax.broadcasted_iota(jnp.int32, (tokens, LANES), 1) < HEAD_DIM
    none = jnp.zeros((tokens, LANES), F32)
    for i, chunk in enumerate(chunks):
        b_here, c_here = place.b(chunk), place.c(chunk)
        cum = cums[i] * LOG2E
        cols = jnp.transpose(cum)
        k_two = dot_nt(b_here, c_here)
        s_hi, s_lo = split2(states[i])
        g_hi, g_lo = split2(grads[i])
        b_grad = end_wides[i] * dot(cat([b_here, b_here], 1), cat([g_hi, g_lo], 0))
        c_state = dot(cat([c_here, c_here], 1), cat([s_hi, s_lo], 0))
        one_sum = jnp.zeros((tokens, tokens), F32)
        rows, alongs = [], []
        for block, (x_here, dy_here) in enumerate(zip(place.x(chunk), place.dy(chunk))):
            lanes = slice(block * LANES, (block + 1) * LANES)
            dy_f32 = dy_here.astype(F32)
            hi = scaled[i][:, lanes].astype(BF16).astype(F32)
            lo = scaled[i][:, lanes] - hi
            pair = cat(
                [
                    cat([jnp.where(left, hi, none), jnp.where(left, lo, none)], 1),
                    cat([jnp.where(left, none, hi), jnp.where(left, none, lo)], 1),
                ],
                0,
            ).astype(BF16)
            k_one = dot_nt(pair, cat([dy_here, dy_here], 1))
            tops, bottoms = [], []
            for side in range(2):
                head = 2 * block + side
                gap = jnp.where(mask, cum[head : head + 1, :] - cols[:, head : head + 1], -1e30)
                decay = jnp.exp2(gap)
                a_one = decay * k_one[side * tokens : (side + 1) * tokens]
                a_two = decay * k_two
                one_sum = one_sum + a_one
                rows.append(jnp.sum(a_one * k_two, axis=0, keepdims=True))
                hi_two, lo_two = split2(a_two)
                tops.append(hi_two)
                bottoms.append(lo_two)
            sides = cat([jnp.where(left, dy_f32, none), jnp.where(left, none, dy_f32)], 0).astype(BF16)
            both = dot(cat([cat(tops, 1), cat(bottoms, 1)], 0), sides)
            dxbar = both[:tokens] + both[tokens:] + b_grad[:, lanes]
            dx_ref[0, i, :, lanes] = dt_wides[i][:, lanes] * dxbar
            alongs.append(dxbar * x_here.astype(F32))
        if len(rows) < ROWS:
            rows.append(jnp.zeros((ROWS - len(rows), tokens), F32))
        (u_hi, u_lo), (v_hi, v_lo) = us[i], vs[i]
        db = dot(cat(list(split2(one_sum)), 1), cat([c_here, c_here], 0))
        dc = dot(cat(list(split2(jnp.transpose(one_sum))), 1), cat([b_here, b_here], 0))
        db_ref[0, i] = db + (dot_nt(u_hi, g_hi) + (dot_nt(u_hi, g_lo) + dot_nt(u_lo, g_hi)))
        dc_ref[0, i] = dc + (dot_nt(v_hi, s_hi) + (dot_nt(v_hi, s_lo) + dot_nt(v_lo, s_hi)))
        sums = head_sums(cat([cat(alongs, 1), cat(place.dy(chunk), 1).astype(F32) * c_state], 0), width)
        along = sums[:, :tokens]
        later = starts[i] * sums[:, tokens:]
        corner = jnp.sum(corners[:, i * ROWS : (i + 1) * ROWS], axis=1, keepdims=True)
        flow = dts[i] * along - cat(rows, 0) - later
        dlog = corner + jnp.sum(later, axis=1, keepdims=True) + cumulate(flow, True)
        ddt_ref[0, i] = along + rate * dlog


def finish_kernel(place, flag_ref, rate_ref, buf, u_ref, v_ref, own, got, dx_in, ddt_in, db_in, dc_in, out):
    seg, tokens, width = pl.program_id(0), place.tokens, place.width
    front, first = flag_ref[0], flag_ref[0] * (1 - seg) > 0.5
    final = (1.0 - flag_ref[0]) * seg > 0.5
    front = front > 0.5
    notes = got[3 * STATE :].astype(F32)
    sent0, sent2, logs = own[:STATE], own[STATE : 2 * STATE], (own[2 * STATE : 2 * STATE + 1], own[2 * STATE + ROWS : 2 * STATE + ROWS + 1])
    got0, got1, got2 = (decode(got[i * STATE : (i + 1) * STATE], notes[i : i + 1]) for i in range(3))
    mine = jnp.where(front, logs[1], logs[0])
    other = jnp.where(front, notes[3:4] + notes[4:5], notes[5:6] + notes[6:7])
    through = jnp.where(seg == 0, logs[0], logs[1])
    far = got1 + other * (jnp.where(front, sent2, sent0) + mine * jnp.where(front, got2, got0))
    near = jnp.where(front, got0, got2) + other * jnp.where(front, sent0, sent2)
    none = jnp.zeros_like(far)
    state = jnp.where(first, none, jnp.where(front, near, jnp.where(seg == 0, got0, far)))
    grad = jnp.where(final, none, jnp.where(front, jnp.where(seg == 0, far, got2), near))
    s_hi, s_lo = split2(state)
    g_hi, g_lo = split2(grad)
    s_both, g_both = cat([s_hi, s_lo], 0), cat([g_hi, g_lo], 0)
    corner = jnp.sum(head_sums(fold(through * (grad * state)), width), axis=1, keepdims=True)
    chunks = [buf.at[0, i] for i in range(buf.shape[1])]
    before, after = jnp.zeros((ROWS, 1), F32), jnp.zeros((ROWS, 1), F32)
    ins, laters, dts = [], [], []
    first_row = place.blocks * tokens
    for i, chunk in enumerate(chunks):
        u_wide, v_wide = spread_rows(u_ref[0, i], width), spread_rows(v_ref[0, i], width)
        b_here, c_here = place.b(chunk), place.c(chunk)
        b_grad = dot(cat([b_here, b_here], 1), g_both)
        c_state = dot(cat([c_here, c_here], 1), s_both)
        dx = (dx_in[0, i] + u_wide * b_grad).astype(BF16)
        for block in range(place.blocks):
            out[0, i, block * tokens : (block + 1) * tokens, :] = dx[:, block * LANES : (block + 1) * LANES]
        u = u_wide * cat(place.x(chunk), 1).astype(F32)
        v = v_wide * cat(place.dy(chunk), 1).astype(F32)
        u_hi, u_lo = split2(u)
        v_hi, v_lo = split2(v)
        db = db_in[0, i] + (dot_nt(u_hi, g_hi) + (dot_nt(u_hi, g_lo) + dot_nt(u_lo, g_hi)))
        dc = dc_in[0, i] + (dot_nt(v_hi, s_hi) + (dot_nt(v_hi, s_lo) + dot_nt(v_lo, s_hi)))
        out[0, i, first_row : first_row + tokens, :] = db.astype(BF16)
        out[0, i, first_row + tokens : first_row + 2 * tokens, :] = dc.astype(BF16)
        ins.append(head_sums(u * b_grad, width))
        laters.append(head_sums(v * c_state, width))
        dts.append(place.dt(chunk))
    into = cumulate(cat(ins, 0), True)
    over = cumulate(cat(laters, 0), True)
    tails = [jnp.sum(later, axis=1, keepdims=True) for later in laters]
    for i in range(len(chunks)):
        rows = slice(i * ROWS, (i + 1) * ROWS)
        rest = corner + before
        for tail in tails[i:]:
            rest = rest + tail
        dlog = rest + (into[rows] - over[rows])
        before = before + jnp.sum(ins[i], axis=1, keepdims=True)
        safe = jnp.where(dts[i] > 0.0, dts[i], 1.0)
        ddt = ddt_in[0, i] + ins[i] / safe + rate_ref[...] * dlog
        out[0, i, first_row + 2 * tokens :, :] = cat([ddt, jnp.zeros_like(ddt)], 0).astype(BF16)


def on_device(x_seq, dy_seq, dt_seq, a_log, b_seq, c_seq):
    tokens = x_seq.shape[0]
    half = lax.axis_size("lo")
    count = 2 * half
    heads = HEADS // count
    width = heads * HEAD_DIM
    copies = count // GROUPS
    place = Place(tokens, width // LANES)
    front = 1.0 - lax.axis_index("hi").astype(F32)
    flags = jnp.stack([front, 1.0 - front])

    def swap(value):
        return lax.all_to_all(value, ("ctx", "lo"), split_axis=0, concat_axis=0, tiled=True)

    rates = -jnp.exp(lax.dynamic_slice_in_dim(a_log, lax.axis_index(("ctx", "lo")) * heads, heads))
    rate = jnp.broadcast_to(jnp.pad(rates, (0, ROWS - heads))[:, None], (ROWS, LANES))

    def f32(*shape):
        return jax.ShapeDtypeStruct((2, half) + shape, F32)

    def bf16(*shape):
        return jax.ShapeDtypeStruct(shape, BF16)

    smem = pl.BlockSpec(memory_space=pltpu.SMEM)
    params = pltpu.CompilerParams(vmem_limit_bytes=40 * 1024 * 1024)

    def whole(*shape):
        return pl.BlockSpec(shape, lambda *k: (0,) * len(shape))

    def segment(*shape):
        return pl.BlockSpec((1, half) + shape, lambda s: (s, 0) + (0,) * len(shape))

    hbm, vmem = pl.BlockSpec(memory_space=pl.ANY), pl.BlockSpec(memory_space=pltpu.VMEM)
    seqs = (x_seq, dy_seq, b_seq, c_seq)
    wides = [pltpu.VMEM((tokens * GROUPS, STATE), F32), pltpu.VMEM((tokens * GROUPS, STATE), F32), pltpu.VMEM((HEADS, tokens), F32)]
    sent = pl.pallas_call(
        functools.partial(pack_kernel, place, count, copies),
        in_specs=[hbm] * 5,
        out_specs=vmem,
        out_shape=bf16(count, place.rows_in, LANES),
        scratch_shapes=[pltpu.VMEM(seq.shape, BF16) for seq in seqs]
        + [pltpu.VMEM((HEADS, tokens), BF16)]
        + wides
        + [pltpu.SemaphoreType.DMA((5,))],
        compiler_params=pltpu.CompilerParams(vmem_limit_bytes=58 * 1024 * 1024),
        name="pack",
    )(x_seq, dy_seq, b_seq, c_seq, dt_seq.T)
    buf = swap(sent).reshape(2, half, place.rows_in, LANES)

    owned, coded = (2 * STATE + 2 * ROWS, width), (3 * STATE + TILE, width)
    u_rows, v_rows, own, send = pl.pallas_call(
        functools.partial(totals_kernel, place),
        grid=(2,),
        in_specs=[smem, whole(ROWS, LANES), segment(place.rows_in, LANES)],
        out_specs=[segment(TILE, tokens), segment(TILE, tokens), whole(*owned), whole(*coded)],
        out_shape=[bf16(2, half, TILE, tokens), bf16(2, half, TILE, tokens), jax.ShapeDtypeStruct(owned, F32), bf16(*coded)],
        scratch_shapes=[pltpu.VMEM((4, STATE, width), F32), pltpu.VMEM((2, ROWS, width), F32)],
        compiler_params=params,
        name="totals",
    )(flags, rate, buf)
    got = lax.ppermute(send, "hi", [(0, 1), (1, 0)])

    within = [f32(tokens, width), f32(ROWS, tokens), f32(tokens, STATE), f32(tokens, STATE)]
    within_specs = [segment(tokens, width), segment(ROWS, tokens), segment(tokens, STATE), segment(tokens, STATE)]
    parts = pl.pallas_call(
        functools.partial(middle_kernel, place),
        grid=(2,),
        in_specs=[whole(ROWS, LANES), segment(place.rows_in, LANES)],
        out_specs=within_specs,
        out_shape=within,
        compiler_params=params,
        cost_estimate=pl.CostEstimate(flops=6_000_000_000, bytes_accessed=20_000_000, transcendentals=2_000_000),
        name="middle",
    )(rate, buf)
    out = pl.pallas_call(
        functools.partial(finish_kernel, place),
        grid=(2,),
        in_specs=[smem, whole(ROWS, LANES), segment(place.rows_in, LANES), segment(TILE, tokens), segment(TILE, tokens)]
        + [whole(*owned), whole(*coded)]
        + within_specs,
        out_specs=segment(place.rows_out, LANES),
        out_shape=bf16(2, half, place.rows_out, LANES),
        compiler_params=params,
        name="finish",
    )(flags, rate, buf, u_rows, v_rows, own, got, *parts)

    home = swap(out.reshape(count, place.rows_out, LANES))
    dx, ddt, db, dc = pl.pallas_call(
        functools.partial(unpack_kernel, place, count, copies),
        in_specs=[vmem],
        out_specs=[hbm] * 4,
        out_shape=[bf16(*x_seq.shape), bf16(HEADS, tokens), bf16(*b_seq.shape), bf16(*c_seq.shape)],
        scratch_shapes=[pltpu.VMEM(x_seq.shape, BF16), pltpu.VMEM(b_seq.shape, BF16), pltpu.VMEM(c_seq.shape, BF16), pltpu.VMEM((HEADS, tokens), BF16)]
        + wides
        + [pltpu.SemaphoreType.DMA((7,))],
        compiler_params=params,
        name="unpack",
    )(home)
    return dx, ddt.T, db, dc


def solution(mesh):
    parts, head, ctx = (mesh.shape[name] for name in ("grp", "head", "ctx"))
    split = jax.sharding.Mesh(mesh.devices.reshape(parts, 2, head // 2, ctx), ("grp", "hi", "lo", "ctx"))
    spec = P(("grp", "ctx", "hi", "lo"))
    return jax.shard_map(
        on_device,
        mesh=split,
        in_specs=(spec, spec, spec, P(), spec, spec),
        out_specs=(spec, spec, spec, spec),
        check_vma=False,
    )
```

time: 154 us -> 97.6 us (0.63)
  waiting for transfers between devices: 60 us -> 37.8 us
  blocking collectives: 42.5 us -> 23.7 us
  local copies, waits for them, and re-layouts: 13 us -> 0.08 us
  Pallas kernels: 30 us -> 27 us
    all_to_all x1, waiting for transfers between devices: 60 us -> 31.9 us  [swap(): lax.all_to_all(value, ('ctx', 'lo'), split_axis=0, concat_axis=0, tiled=T...]
    all_to_all x1, blocking collectives: 42.5 us -> 23.7 us  [swap(): lax.all_to_all(value, ('ctx', 'lo'), split_axis=0, concat_axis=0, tiled=T...]
    ppermute x1, waiting for transfers between devices: 0.01 us -> 5.86 us  [on_device(): got = lax.ppermute(send, 'hi', [(0, 1), (1, 0)])]
    unnamed x16 -> x2, local copies, waits for them, and re-layouts: 5.7 us -> 0.01 us
    reshape x5 -> x0, local copies, waits for them, and re-layouts: 5.07 us -> none  [the longest x4 3.46 us: by_owner(): value.reshape(tokens, count, blocks, LANES).transpose(1, 2, 0, 3)]
    pallas_call x3 -> x5, Pallas kernels: 30 us -> 27 us  [the longest x1 12.7 us: on_device(): pl.pallas_call(functools.partial(middle_kernel, place), grid=(2,), in_spe...]
    ppermute x1, starting transfers between devices: 0.07 us -> 2.65 us  [on_device(): got = lax.ppermute(send, 'hi', [(0, 1), (1, 0)])]
    all_to_all x1, starting transfers between devices: 7.41 us -> 5.27 us  [swap(): lax.all_to_all(value, ('ctx', 'lo'), split_axis=0, concat_axis=0, tiled=T...]
  transfers between devices with their start and end apart: 2 -> 2, of which waited for: 1 -> 2; matrix products, arithmetic and copies ran while one was open for 0% -> 0% of each run, Pallas kernels for 6% -> 13%
where the time goes in v3:
time: 97.6 us; the launch traced here: 97.3 us
  waiting for transfers between devices  37.8 us (39%)
  Pallas kernels  27 us (28%)
  blocking collectives  23.7 us (24%)
  starting transfers between devices  7.92 us (8%)
    all_to_all x1, waiting for transfers between devices, swap(): lax.all_to_all(value, ('ctx', 'lo'), split_axis=0, concat_axis=0, tiled=T...  31.9 us
    all_to_all x1, blocking collectives, swap(): lax.all_to_all(value, ('ctx', 'lo'), split_axis=0, concat_axis=0, tiled=T...  23.7 us
    pallas_call x1, Pallas kernels, on_device(): pl.pallas_call(functools.partial(middle_kernel, place), grid=(2,), in_spe...  12.7 us
    pallas_call x1, Pallas kernels, on_device(): pl.pallas_call(functools.partial(finish_kernel, place), grid=(2,), in_spe...  6.29 us
    ppermute x1, waiting for transfers between devices, on_device(): got = lax.ppermute(send, 'hi', [(0, 1), (1, 0)])  5.86 us
    all_to_all x1, starting transfers between devices, swap(): lax.all_to_all(value, ('ctx', 'lo'), split_axis=0, concat_axis=0, tiled=T...  5.27 us
    pallas_call x1, Pallas kernels, on_device(): pl.pallas_call(functools.partial(pack_kernel, place, count, copies), in_s...  3.47 us
    pallas_call x1, Pallas kernels, on_device(): pl.pallas_call(functools.partial(totals_kernel, place), grid=(2,), in_spe...  3.17 us
  transfers between devices with their start and end apart: 2, of which 2 were waited for; matrix products, arithmetic and copies ran while one was open for 0% of the time, Pallas kernels for 13%

profile of v3, /device:TPU:0, one launch (start us, length us, event | category | flops | bytes accessed | tf_op | source)
XLA Modules:
  0.0 97.3 jit_solution(10152429978961784335)
XLA Ops:
  0.6 3.5 %pack.1 = bf16[8,1296,128]{2,1,0:T(8,128)(2,1)} custom-call(bf16[128,4096]{1,0:T(8,128)(2,1)} %x_hbm.1, bf16[128,4096]{1,0:T(8,128)(2,1)} %dy_hbm.1, bf16[128,8,128]{2,1,0:T(8,128)(2,1)} %b_hbm.1, bf16[128,8,128]{2,1,0:T(8,128)(2,1)} %c_hbm.1, bf16[64,128]{1,0:T(8,128)(2,1)} %bitcast.10), custom_call_target="tpu_custom_call" | custom-call | tf_op jit(solution)/shard_map/pack/pallas_call | solution.py:446
  4.1 0.0 copy-start
  4.1 5.3 %all-to-all-start = ((bf16[8,1296,128]{2,1,0:T(8,128)(2,1)}), bf16[8,1296,128]{2,1,0:T(8,128)(2,1)S(1)}, u32[]{:S(2)}, u32[]{:S(2)}) async-start(bf16[8,1296,128]{2,1,0:T(8,128)(2,1)} %pack.1), calls=%async_computation | async-start | bytes 5308416 | tf_op jit(solution)/shard_map/all_to_all | solution.py:423
  9.4 0.1 pad_maximum_fusion.flag_ref
  9.5 0.0 copy-done
  9.5 0.1 exponential_negate_fusion
  9.5 31.9 %all-to-all-done = bf16[8,1296,128]{2,1,0:T(8,128)(2,1)S(1)} async-done(((bf16[8,1296,128]{2,1,0:T(8,128)(2,1)}), bf16[8,1296,128]{2,1,0:T(8,128)(2,1)S(1)}, u32[]{:S(2)}, u32[]{:S(2)}) %all-to-all-start) | async-done | bytes 2654240 | tf_op jit(solution)/shard_map/all_to_all | solution.py:423
  41.5 0.1 broadcast_in_dim.2.rate_ref
  41.6 3.2 %totals.1 = (bf16[2,4,16,128]{3,2,1,0:T(8,128)(2,1)S(1)}, bf16[2,4,16,128]{3,2,1,0:T(8,128)(2,1)S(1)}, f32[272,512]{1,0:T(8,128)S(1)}, bf16[400,512]{1,0:T(8,128)(2,1)S(1)}) custom-call(f32[2]{0:T(128)S(1)} %pad_maximum_fusion.flag_ref, f32[8,128]{1,0:T(8,128)S(1)} %broadcast_in_dim.2.rate_ref, bf16[2,4,1296,128]{3,2,1,0:T(8,128)(2,1)S(1)} %bitcast.6), custom_call_target="tpu_custom_call" | custom-call | tf_op jit(solution)/shard_map/totals/pallas_call | solution.py:461
  44.7 2.7 %collective-permute-start = (bf16[400,512]{1,0:T(8,128)(2,1)S(1)}, bf16[400,512]{1,0:T(8,128)(2,1)S(1)}, u32[]{:S(2)}, u32[]{:S(2)}) collective-permute-start(bf16[400,512]{1,0:T(8,128)(2,1)S(1)} %get-tuple-element.19), channel_id=1, source_target_pairs={{0,8},{8,0},{1,9},{9,1},{2,10},{10,2},{3,11},{11,3},{4,12},{12,4},... | collective-permute-start | bytes 1228808 | tf_op jit(solution)/shard_map/ppermute | solution.py:471
  47.4 12.7 %middle.1 = (f32[2,4,128,512]{3,2,1,0:T(8,128)S(1)}, f32[2,4,8,128]{3,2,1,0:T(8,128)S(1)}, f32[2,4,128,128]{3,2,1,0:T(8,128)S(1)}, f32[2,4,128,128]{3,2,1,0:T(8,128)S(1)}) custom-call(f32[8,128]{1,0:T(8,128)S(1)} %broadcast_in_dim.2.rate_ref, bf16[2,4,1296,128]{3,2,1,0:T(8,128)(2,1)S(1)} %bitcast.7), custom_call_target="tpu_custom_call" | custom-call | flops 6000000000 | bytes 20000000 | tf_op jit(solution)/shard_map/middle/pallas_call | solution.py:475
  60.1 5.9 %collective-permute-done.got = bf16[400,512]{1,0:T(8,128)(2,1)S(1)} collective-permute-done((bf16[400,512]{1,0:T(8,128)(2,1)S(1)}, bf16[400,512]{1,0:T(8,128)(2,1)S(1)}, u32[]{:S(2)}, u32[]{:S(2)}) %collective-permute-start) | collective-permute-done | bytes 409632 | tf_op jit(solution)/shard_map/ppermute | solution.py:471
  66.0 6.3 %finish.1 = bf16[2,4,784,128]{3,2,1,0:T(8,128)(2,1)S(1)} custom-call(f32[2]{0:T(128)S(1)} %pad_maximum_fusion.flag_ref, f32[8,128]{1,0:T(8,128)S(1)} %broadcast_in_dim.2.rate_ref, bf16[2,4,1296,128]{3,2,1,0:T(8,128)(2,1)S(1)} %bitcast.8, bf16[2,4,16,128]{3,2,1,0:T(8,128)(2,1)S(1)} %get-tuple-element.16.u_ref, ...), custom_call_target="tpu_custom_call" | custom-call | tf_op jit(solution)/shard_map/finish/pallas_call | solution.py:485
  72.3 23.7 %all_to_all.10.home = bf16[8,784,128]{2,1,0:T(8,128)(2,1)S(1)} all-to-all(bf16[8,784,128]{2,1,0:T(8,128)(2,1)S(1)} %bitcast.9), channel_id=1, replica_groups=mesh['grp'=2,'hi'=2,'lo'=4,'ctx'=2] {'ctx','lo'}, dimensions={0} | all-to-all | bytes 3211264 | tf_op jit(solution)/shard_map/all_to_all | solution.py:423
  95.9 1.4 %unpack.1 = (bf16[128,4096]{1,0:T(8,128)(2,1)}, bf16[64,128]{1,0:T(8,128)(2,1)}, bf16[128,8,128]{2,1,0:T(8,128)(2,1)}, bf16[128,8,128]{2,1,0:T(8,128)(2,1)}) custom-call(bf16[8,784,128]{2,1,0:T(8,128)(2,1)S(1)} %all_to_all.10.home), custom_call_target="tpu_custom_call" | custom-call | tf_op jit(solution)/shard_map/unpack/pallas_call | solution.py:498
Async XLA Ops:
  4.1 5.4 %copy-start = (f32[64]{0:T(128)S(1)}, f32[64]{0:T(128)}, u32[]{:S(2)}) copy-start(f32[64]{0:T(128)} %param.9) | copy-start | bytes 772
  4.1 37.4 %all-to-all-start = ((bf16[8,1296,128]{2,1,0:T(8,128)(2,1)}), bf16[8,1296,128]{2,1,0:T(8,128)(2,1)S(1)}, u32[]{:S(2)}, u32[]{:S(2)}) async-start(bf16[8,1296,128]{2,1,0:T(8,128)(2,1)} %pack.1), calls=%async_computation | async-start | bytes 5308416 | tf_op jit(solution)/shard_map/all_to_all | solution.py:423
  44.7 21.2 %collective-permute-start = (bf16[400,512]{1,0:T(8,128)(2,1)S(1)}, bf16[400,512]{1,0:T(8,128)(2,1)S(1)}, u32[]{:S(2)}, u32[]{:S(2)}) collective-permute-start(bf16[400,512]{1,0:T(8,128)(2,1)S(1)} %get-tuple-element.19), channel_id=1, source_target_pairs={{0,8},{8,0},{1,9},{9,1},{2,10},{10,2},{3,11},{11,3},{4,12},{12,4},... | collective-permute-start | bytes 1228808 | tf_op jit(solution)/shard_map/ppermute | solution.py:471

commit v4 on v3

v4 whole, which is shorter than its diff:
```python
import functools
from typing import NamedTuple

import jax
import jax.numpy as jnp
from jax import lax
from jax.experimental import pallas as pl
from jax.experimental.pallas import tpu as pltpu
from jax.sharding import PartitionSpec as P

HEADS = 64
HEAD_DIM = 64
STATE = 128
GROUPS = 8
LANES = 128
ROWS = 8
TILE = 16
LOG2E = 1.4426950408889634
CODE_SPAN = 250.0
PIECES = 1
F32 = jnp.float32
BF16 = jnp.bfloat16


def split2(value):
    hi = value.astype(BF16)
    return hi, (value - hi.astype(F32)).astype(BF16)


def split3(value):
    hi = value.astype(BF16)
    rest = value - hi.astype(F32)
    mid = rest.astype(BF16)
    return hi, mid, (rest - mid.astype(F32)).astype(BF16)


def dot(a, b):
    return lax.dot_general(a, b, (((1,), (0,)), ((), ())), preferred_element_type=F32)


def dot_nt(a, b):
    return lax.dot_general(a, b, (((1,), (1,)), ((), ())), preferred_element_type=F32)


def dot_tn(a, b):
    return lax.dot_general(a, b, (((0,), (0,)), ((), ())), preferred_element_type=F32)


def cat(parts, axis):
    return jnp.concatenate(parts, axis=axis)


def upper(size, strict):
    row = lax.broadcasted_iota(jnp.int32, (size, size), 0)
    col = lax.broadcasted_iota(jnp.int32, (size, size), 1)
    return row < col if strict else row <= col


def cumulate(rows, strict):
    tri = upper(rows.shape[1], strict).astype(F32).astype(BF16)
    sums = dot(cat([part.astype(F32) for part in split3(rows)], 0).astype(BF16), tri)
    size = rows.shape[0]
    return sums[:size] + sums[size : 2 * size] + sums[2 * size :]


def spread_matrix(terms, width):
    row = lax.broadcasted_iota(jnp.int32, (terms * ROWS, width), 0)
    col = lax.broadcasted_iota(jnp.int32, (terms * ROWS, width), 1)
    return (row % ROWS == col // HEAD_DIM).astype(F32).astype(BF16)


def spread_rows(rows, width):
    hi, lo = split2(rows)
    terms = cat([hi.astype(F32), lo.astype(F32)], 0).astype(BF16)
    return dot_tn(terms, spread_matrix(2, width))


def columns(rows):
    return jnp.transpose(cat([rows, jnp.zeros((LANES - rows.shape[0], rows.shape[1]), F32)], 0))


def widen(cols, first, width):
    lane = lax.broadcasted_iota(jnp.int32, cols.shape, 1)
    heads = [first + lane // HEAD_DIM + 2 * block for block in range(width // LANES)]
    return cat([jnp.take_along_axis(cols, head, axis=1) for head in heads], 1)


def head_products(values, factors):
    rows = values[0].shape[0]
    both = dot_nt(cat(list(values), 0), cat(list(factors), 0))
    size = factors[0].shape[0]
    return (both[:rows, :size] + (both[:rows, size:] + both[rows:, :size])) + both[rows:, size:]


class Place(NamedTuple):
    tokens: int
    half: int
    blocks: int
    pieces: int
    piece: int

    @property
    def width(self):
        return self.blocks * LANES

    @property
    def last(self):
        return self.piece == self.pieces - 1

    @property
    def b_row(self):
        return 2 * self.blocks * self.tokens

    @property
    def dt_row(self):
        return self.b_row + 2 * self.tokens

    @property
    def dt_rows(self):
        return -(-self.pieces * ROWS // TILE) * TILE

    @property
    def rows_in(self):
        return self.dt_row + self.dt_rows if self.piece == 0 else self.b_row

    @property
    def rows_out(self):
        return (self.blocks + (2 if self.last else 0)) * self.tokens + TILE

    def x(self, buf):
        return [buf[i * self.tokens : (i + 1) * self.tokens, :] for i in range(self.blocks)]

    def dy(self, buf):
        return [buf[i * self.tokens : (i + 1) * self.tokens, :] for i in range(self.blocks, 2 * self.blocks)]

    def b(self, buf):
        return buf[self.b_row : self.b_row + self.tokens, :]

    def c(self, buf):
        return buf[self.b_row + self.tokens : self.b_row + 2 * self.tokens, :]

    def dt(self, buf):
        return buf[self.dt_row : self.dt_row + self.dt_rows, :].astype(F32)[self.piece * ROWS : (self.piece + 1) * ROWS]

    def bufs(self, refs):
        return (refs[0], refs[0], refs[1:]) if self.piece == 0 else (refs[0], refs[1], refs[2:])


def pack_kernel(place, count, copies, *refs):
    hbm, (out, *refs) = refs[:5], refs[5:]
    b_ref, c_ref, dt_ref, x_ref, dy_ref, b_wide, c_wide, dt_wide, sems = refs
    tokens, blocks, width = place.tokens, place.blocks, place.width
    heads = HEADS // count // place.pieces
    moves = [pltpu.make_async_copy(source, target, sems.at[i]) for i, (source, target) in enumerate(zip(hbm, refs))]
    for move in moves:
        move.start()
    for move in moves[:3]:
        move.wait()
    b_wide[...] = b_ref[...].astype(F32).reshape(b_wide.shape)
    c_wide[...] = c_ref[...].astype(F32).reshape(c_wide.shape)
    dt_wide[...] = dt_ref[...].astype(F32)
    for dest in range(count):
        mine = pl.ds(dest // copies, tokens, stride=GROUPS)
        out[dest, place.b_row : place.b_row + tokens, :] = b_wide[mine, :].astype(BF16)
        out[dest, place.b_row + tokens : place.dt_row, :] = c_wide[mine, :].astype(BF16)
        rows = []
        for piece in range(place.pieces):
            at = (dest * place.pieces + piece) * heads
            rows += [dt_wide[at : at + heads, :]] + [jnp.zeros((ROWS - heads, tokens), F32)] * (heads < ROWS)
        rows += [jnp.zeros((place.dt_rows - place.pieces * ROWS, tokens), F32)] * (place.dt_rows > place.pieces * ROWS)
        out[dest, place.dt_row :, :] = cat(rows, 0).astype(BF16)
    for move, ref, first in ((moves[3], x_ref, 0), (moves[4], dy_ref, blocks * tokens)):
        move.wait()
        for dest in range(count):
            for i in range(blocks):
                at = dest * place.pieces * width + i * LANES
                out[dest, first + i * tokens : first + (i + 1) * tokens, :] = ref[:, at : at + LANES]


def pack_more_kernel(place, count, x_hbm, dy_hbm, out, x_ref, dy_ref, sems):
    tokens, blocks, width = place.tokens, place.blocks, place.width
    moves = [pltpu.make_async_copy(x_hbm, x_ref, sems.at[0]), pltpu.make_async_copy(dy_hbm, dy_ref, sems.at[1])]
    for move in moves:
        move.start()
    for move, ref, first in ((moves[0], x_ref, 0), (moves[1], dy_ref, blocks * tokens)):
        move.wait()
        for dest in range(count):
            for i in range(blocks):
                at = (dest * place.pieces + place.piece) * width + i * LANES
                out[dest, first + i * tokens : first + (i + 1) * tokens, :] = ref[:, at : at + LANES]


def unpack_kernel(places, count, copies, *refs):
    pieces, last = len(places), places[-1]
    homes, (dx_hbm, ddt_hbm, db_hbm, dc_hbm, dx_ref, db_ref, dc_ref, ddt_ref, db_wide, dc_wide, ddt_wide, sems) = refs[:pieces], refs[pieces:]
    tokens, blocks, width = last.tokens, last.blocks, last.width
    heads = HEADS // count // pieces
    moves = []
    step = max(count // 4, 1)
    for source in range(count):
        for piece, home in enumerate(homes):
            for i in range(blocks):
                at = (source * pieces + piece) * width + i * LANES
                dx_ref[:, at : at + LANES] = home[source, i * tokens : (i + 1) * tokens, :]
        if (source + 1) % step == 0:
            columns = slice((source + 1 - step) * pieces * width, (source + 1) * pieces * width)
            moves.append(pltpu.make_async_copy(dx_ref.at[:, columns], dx_hbm.at[:, columns], sems.at[len(moves)]))
            moves[-1].start()
    first = blocks * tokens
    for to, at in ((db_wide, first), (dc_wide, first + tokens)):
        for group in range(GROUPS):
            part = homes[-1][group * copies, at : at + tokens, :].astype(F32)
            for copy in range(1, copies):
                part = part + homes[-1][group * copies + copy, at : at + tokens, :].astype(F32)
            to[pl.ds(group, tokens, stride=GROUPS), :] = part
    for source in range(count):
        for place, home in zip(places, homes):
            at = (source * pieces + place.piece) * heads
            ddt_wide[at : at + heads, :] = home[source, place.rows_out - TILE :, :].astype(F32)[:heads]
    db_ref[...] = db_wide[...].reshape(db_ref.shape).astype(BF16)
    dc_ref[...] = dc_wide[...].reshape(dc_ref.shape).astype(BF16)
    ddt_ref[...] = ddt_wide[...].astype(BF16)
    for source, target in ((db_ref, db_hbm), (dc_ref, dc_hbm), (ddt_ref, ddt_hbm)):
        moves.append(pltpu.make_async_copy(source, target, sems.at[len(moves)]))
        moves[-1].start()
    for move in moves:
        move.wait()


def segment_decays(place, bufs, rate):
    dts = [place.dt(buf) for buf in bufs]
    cums = cumulate(cat([dt * rate for dt in dts], 0), False)
    cums = [cums[i * ROWS : (i + 1) * ROWS] for i in range(len(bufs))]
    starts, start = [], jnp.zeros((ROWS, 1), F32)
    for cum in cums:
        starts.append(start + cum)
        start = start + cum[:, place.tokens - 1 :]
    return dts, [start - one for one in starts], starts


def encode(value, scale):
    size = jnp.exp2(jnp.abs(value) * (CODE_SPAN / scale) - CODE_SPAN / 2)
    return jnp.where(value < 0.0, -size, size).astype(BF16)


def decode(code, scale):
    code = code.astype(F32)
    size = (jnp.log(jnp.abs(code)) * LOG2E + CODE_SPAN / 2) * (scale / CODE_SPAN)
    return jnp.where(code < 0.0, -size, size)


def totals_kernel(place, flag_ref, rate_ref, *refs):
    xy_ref, bc_ref, (u_rows, u_parts, v_parts, own_ref, send_ref) = place.bufs(refs)
    width, tokens = place.width, place.tokens
    totals_s, totals_g, logs = [], [], []
    for seg in range(2):
        xys, bcs = ([ref.at[seg, i] for i in range(place.half)] for ref in (xy_ref, bc_ref))
        dts, ends, starts = segment_decays(place, bcs, rate_ref[...])
        for i, xy in enumerate(xys):
            u_rows[seg, i] = dts[i] * jnp.exp(ends[i])
            rows = slice(i * tokens, (i + 1) * tokens)
            hi, lo = split2(spread_rows(u_rows[seg, i], width) * cat(place.x(xy), 1).astype(F32))
            u_parts[seg, 0, rows], u_parts[seg, 1, rows] = hi, lo
            start_wide = spread_rows(jnp.exp(starts[i]), width)
            hi, lo = split2(start_wide * cat(place.dy(xy), 1).astype(F32))
            v_parts[seg, 0, rows], v_parts[seg, 1, rows] = hi, lo
        b_turned = jnp.transpose(cat([place.b(bc) for bc in bcs], 0).astype(F32)).astype(BF16)
        c_turned = jnp.transpose(cat([place.c(bc) for bc in bcs], 0).astype(F32)).astype(BF16)
        totals_s.append(dot(b_turned, u_parts[seg, 0]) + dot(b_turned, u_parts[seg, 1]))
        totals_g.append(dot(c_turned, v_parts[seg, 0]) + dot(c_turned, v_parts[seg, 1]))
        logs.append(jnp.broadcast_to(start_wide[tokens - 1 :, :], (ROWS, width)))
    front = flag_ref[0] > 0.5
    values = [totals_s[0], jnp.where(front, totals_s[1], totals_g[0]), totals_g[1]]
    tops = [jnp.maximum(jnp.max(jnp.abs(value), axis=0, keepdims=True), 1e-30) for value in values]
    scales = [(top * 1.01).astype(BF16).astype(F32) for top in tops]
    for i, (value, scale) in enumerate(zip(values, scales)):
        send_ref[i * STATE : (i + 1) * STATE] = encode(value, scale)
    notes = scales + [part.astype(F32) for log in logs for part in split2(log[:1])]
    send_ref[3 * STATE :] = cat(notes + [jnp.zeros((TILE - len(notes), width), F32)], 0).astype(BF16)
    own_ref[:STATE] = values[0]
    own_ref[STATE : 2 * STATE] = values[2]
    own_ref[2 * STATE :] = cat(logs, 0)


def head_sums(values, width):
    hi, lo = split2(values)
    picker = spread_matrix(2, width)
    return (dot_nt(picker, hi) + dot_nt(picker, lo))[:ROWS]


def fold(value):
    total = value[:ROWS]
    for i in range(1, value.shape[0] // ROWS):
        total = total + value[i * ROWS : (i + 1) * ROWS]
    return total


def middle_kernel(place, rate_ref, *refs):
    xy_ref, bc_ref, outs = place.bufs(refs)
    for seg in range(2):
        chunks = [ref.at[seg] for ref in (xy_ref, bc_ref)]
        middle_segment(place, rate_ref[...], *chunks, *[ref.at[seg] for ref in outs])


def middle_segment(place, rate, xy_ref, bc_ref, dx_ref, ddt_ref, db_ref, dc_ref):
    tokens, width = place.tokens, place.width
    chunks, xys = ([ref.at[i] for i in range(place.half)] for ref in (bc_ref, xy_ref))
    dts = [place.dt(chunk) for chunk in chunks]
    cums = cumulate(cat([dt * rate for dt in dts], 0), False)
    cums = [cums[i * ROWS : (i + 1) * ROWS] for i in range(len(chunks))]
    ends = [cum[:, tokens - 1 :] for cum in cums]
    starts = [jnp.exp(cum) for cum in cums]

    us, vs, end_wides, adds_s, adds_g, through = [], [], [], [], [], []
    for i, chunk in enumerate(chunks):
        cols = columns(cat([dts[i] * jnp.exp(ends[i] - cums[i]), starts[i]], 0))
        end_wide, start_wide = widen(cols, 0, width), widen(cols, ROWS, width)
        u, v = split2(end_wide * cat(place.x(xys[i]), 1).astype(F32)), split2(start_wide * cat(place.dy(xys[i]), 1).astype(F32))
        b_here, c_here = place.b(chunk), place.c(chunk)
        adds_s.append(dot_tn(cat([b_here, b_here], 0), cat(list(u), 0)))
        adds_g.append(dot_tn(cat([c_here, c_here], 0), cat(list(v), 0)))
        through.append(start_wide[tokens - 1 :, :])
        us.append(u)
        vs.append(v)
        end_wides.append(end_wide)
    states, grads = [jnp.zeros((STATE, width), F32)], [jnp.zeros((STATE, width), F32)]
    for i in range(len(chunks) - 1):
        states.append(through[i] * states[-1] + adds_s[i])
        grads.append(through[-1 - i] * grads[-1] + adds_g[-1 - i])
    grads = grads[::-1]
    corners = head_sums(cat([fold(through[i] * (states[i] * grads[i])) for i in range(len(chunks))], 0), width)

    mask = upper(tokens, False)
    left = lax.broadcasted_iota(jnp.int32, (tokens, LANES), 1) < HEAD_DIM
    left, right = left.astype(F32).astype(BF16), (~left).astype(F32).astype(BF16)
    for i, chunk in enumerate(chunks):
        b_here, c_here = place.b(chunk), place.c(chunk)
        cum = cums[i] * LOG2E
        cols = jnp.transpose(cum - jnp.log(jnp.where(dts[i] > 0.0, dts[i], 1.0)) * LOG2E)
        k_two = dot_nt(b_here, c_here)
        s_hi, s_lo = split2(states[i])
        g_hi, g_lo = split2(grads[i])
        b_grad = end_wides[i] * dot(cat([b_here, b_here], 1), cat([g_hi, g_lo], 0))
        c_state = dot(cat([c_here, c_here], 1), cat([s_hi, s_lo], 0))
        one_sum = jnp.zeros((tokens, tokens), F32)
        rows, alongs = [], []
        for block, (x_here, dy_here) in enumerate(zip(place.x(xys[i]), place.dy(xys[i]))):
            lanes = slice(block * LANES, (block + 1) * LANES)
            sides = cat([dy_here * left, dy_here * right], 0)
            k_one = dot_nt(x_here, sides)
            tops, bottoms = [], []
            for side in range(2):
                head = 2 * block + side
                gap = jnp.where(mask, cum[head : head + 1, :] - cols[:, head : head + 1], -1e30)
                decay = jnp.exp2(gap)
                a_one = decay * k_one[:, side * tokens : (side + 1) * tokens]
                a_two = decay * k_two
                one_sum = one_sum + a_one
                rows.append(jnp.sum(a_one * k_two, axis=0, keepdims=True))
                hi_two, lo_two = split2(a_two)
                tops.append(hi_two)
                bottoms.append(lo_two)
            both = dot(cat([cat(tops, 1), cat(bottoms, 1)], 0), sides)
            dx = both[:tokens] + both[tokens:] + b_grad[:, lanes]
            dx_ref[i, :, lanes] = dx
            alongs.append(dx * x_here.astype(F32))
        if len(rows) < ROWS:
            rows.append(jnp.zeros((ROWS - len(rows), tokens), F32))
        db = dot(cat(list(split2(one_sum)), 1), cat([c_here, c_here], 0))
        dc = dot(cat(list(split2(jnp.transpose(one_sum))), 1), cat([b_here, b_here], 0))
        db_ref[i] = db + head_products(us[i], (g_hi, g_lo))
        dc_ref[i] = dc + head_products(vs[i], (s_hi, s_lo))
        sums = head_sums(cat([cat(alongs, 1), cat(place.dy(xys[i]), 1).astype(F32) * c_state], 0), width)
        along = sums[:, :tokens]
        later = starts[i] * sums[:, tokens:]
        corner = jnp.sum(corners[:, i * ROWS : (i + 1) * ROWS], axis=1, keepdims=True)
        flow = along - cat(rows, 0) - later
        dlog = corner + jnp.sum(later, axis=1, keepdims=True) + cumulate(flow, True)
        ddt_ref[i] = along / jnp.where(dts[i] > 0.0, dts[i], 1.0) + rate * dlog


def finish_kernel(place, flag_ref, rate_ref, *refs):
    xy_ref, bc_ref, (u_rows, u_parts, v_parts, own, got, dx_in, ddt_in, db_in, dc_in, *refs) = place.bufs(refs)
    old = [] if place.piece == 0 else [refs.pop(0), refs.pop(0)]
    out, *new = refs
    rate, tokens, width = rate_ref[...], place.tokens, place.width
    front = flag_ref[0] > 0.5
    notes = got[3 * STATE :].astype(F32)
    sent0, sent2, logs = own[:STATE], own[STATE : 2 * STATE], (own[2 * STATE : 2 * STATE + 1], own[2 * STATE + ROWS : 2 * STATE + ROWS + 1])
    got0, got1, got2 = (decode(got[i * STATE : (i + 1) * STATE], notes[i : i + 1]) for i in range(3))
    mine = jnp.where(front, logs[1], logs[0])
    other = jnp.where(front, notes[3:4] + notes[4:5], notes[5:6] + notes[6:7])
    far = got1 + other * (jnp.where(front, sent2, sent0) + mine * jnp.where(front, got2, got0))
    near = jnp.where(front, got0, got2) + other * jnp.where(front, sent0, sent2)
    none = jnp.zeros_like(far)
    states = [jnp.where(front, none, got0), jnp.where(front, near, far)]
    grads = [jnp.where(front, far, near), jnp.where(front, got2, none)]
    for seg, (state, grad, through) in enumerate(zip(states, grads, logs)):
        s_hi, s_lo = split2(state)
        g_hi, g_lo = split2(grad)
        corner = jnp.sum(head_sums(fold(through * (grad * state)), width), axis=1, keepdims=True)
        xys, bcs = ([ref.at[seg, i] for i in range(place.half)] for ref in (xy_ref, bc_ref))
        b_all, c_all = cat([place.b(bc) for bc in bcs], 0), cat([place.c(bc) for bc in bcs], 0)
        b_grad = dot(cat([b_all, b_all], 1), cat([g_hi, g_lo], 0))
        c_state = dot(cat([c_all, c_all], 1), cat([s_hi, s_lo], 0))
        u_hi, u_lo, v_hi, v_lo = u_parts[seg, 0], u_parts[seg, 1], v_parts[seg, 0], v_parts[seg, 1]
        db = head_products((u_hi, u_lo), (g_hi, g_lo))
        dc = head_products((v_hi, v_lo), (s_hi, s_lo))
        ins = []
        for i, xy in enumerate(xys):
            rows = slice(i * tokens, (i + 1) * tokens)
            extra = widen(columns(u_rows[seg, i]), 0, width) * b_grad[rows]
            dx = (dx_in[seg, i] + extra).astype(BF16)
            for block in range(place.blocks):
                out[seg, i, block * tokens : (block + 1) * tokens, :] = dx[:, block * LANES : (block + 1) * LANES]
            ins.append(extra * cat(place.x(xy), 1).astype(F32))
            db_here, dc_here = db_in[seg, i] + db[rows], dc_in[seg, i] + dc[rows]
            if old:
                db_here, dc_here = db_here + old[0][seg, i], dc_here + old[1][seg, i]
            if place.last:
                first = place.blocks * tokens
                out[seg, i, first : first + tokens, :] = db_here.astype(BF16)
                out[seg, i, first + tokens : first + 2 * tokens, :] = dc_here.astype(BF16)
            else:
                new[0][seg, i], new[1][seg, i] = db_here, dc_here
        ins = head_sums(cat(ins, 0), width)
        laters = head_sums((v_hi.astype(F32) + v_lo.astype(F32)) * c_state, width)
        ins, laters = ([sums[:, i * tokens : (i + 1) * tokens] for i in range(place.half)] for sums in (ins, laters))
        over = cumulate(cat([one - other for one, other in zip(ins, laters)], 0), True)
        rest = corner
        for later in laters:
            rest = rest + jnp.sum(later, axis=1, keepdims=True)
        for i, bc in enumerate(bcs):
            dlog = rest + over[i * ROWS : (i + 1) * ROWS]
            rest = rest + jnp.sum(ins[i] - laters[i], axis=1, keepdims=True)
            dt = place.dt(bc)
            ddt = ddt_in[seg, i] + ins[i] / jnp.where(dt > 0.0, dt, 1.0) + rate * dlog
            out[seg, i, place.rows_out - TILE :, :] = cat([ddt, jnp.zeros_like(ddt)], 0).astype(BF16)


def on_device(x_seq, dy_seq, dt_seq, a_log, b_seq, c_seq):
    tokens = x_seq.shape[0]
    half = lax.axis_size("lo")
    count = 2 * half
    heads = HEADS // count
    blocks = heads * HEAD_DIM // LANES
    copies = count // GROUPS
    pieces = PIECES if blocks % PIECES == 0 else 1
    places = [Place(tokens, half, blocks // pieces, pieces, piece) for piece in range(pieces)]
    width = places[0].width
    front = 1.0 - lax.axis_index("hi").astype(F32)
    flags = jnp.stack([front, 1.0 - front])

    def swap(value):
        return lax.all_to_all(value, ("ctx", "lo"), split_axis=0, concat_axis=0, tiled=True)

    rates = -jnp.exp(lax.dynamic_slice_in_dim(a_log, lax.axis_index(("ctx", "lo")) * heads, heads)).reshape(pieces, -1)
    rates = jnp.pad(rates, ((0, 0), (0, ROWS - heads // pieces)))
    rates = jnp.broadcast_to(rates[:, :, None], (pieces, ROWS, LANES))

    def f32(*shape):
        return jax.ShapeDtypeStruct((2, half) + shape, F32)

    def bf16(*shape):
        return jax.ShapeDtypeStruct(shape, BF16)

    smem = pl.BlockSpec(memory_space=pltpu.SMEM)
    hbm, vmem = pl.BlockSpec(memory_space=pl.ANY), pl.BlockSpec(memory_space=pltpu.VMEM)
    params = pltpu.CompilerParams(vmem_limit_bytes=24 * 1024 * 1024)
    alone = pltpu.CompilerParams(vmem_limit_bytes=58 * 1024 * 1024)
    wides = [pltpu.VMEM((tokens * GROUPS, STATE), F32), pltpu.VMEM((tokens * GROUPS, STATE), F32), pltpu.VMEM((HEADS, tokens), F32)]
    seqs = (b_seq, c_seq, dt_seq.T, x_seq, dy_seq)

    def packed(place):
        if place.piece == 0:
            return pl.pallas_call(
                functools.partial(pack_kernel, place, count, copies),
                in_specs=[hbm] * 5,
                out_specs=vmem,
                out_shape=bf16(count, place.rows_in, LANES),
                scratch_shapes=[pltpu.VMEM(seq.shape, BF16) for seq in seqs] + wides + [pltpu.SemaphoreType.DMA((5,))],
                compiler_params=alone,
                name="pack",
            )(*seqs)
        return pl.pallas_call(
            functools.partial(pack_more_kernel, place, count),
            in_specs=[hbm] * 2,
            out_specs=vmem,
            out_shape=bf16(count, place.rows_in, LANES),
            scratch_shapes=[pltpu.VMEM(x_seq.shape, BF16), pltpu.VMEM(x_seq.shape, BF16), pltpu.SemaphoreType.DMA((2,))],
            compiler_params=params,
            name="pack_more",
        )(x_seq, dy_seq)

    bufs = [swap(packed(place)).reshape(2, half, place.rows_in, LANES) for place in places]
    owned, coded = (2 * STATE + 2 * ROWS, width), (3 * STATE + TILE, width)
    within = [f32(tokens, width), f32(ROWS, tokens), f32(tokens, STATE), f32(tokens, STATE)]
    parts_shape = bf16(2, 2, half * tokens, width)
    def data_of(place):
        return [bufs[0]] if place.piece == 0 else [bufs[place.piece], bufs[0]]

    def totals_of(place):
        data = data_of(place)
        return pl.pallas_call(
            functools.partial(totals_kernel, place),
            in_specs=[smem] + [vmem] * (1 + len(data)),
            out_specs=[vmem] * 5,
            out_shape=[f32(ROWS, tokens), parts_shape, parts_shape, jax.ShapeDtypeStruct(owned, F32), bf16(*coded)],
            compiler_params=params,
            name="totals",
        )(flags, rates[place.piece], *data)

    def middle_of(place, rate):
        data = data_of(place)
        return pl.pallas_call(
            functools.partial(middle_kernel, place),
            in_specs=[vmem] * (1 + len(data)),
            out_specs=[vmem] * 4,
            out_shape=within,
            compiler_params=params,
            cost_estimate=pl.CostEstimate(flops=6_000_000_000, bytes_accessed=20_000_000, transcendentals=2_000_000),
            name="middle",
        )(rate, *data)

    def finish_of(place, passed, got, parts, sums):
        data = data_of(place)
        new = [] if place.last else [f32(tokens, STATE)] * 2
        return pl.pallas_call(
            functools.partial(finish_kernel, place),
            in_specs=[smem] + [vmem] * (10 + len(data) + len(sums)),
            out_specs=[vmem] * (1 + len(new)),
            out_shape=[bf16(2, half, place.rows_out, LANES)] + new,
            compiler_params=params,
            name="finish",
        )(flags, rates[place.piece], *data, *passed, got, *parts, *sums)

    def after(value, *others):
        return lax.optimization_barrier((value, *others))[0]

    homes, sums, pending = [], [], []
    for place in places:
        *passed, send = totals_of(place)
        pending.append((place, passed, lax.ppermute(send, "hi", [(0, 1), (1, 0)]), send))
    rate = rates[0]
    for i, (place, passed, got, _) in enumerate(pending):
        parts = middle_of(place, rate)
        if not place.last:
            got = after(got, pending[i + 1][3])
        out, *sums = finish_of(place, passed, got, parts, sums)
        homes.append(swap(out.reshape(count, place.rows_out, LANES)))
        if not place.last:
            rate = after(rates[i + 1], out)

    dx, ddt, db, dc = pl.pallas_call(
        functools.partial(unpack_kernel, places, count, copies),
        in_specs=[vmem] * pieces,
        out_specs=[hbm] * 4,
        out_shape=[bf16(*x_seq.shape), bf16(HEADS, tokens), bf16(*b_seq.shape), bf16(*c_seq.shape)],
        scratch_shapes=[pltpu.VMEM(x_seq.shape, BF16), pltpu.VMEM(b_seq.shape, BF16), pltpu.VMEM(c_seq.shape, BF16), pltpu.VMEM((HEADS, tokens), BF16)]
        + wides
        + [pltpu.SemaphoreType.DMA((7,))],
        compiler_params=params,
        name="unpack",
    )(*homes)
    return dx, ddt.T, db, dc


def solution(mesh):
    parts, head, ctx = (mesh.shape[name] for name in ("grp", "head", "ctx"))
    split = jax.sharding.Mesh(mesh.devices.reshape(parts, 2, head // 2, ctx), ("grp", "hi", "lo", "ctx"))
    spec = P(("grp", "ctx", "hi", "lo"))
    return jax.shard_map(
        on_device,
        mesh=split,
        in_specs=(spec, spec, spec, P(), spec, spec),
        out_specs=(spec, spec, spec, spec),
        check_vma=False,
    )
```

time: 97.6 us -> 95.9 us (0.983)
  Pallas kernels: 27 us -> 23.9 us
  waiting for transfers between devices: 37.8 us -> 39.1 us
    pallas_call x5, Pallas kernels: 27 us -> 23.9 us  [the longest x1 11.5 us: middle_of(): pl.pallas_call(functools.partial(middle_kernel, place), in_specs=[vmem] *...]
    ppermute x1, waiting for transfers between devices: 5.86 us -> 7.12 us  [on_device(): lax.ppermute(send, 'hi', [(0, 1), (1, 0)])]
  transfers between devices with their start and end apart: 2 -> 2, of which waited for: 2 -> 2; matrix products, arithmetic and copies ran while one was open for 0% -> 0% of each run, Pallas kernels for 13% -> 12%
where the time goes in v4:
time: 95.9 us; the launch traced here: 95.6 us
  waiting for transfers between devices  39.1 us (41%)
  Pallas kernels  23.9 us (25%)
  blocking collectives  23.7 us (25%)
  starting transfers between devices  7.92 us (8%)
    all_to_all x1, waiting for transfers between devices, swap(): lax.all_to_all(value, ('ctx', 'lo'), split_axis=0, concat_axis=0, tiled=T...  31.9 us
    all_to_all x1, blocking collectives, swap(): lax.all_to_all(value, ('ctx', 'lo'), split_axis=0, concat_axis=0, tiled=T...  23.7 us
    pallas_call x1, Pallas kernels, middle_of(): pl.pallas_call(functools.partial(middle_kernel, place), in_specs=[vmem] *...  11.5 us
    ppermute x1, waiting for transfers between devices, on_device(): lax.ppermute(send, 'hi', [(0, 1), (1, 0)])  7.12 us
    all_to_all x1, starting transfers between devices, swap(): lax.all_to_all(value, ('ctx', 'lo'), split_axis=0, concat_axis=0, tiled=T...  5.27 us
    pallas_call x1, Pallas kernels, finish_of(): pl.pallas_call(functools.partial(finish_kernel, place), in_specs=[smem] +...  4.7 us
    pallas_call x1, Pallas kernels, packed(): pl.pallas_call(functools.partial(pack_kernel, place, count, copies), in_s...  3.47 us
    pallas_call x1, Pallas kernels, totals_of(): pl.pallas_call(functools.partial(totals_kernel, place), in_specs=[smem] +...  2.88 us
  transfers between devices with their start and end apart: 2, of which 2 were waited for; matrix products, arithmetic and copies ran while one was open for 0% of the time, Pallas kernels for 12%

profile of v4, /device:TPU:0, one launch (start us, length us, event | category | flops | bytes accessed | tf_op | source)
XLA Modules:
  0.0 95.6 jit_solution(298908754033931010)
XLA Ops:
  0.6 3.5 %pack.1 = bf16[8,1296,128]{2,1,0:T(8,128)(2,1)} custom-call(bf16[128,8,128]{2,1,0:T(8,128)(2,1)} %refs_0_.1, bf16[128,8,128]{2,1,0:T(8,128)(2,1)} %refs_1_.1, bf16[64,128]{1,0:T(8,128)(2,1)} %bitcast.10, bf16[128,4096]{1,0:T(8,128)(2,1)} %refs_3_.1, bf16[128,4096]{1,0:T(8,128)(2,1)} %refs_4_.1), custom_call_target="tpu_custom_call" | custom-call | tf_op jit(solution)/shard_map/pack/pallas_call | solution.py:476
  4.1 0.0 copy-start
  4.1 5.3 %all-to-all-start = ((bf16[8,1296,128]{2,1,0:T(8,128)(2,1)}), bf16[8,1296,128]{2,1,0:T(8,128)(2,1)S(1)}, u32[]{:S(2)}, u32[]{:S(2)}) async-start(bf16[8,1296,128]{2,1,0:T(8,128)(2,1)} %pack.1), calls=%async_computation | async-start | bytes 5308416 | tf_op jit(solution)/shard_map/all_to_all | solution.py:455
  9.4 0.1 pad_maximum_fusion.flag_ref
  9.5 0.0 copy-done
  9.5 0.1 exponential_negate_fusion
  9.5 31.9 %all-to-all-done = bf16[8,1296,128]{2,1,0:T(8,128)(2,1)S(1)} async-done(((bf16[8,1296,128]{2,1,0:T(8,128)(2,1)}), bf16[8,1296,128]{2,1,0:T(8,128)(2,1)S(1)}, u32[]{:S(2)}, u32[]{:S(2)}) %all-to-all-start) | async-done | bytes 2654240 | tf_op jit(solution)/shard_map/all_to_all | solution.py:455
  41.5 0.1 squeeze.2.rate_ref
  41.6 2.9 %totals.1 = (f32[2,4,8,128]{3,2,1,0:T(8,128)S(1)}, bf16[2,2,512,512]{3,2,1,0:T(8,128)(2,1)S(1)}, bf16[2,2,512,512]{3,2,1,0:T(8,128)(2,1)S(1)}, f32[272,512]{1,0:T(8,128)S(1)}, bf16[400,512]{1,0:T(8,128)(2,1)S(1)}) custom-call(f32[2]{0:T(128)S(1)} %pad_maximum_fusion.flag_ref, f32[8,128]{1,0:T(8,128)S(1)} %squeeze.2.rate_ref, ...), custom_call_target="tpu_custom_call" | custom-call | tf_op jit(solution)/shard_map/totals/pallas_call | solution.py:504
  44.4 2.6 %collective-permute-start = (bf16[400,512]{1,0:T(8,128)(2,1)S(1)}, bf16[400,512]{1,0:T(8,128)(2,1)S(1)}, u32[]{:S(2)}, u32[]{:S(2)}) collective-permute-start(bf16[400,512]{1,0:T(8,128)(2,1)S(1)} %get-tuple-element.21), channel_id=1, source_target_pairs={{0,8},{8,0},{1,9},{9,1},{2,10},{10,2},{3,11},{11,3},{4,12},{12,4},... | collective-permute-start | bytes 1228808 | tf_op jit(solution)/shard_map/ppermute | solution.py:543
  47.1 11.5 %middle.1 = (f32[2,4,128,512]{3,2,1,0:T(8,128)S(1)}, f32[2,4,8,128]{3,2,1,0:T(8,128)S(1)}, f32[2,4,128,128]{3,2,1,0:T(8,128)S(1)}, f32[2,4,128,128]{3,2,1,0:T(8,128)S(1)}) custom-call(f32[8,128]{1,0:T(8,128)S(1)} %squeeze.2.rate_ref, bf16[2,4,1296,128]{3,2,1,0:T(8,128)(2,1)S(1)} %bitcast.7), custom_call_target="tpu_custom_call" | custom-call | flops 6000000000 | bytes 20000000 | tf_op jit(solution)/shard_map/middle/pallas_call | solution.py:515
  58.5 7.1 %collective-permute-done.refs_5_ = bf16[400,512]{1,0:T(8,128)(2,1)S(1)} collective-permute-done((bf16[400,512]{1,0:T(8,128)(2,1)S(1)}, bf16[400,512]{1,0:T(8,128)(2,1)S(1)}, u32[]{:S(2)}, u32[]{:S(2)}) %collective-permute-start) | collective-permute-done | bytes 409632 | tf_op jit(solution)/shard_map/ppermute | solution.py:543
  65.7 4.7 %finish.1 = bf16[2,4,784,128]{3,2,1,0:T(8,128)(2,1)S(1)} custom-call(f32[2]{0:T(128)S(1)} %pad_maximum_fusion.flag_ref, f32[8,128]{1,0:T(8,128)S(1)} %squeeze.2.rate_ref, bf16[2,4,1296,128]{3,2,1,0:T(8,128)(2,1)S(1)} %bitcast.8, f32[2,4,8,128]{3,2,1,0:T(8,128)S(1)} %get-tuple-element.17.refs_1_, bf16[2,2,512,512]{3,2,1,0:T(8,128)(2,1)S(1)} %get-tuple-element.18.refs_2_, ...), custom_call_target="tpu_custom_call" | custom-call | tf_op jit(solution)/shard_map/finish/pallas_call | solution.py:528
  70.4 23.7 %all_to_all.10.refs_0_ = bf16[8,784,128]{2,1,0:T(8,128)(2,1)S(1)} all-to-all(bf16[8,784,128]{2,1,0:T(8,128)(2,1)S(1)} %bitcast.9), channel_id=1, replica_groups=mesh['grp'=2,'hi'=2,'lo'=4,'ctx'=2] {'ctx','lo'}, dimensions={0} | all-to-all | bytes 3211264 | tf_op jit(solution)/shard_map/all_to_all | solution.py:455
  94.0 1.4 %unpack.1 = (bf16[128,4096]{1,0:T(8,128)(2,1)}, bf16[64,128]{1,0:T(8,128)(2,1)}, bf16[128,8,128]{2,1,0:T(8,128)(2,1)}, bf16[128,8,128]{2,1,0:T(8,128)(2,1)}) custom-call(bf16[8,784,128]{2,1,0:T(8,128)(2,1)S(1)} %all_to_all.10.refs_0_), custom_call_target="tpu_custom_call" | custom-call | tf_op jit(solution)/shard_map/unpack/pallas_call | solution.py:554
Async XLA Ops:
  4.1 5.4 %copy-start = (f32[64]{0:T(128)S(1)}, f32[64]{0:T(128)}, u32[]{:S(2)}) copy-start(f32[64]{0:T(128)} %param.9) | copy-start | bytes 772
  4.1 37.4 %all-to-all-start = ((bf16[8,1296,128]{2,1,0:T(8,128)(2,1)}), bf16[8,1296,128]{2,1,0:T(8,128)(2,1)S(1)}, u32[]{:S(2)}, u32[]{:S(2)}) async-start(bf16[8,1296,128]{2,1,0:T(8,128)(2,1)} %pack.1), calls=%async_computation | async-start | bytes 5308416 | tf_op jit(solution)/shard_map/all_to_all | solution.py:455
  44.4 21.2 %collective-permute-start = (bf16[400,512]{1,0:T(8,128)(2,1)S(1)}, bf16[400,512]{1,0:T(8,128)(2,1)S(1)}, u32[]{:S(2)}, u32[]{:S(2)}) collective-permute-start(bf16[400,512]{1,0:T(8,128)(2,1)S(1)} %get-tuple-element.21), channel_id=1, source_target_pairs={{0,8},{8,0},{1,9},{9,1},{2,10},{10,2},{3,11},{11,3},{4,12},{12,4},... | collective-permute-start | bytes 1228808 | tf_op jit(solution)/shard_map/ppermute | solution.py:543

commit v5 on v4

v5 whole, which is shorter than its diff:
```python
import functools
from typing import NamedTuple

import jax
import jax.numpy as jnp
from jax import lax
from jax.experimental import pallas as pl
from jax.experimental.pallas import tpu as pltpu
from jax.sharding import PartitionSpec as P

HEADS = 64
HEAD_DIM = 64
STATE = 128
GROUPS = 8
LANES = 128
ROWS = 8
TILE = 16
LOG2E = 1.4426950408889634
CODE_SPAN = 250.0
IN_FLIGHT = 5
F32 = jnp.float32
BF16 = jnp.bfloat16


def split2(value):
    hi = value.astype(BF16)
    return hi, (value - hi.astype(F32)).astype(BF16)


def split3(value):
    hi = value.astype(BF16)
    rest = value - hi.astype(F32)
    mid = rest.astype(BF16)
    return hi, mid, (rest - mid.astype(F32)).astype(BF16)


def dot(a, b):
    return lax.dot_general(a, b, (((1,), (0,)), ((), ())), preferred_element_type=F32)


def dot_nt(a, b):
    return lax.dot_general(a, b, (((1,), (1,)), ((), ())), preferred_element_type=F32)


def dot_tn(a, b):
    return lax.dot_general(a, b, (((0,), (0,)), ((), ())), preferred_element_type=F32)


def cat(parts, axis):
    return jnp.concatenate(parts, axis=axis)


def upper(size, strict):
    row = lax.broadcasted_iota(jnp.int32, (size, size), 0)
    col = lax.broadcasted_iota(jnp.int32, (size, size), 1)
    return row < col if strict else row <= col


def cumulate(rows, strict):
    tri = upper(rows.shape[1], strict).astype(F32).astype(BF16)
    sums = dot(cat([part.astype(F32) for part in split3(rows)], 0).astype(BF16), tri)
    size = rows.shape[0]
    return sums[:size] + sums[size : 2 * size] + sums[2 * size :]


def spread_matrix(terms, width):
    row = lax.broadcasted_iota(jnp.int32, (terms * ROWS, width), 0)
    col = lax.broadcasted_iota(jnp.int32, (terms * ROWS, width), 1)
    return (row % ROWS == col // HEAD_DIM).astype(F32).astype(BF16)


def spread_rows(rows, width):
    hi, lo = split2(rows)
    terms = cat([hi.astype(F32), lo.astype(F32)], 0).astype(BF16)
    return dot_tn(terms, spread_matrix(2, width))


def columns(rows):
    return jnp.transpose(cat([rows, jnp.zeros((LANES - rows.shape[0], rows.shape[1]), F32)], 0))


def widen(cols, first, width):
    lane = lax.broadcasted_iota(jnp.int32, cols.shape, 1)
    heads = [first + lane // HEAD_DIM + 2 * block for block in range(width // LANES)]
    return cat([jnp.take_along_axis(cols, head, axis=1) for head in heads], 1)


def head_products(values, factors):
    rows = values[0].shape[0]
    both = dot_nt(cat(list(values), 0), cat(list(factors), 0))
    size = factors[0].shape[0]
    return (both[:rows, :size] + (both[:rows, size:] + both[rows:, :size])) + both[rows:, size:]


class Place(NamedTuple):
    tokens: int
    half: int
    blocks: int

    @property
    def width(self):
        return self.blocks * LANES

    @property
    def b_row(self):
        return 2 * self.blocks * self.tokens

    @property
    def dt_row(self):
        return self.b_row + 2 * self.tokens

    @property
    def rows_in(self):
        return self.dt_row + TILE

    @property
    def rows_out(self):
        return (self.blocks + 2) * self.tokens + TILE

    def x(self, buf):
        return [buf[i * self.tokens : (i + 1) * self.tokens, :] for i in range(self.blocks)]

    def dy(self, buf):
        return [buf[i * self.tokens : (i + 1) * self.tokens, :] for i in range(self.blocks, 2 * self.blocks)]

    def b(self, buf):
        return buf[self.b_row : self.b_row + self.tokens, :]

    def c(self, buf):
        return buf[self.b_row + self.tokens : self.b_row + 2 * self.tokens, :]

    def dt(self, buf):
        return buf[self.dt_row : self.dt_row + TILE, :].astype(F32)[:ROWS]


def partner(place, k):
    return (lax.axis_index("ctx") ^ (k // place.half)) * place.half + (lax.axis_index("lo") ^ (k % place.half))


def pack_kernel(place, count, copies, *refs):
    (b_hbm, c_hbm, dt_hbm, x_hbm, dy_hbm), outs, refs = refs[:5], refs[5 : 5 + count], refs[5 + count :]
    b_ref, c_ref, dt_ref, b_wide, c_wide, dt_wide, x_ref, dy_ref, ready, sems, out_sems = refs
    tokens, blocks, width = place.tokens, place.blocks, place.width
    heads = HEADS // count
    dests = [partner(place, k) for k in range(count)]
    loads = [(b_hbm, b_ref), (c_hbm, c_ref), (dt_hbm, dt_ref)]
    for k, dest in enumerate(dests):
        columns = pl.ds(pl.multiple_of(dest * width, LANES), width)
        loads += [(x_hbm.at[:, columns], x_ref.at[k]), (dy_hbm.at[:, columns], dy_ref.at[k])]
    loads = [pltpu.make_async_copy(source, target, sems.at[i]) for i, (source, target) in enumerate(loads)]
    for load in loads:
        load.start()
    for load in loads[:3]:
        load.wait()
    every = tokens * GROUPS
    b_wide[:every] = b_ref[...].astype(F32).reshape(every, STATE)
    c_wide[:every] = c_ref[...].astype(F32).reshape(every, STATE)
    dt_wide[...] = dt_ref[...].astype(F32)
    stores = []
    for k, (dest, out) in enumerate(zip(dests, outs)):
        mine = pl.ds(lax.div(dest, copies), tokens, stride=GROUPS)
        ready[k, place.b_row : place.b_row + tokens] = b_wide[mine, :].astype(BF16)
        ready[k, place.b_row + tokens : place.dt_row] = c_wide[mine, :].astype(BF16)
        dt = dt_wide[pl.ds(dest * heads, heads), :]
        ready[k, place.dt_row :] = cat([dt, jnp.zeros((TILE - heads, tokens), F32)], 0).astype(BF16)
        for load in loads[3 + 2 * k : 5 + 2 * k]:
            load.wait()
        for part, ref in enumerate((x_ref, dy_ref)):
            for i in range(blocks):
                row = (part * blocks + i) * tokens
                ready[k, row : row + tokens] = ref[k, :, i * LANES : (i + 1) * LANES]
        stores.append(pltpu.make_async_copy(ready.at[k], out, out_sems.at[k]))
        stores[-1].start()
    for store in stores:
        store.wait()


def unpack_kernel(place, count, copies, *refs):
    homes, refs = refs[:count], refs[count:]
    dx_hbm, ddt_hbm, db_hbm, dc_hbm, dx_ref, db_ref, dc_ref, ddt_ref, db_wide, dc_wide, ddt_wide, sems = refs
    tokens, blocks, width = place.tokens, place.blocks, place.width
    heads = HEADS // count
    first = blocks * tokens
    moves = []

    def move(source, target):
        moves.append(pltpu.make_async_copy(source, target, sems.at[len(moves)]))
        moves[-1].start()

    if copies > 1:
        db_wide[...] = jnp.zeros_like(db_wide)
        dc_wide[...] = jnp.zeros_like(dc_wide)
    for k, home in enumerate(homes):
        source = partner(place, k)
        mine = pl.ds(lax.div(source, copies), tokens, stride=GROUPS)
        for to, at in ((db_wide, first), (dc_wide, first + tokens)):
            part = home[at : at + tokens, :].astype(F32)
            to[mine, :] = part if copies == 1 else to[mine, :] + part
        ddt_wide[pl.ds(source * heads, heads), :] = home[place.rows_out - TILE :, :].astype(F32)[:heads]
        for i in range(blocks):
            dx_ref[k, :, i * LANES : (i + 1) * LANES] = home[i * tokens : (i + 1) * tokens, :]
        move(dx_ref.at[k], dx_hbm.at[:, pl.ds(pl.multiple_of(source * width, LANES), width)])
    every = tokens * GROUPS
    db_ref[...] = db_wide[:every].reshape(db_ref.shape).astype(BF16)
    dc_ref[...] = dc_wide[:every].reshape(dc_ref.shape).astype(BF16)
    ddt_ref[...] = ddt_wide[...].astype(BF16)
    for source, target in ((db_ref, db_hbm), (dc_ref, dc_hbm), (ddt_ref, ddt_hbm)):
        move(source, target)
    for one in moves:
        one.wait()


def segment_decays(place, bufs, rate):
    dts = [place.dt(buf) for buf in bufs]
    cums = cumulate(cat([dt * rate for dt in dts], 0), False)
    cums = [cums[i * ROWS : (i + 1) * ROWS] for i in range(len(bufs))]
    starts, start = [], jnp.zeros((ROWS, 1), F32)
    for cum in cums:
        starts.append(start + cum)
        start = start + cum[:, place.tokens - 1 :]
    return dts, [start - one for one in starts], starts


def encode(value, scale):
    size = jnp.exp2(jnp.abs(value) * (CODE_SPAN / scale) - CODE_SPAN / 2)
    return jnp.where(value < 0.0, -size, size).astype(BF16)


def decode(code, scale):
    code = code.astype(F32)
    size = (jnp.log(jnp.abs(code)) * LOG2E + CODE_SPAN / 2) * (scale / CODE_SPAN)
    return jnp.where(code < 0.0, -size, size)


def totals_kernel(place, turn, rate_ref, *refs):
    blocks, refs = refs[: place.half], refs[place.half :]
    others, refs = ([], refs) if turn else (refs[:3], refs[3:])
    buf, u_rows, u_parts, v_parts, *refs = refs
    width, tokens = place.width, place.tokens
    for k, block in enumerate(blocks):
        lo = lax.axis_index("lo") ^ k
        for at in range(0, place.rows_in, tokens):
            rows = slice(at, min(at + tokens, place.rows_in))
            buf[lo, rows] = block[rows]
    chunks = [buf.at[i] for i in range(place.half)]
    dts, ends, starts = segment_decays(place, chunks, rate_ref[...])
    for i, chunk in enumerate(chunks):
        u_rows[i] = dts[i] * jnp.exp(ends[i])
        rows = slice(i * tokens, (i + 1) * tokens)
        hi, lo = split2(spread_rows(u_rows[i], width) * cat(place.x(chunk), 1).astype(F32))
        u_parts[0, rows], u_parts[1, rows] = hi, lo
        start_wide = spread_rows(jnp.exp(starts[i]), width)
        hi, lo = split2(start_wide * cat(place.dy(chunk), 1).astype(F32))
        v_parts[0, rows], v_parts[1, rows] = hi, lo
    b_turned = jnp.transpose(cat([place.b(chunk) for chunk in chunks], 0).astype(F32)).astype(BF16)
    c_turned = jnp.transpose(cat([place.c(chunk) for chunk in chunks], 0).astype(F32)).astype(BF16)
    total_s = dot(b_turned, u_parts[0]) + dot(b_turned, u_parts[1])
    total_g = dot(c_turned, v_parts[0]) + dot(c_turned, v_parts[1])
    log = jnp.broadcast_to(start_wide[tokens - 1 :, :], (ROWS, width))
    if turn:
        for ref, value in zip(refs, (total_s, total_g, log)):
            ref[...] = value
        return
    own_ref, send_ref = refs
    front, early = lax.axis_index("hi") == 0, lax.axis_index("ctx") == 0
    other_s, other_g, other_log = (ref[...] for ref in others)
    logs = [jnp.where(early, log, other_log), jnp.where(early, other_log, log)]
    middle = jnp.where(front, jnp.where(early, other_s, total_s), jnp.where(early, total_g, other_g))
    values = [jnp.where(early, total_s, other_s), middle, jnp.where(early, other_g, total_g)]
    tops = [jnp.maximum(jnp.max(jnp.abs(value), axis=0, keepdims=True), 1e-30) for value in values]
    scales = [(top * 1.01).astype(BF16).astype(F32) for top in tops]
    for i, (value, scale) in enumerate(zip(values, scales)):
        send_ref[i * STATE : (i + 1) * STATE] = encode(value, scale)
    notes = scales + [part.astype(F32) for log in logs for part in split2(log[:1])]
    send_ref[3 * STATE :] = cat(notes + [jnp.zeros((TILE - len(notes), width), F32)], 0).astype(BF16)
    own_ref[:STATE] = values[0]
    own_ref[STATE : 2 * STATE] = values[2]
    own_ref[2 * STATE :] = cat(logs, 0)


def head_sums(values, width):
    hi, lo = split2(values)
    picker = spread_matrix(2, width)
    return (dot_nt(picker, hi) + dot_nt(picker, lo))[:ROWS]


def fold(value):
    total = value[:ROWS]
    for i in range(1, value.shape[0] // ROWS):
        total = total + value[i * ROWS : (i + 1) * ROWS]
    return total


def middle_kernel(place, rate_ref, *refs):
    for turn in range(2):
        middle_segment(place, rate_ref[...], refs[turn], *refs[2 + 4 * turn : 6 + 4 * turn])


def middle_segment(place, rate, buf, dx_ref, ddt_ref, db_ref, dc_ref):
    tokens, width = place.tokens, place.width
    chunks = [buf.at[i] for i in range(place.half)]
    dts = [place.dt(chunk) for chunk in chunks]
    cums = cumulate(cat([dt * rate for dt in dts], 0), False)
    cums = [cums[i * ROWS : (i + 1) * ROWS] for i in range(len(chunks))]
    ends = [cum[:, tokens - 1 :] for cum in cums]
    starts = [jnp.exp(cum) for cum in cums]

    us, vs, end_wides, adds_s, adds_g, through = [], [], [], [], [], []
    for i, chunk in enumerate(chunks):
        cols = columns(cat([dts[i] * jnp.exp(ends[i] - cums[i]), starts[i]], 0))
        end_wide, start_wide = widen(cols, 0, width), widen(cols, ROWS, width)
        u, v = split2(end_wide * cat(place.x(chunk), 1).astype(F32)), split2(start_wide * cat(place.dy(chunk), 1).astype(F32))
        b_here, c_here = place.b(chunk), place.c(chunk)
        adds_s.append(dot_tn(cat([b_here, b_here], 0), cat(list(u), 0)))
        adds_g.append(dot_tn(cat([c_here, c_here], 0), cat(list(v), 0)))
        through.append(start_wide[tokens - 1 :, :])
        us.append(u)
        vs.append(v)
        end_wides.append(end_wide)
    states, grads = [jnp.zeros((STATE, width), F32)], [jnp.zeros((STATE, width), F32)]
    for i in range(len(chunks) - 1):
        states.append(through[i] * states[-1] + adds_s[i])
        grads.append(through[-1 - i] * grads[-1] + adds_g[-1 - i])
    grads = grads[::-1]
    corners = head_sums(cat([fold(through[i] * (states[i] * grads[i])) for i in range(len(chunks))], 0), width)

    mask = upper(tokens, False)
    left = lax.broadcasted_iota(jnp.int32, (tokens, LANES), 1) < HEAD_DIM
    left, right = left.astype(F32).astype(BF16), (~left).astype(F32).astype(BF16)
    for i, chunk in enumerate(chunks):
        b_here, c_here = place.b(chunk), place.c(chunk)
        cum = cums[i] * LOG2E
        cols = jnp.transpose(cum - jnp.log(jnp.where(dts[i] > 0.0, dts[i], 1.0)) * LOG2E)
        k_two = dot_nt(b_here, c_here)
        s_hi, s_lo = split2(states[i])
        g_hi, g_lo = split2(grads[i])
        b_grad = end_wides[i] * dot(cat([b_here, b_here], 1), cat([g_hi, g_lo], 0))
        c_state = dot(cat([c_here, c_here], 1), cat([s_hi, s_lo], 0))
        one_sum = jnp.zeros((tokens, tokens), F32)
        rows, alongs = [], []
        for block, (x_here, dy_here) in enumerate(zip(place.x(chunk), place.dy(chunk))):
            lanes = slice(block * LANES, (block + 1) * LANES)
            sides = cat([dy_here * left, dy_here * right], 0)
            k_one = dot_nt(x_here, sides)
            tops, bottoms = [], []
            for side in range(2):
                head = 2 * block + side
                gap = jnp.where(mask, cum[head : head + 1, :] - cols[:, head : head + 1], -1e30)
                decay = jnp.exp2(gap)
                a_one = decay * k_one[:, side * tokens : (side + 1) * tokens]
                a_two = decay * k_two
                one_sum = one_sum + a_one
                rows.append(jnp.sum(a_one * k_two, axis=0, keepdims=True))
                hi_two, lo_two = split2(a_two)
                tops.append(hi_two)
                bottoms.append(lo_two)
            both = dot(cat([cat(tops, 1), cat(bottoms, 1)], 0), sides)
            dx = both[:tokens] + both[tokens:] + b_grad[:, lanes]
            dx_ref[i, :, lanes] = dx
            alongs.append(dx * x_here.astype(F32))
        if len(rows) < ROWS:
            rows.append(jnp.zeros((ROWS - len(rows), tokens), F32))
        db = dot(cat(list(split2(one_sum)), 1), cat([c_here, c_here], 0))
        dc = dot(cat(list(split2(jnp.transpose(one_sum))), 1), cat([b_here, b_here], 0))
        db_ref[i] = db + head_products(us[i], (g_hi, g_lo))
        dc_ref[i] = dc + head_products(vs[i], (s_hi, s_lo))
        sums = head_sums(cat([cat(alongs, 1), cat(place.dy(chunk), 1).astype(F32) * c_state], 0), width)
        along = sums[:, :tokens]
        later = starts[i] * sums[:, tokens:]
        corner = jnp.sum(corners[:, i * ROWS : (i + 1) * ROWS], axis=1, keepdims=True)
        flow = along - cat(rows, 0) - later
        dlog = corner + jnp.sum(later, axis=1, keepdims=True) + cumulate(flow, True)
        ddt_ref[i] = along / jnp.where(dts[i] > 0.0, dts[i], 1.0) + rate * dlog


def carried_in(own, got, seg, front):
    notes = got[3 * STATE :].astype(F32)
    sent0, sent2, logs = own[:STATE], own[STATE : 2 * STATE], (own[2 * STATE : 2 * STATE + 1], own[2 * STATE + ROWS : 2 * STATE + ROWS + 1])
    got0, got1, got2 = (decode(got[i * STATE : (i + 1) * STATE], notes[i : i + 1]) for i in range(3))
    mine = jnp.where(front, logs[1], logs[0])
    other = jnp.where(front, notes[3:4] + notes[4:5], notes[5:6] + notes[6:7])
    far = got1 + other * (jnp.where(front, sent2, sent0) + mine * jnp.where(front, got2, got0))
    near = jnp.where(front, got0, got2) + other * jnp.where(front, sent0, sent2)
    none = jnp.zeros_like(far)
    states = [jnp.where(front, none, got0), jnp.where(front, near, far)]
    grads = [jnp.where(front, far, near), jnp.where(front, got2, none)]
    return [[jnp.where(here == 0, pair[0], pair[1]) for pair in (states, grads, logs)] for here in (seg, 1 - seg)]


def finish_kernel(place, turn, rate_ref, buf, u_rows, u_parts, v_parts, dx_in, ddt_in, db_in, dc_in, *refs):
    rate, tokens, width = rate_ref[...], place.tokens, place.width
    if turn == 0:
        (own, got), *refs = refs[:2], *refs[2:]
        (state, grad, through), rest = carried_in(own, got, lax.axis_index("ctx"), lax.axis_index("hi") == 0)
        for ref, value in zip(refs, rest):
            ref[...] = jnp.broadcast_to(value, ref.shape)
    else:
        state, grad, through = (ref[...] for ref in refs[:3])
        through = through[:1]
    *outs, out = refs[3:]
    s_hi, s_lo = split2(state)
    g_hi, g_lo = split2(grad)
    corner = jnp.sum(head_sums(fold(through * (grad * state)), width), axis=1, keepdims=True)
    chunks = [buf.at[i] for i in range(place.half)]
    b_all, c_all = cat([place.b(chunk) for chunk in chunks], 0), cat([place.c(chunk) for chunk in chunks], 0)
    b_grad = dot(cat([b_all, b_all], 1), cat([g_hi, g_lo], 0))
    c_state = dot(cat([c_all, c_all], 1), cat([s_hi, s_lo], 0))
    v_hi, v_lo = v_parts[0], v_parts[1]
    db = head_products((u_parts[0], u_parts[1]), (g_hi, g_lo))
    dc = head_products((v_hi, v_lo), (s_hi, s_lo))
    ins = []
    for i, chunk in enumerate(chunks):
        rows = slice(i * tokens, (i + 1) * tokens)
        extra = widen(columns(u_rows[i]), 0, width) * b_grad[rows]
        dx = (dx_in[i] + extra).astype(BF16)
        for block in range(place.blocks):
            out[i, block * tokens : (block + 1) * tokens, :] = dx[:, block * LANES : (block + 1) * LANES]
        ins.append(extra * cat(place.x(chunk), 1).astype(F32))
        first = place.blocks * tokens
        out[i, first : first + tokens, :] = (db_in[i] + db[rows]).astype(BF16)
        out[i, first + tokens : first + 2 * tokens, :] = (dc_in[i] + dc[rows]).astype(BF16)
    ins = head_sums(cat(ins, 0), width)
    laters = head_sums((v_hi.astype(F32) + v_lo.astype(F32)) * c_state, width)
    ins, laters = ([sums[:, i * tokens : (i + 1) * tokens] for i in range(place.half)] for sums in (ins, laters))
    over = cumulate(cat([one - other for one, other in zip(ins, laters)], 0), True)
    rest = corner
    for later in laters:
        rest = rest + jnp.sum(later, axis=1, keepdims=True)
    for i, chunk in enumerate(chunks):
        dlog = rest + over[i * ROWS : (i + 1) * ROWS]
        rest = rest + jnp.sum(ins[i] - laters[i], axis=1, keepdims=True)
        dt = place.dt(chunk)
        ddt = ddt_in[i] + ins[i] / jnp.where(dt > 0.0, dt, 1.0) + rate * dlog
        out[i, place.rows_out - TILE :, :] = cat([ddt, jnp.zeros_like(ddt)], 0).astype(BF16)
    for k, target in enumerate(outs):
        lo = lax.axis_index("lo") ^ k
        for at in range(0, place.rows_out, tokens):
            part = slice(at, min(at + tokens, place.rows_out))
            target[part] = out[lo, part]


def on_device(x_seq, dy_seq, dt_seq, a_log, b_seq, c_seq):
    tokens = x_seq.shape[0]
    half = lax.axis_size("lo")
    count = 2 * half
    heads = HEADS // count
    copies = count // GROUPS
    place = Place(tokens, half, heads * HEAD_DIM // LANES)
    width = place.width

    def after(value, *others):
        return lax.optimization_barrier((value, *others))[0]

    def swap(blocks, order):
        got, under_way = {0: blocks[0]}, []
        for k in order:
            turn = (k % half) * 2 + k // half
            block = blocks[k]
            if len(under_way) >= IN_FLIGHT:
                block = after(block, under_way[-IN_FLIGHT])
            got[k] = lax.ppermute(block, ("lo", "ctx"), [(i, i ^ turn) for i in range(count)])
            under_way.append(got[k])
        return [got[k] for k in range(count)]

    rates = -jnp.exp(lax.dynamic_slice_in_dim(a_log, lax.axis_index(("ctx", "lo")) * heads, heads))
    rate = jnp.broadcast_to(jnp.pad(rates, (0, ROWS - heads))[:, None], (ROWS, LANES))

    def f32(*shape):
        return jax.ShapeDtypeStruct(shape, F32)

    def bf16(*shape):
        return jax.ShapeDtypeStruct(shape, BF16)

    hbm, vmem = pl.BlockSpec(memory_space=pltpu.HBM), pl.BlockSpec(memory_space=pltpu.VMEM)
    params = pltpu.CompilerParams(vmem_limit_bytes=24 * 1024 * 1024)
    spaced = pltpu.VMEM((tokens * GROUPS + GROUPS, STATE), F32)
    wides = [spaced, spaced, pltpu.VMEM((HEADS, tokens), F32)]
    seqs = (b_seq, c_seq, dt_seq.T, x_seq, dy_seq)
    by_partner = [pltpu.VMEM((count, tokens, width), BF16)]

    sent = pl.pallas_call(
        functools.partial(pack_kernel, place, count, copies),
        in_specs=[hbm] * 5,
        out_specs=[hbm] * count,
        out_shape=[bf16(place.rows_in, LANES)] * count,
        scratch_shapes=[pltpu.VMEM(seq.shape, BF16) for seq in seqs[:3]]
        + wides
        + by_partner * 2
        + [pltpu.VMEM((count, place.rows_in, LANES), BF16), pltpu.SemaphoreType.DMA((3 + 2 * count,)), pltpu.SemaphoreType.DMA((count,))],
        compiler_params=pltpu.CompilerParams(vmem_limit_bytes=58 * 1024 * 1024),
        name="pack",
    )(*seqs)
    arrived = swap(sent, [*range(half, count), *range(1, half)])

    owned, coded = (2 * STATE + 2 * ROWS, width), (3 * STATE + TILE, width)
    data_shapes = [bf16(half, place.rows_in, LANES), f32(half, ROWS, tokens)] + [bf16(2, half * tokens, width)] * 2
    carry_shapes = [f32(STATE, width), f32(STATE, width), f32(ROWS, width)]

    def totals(turn, blocks, others, shapes):
        return pl.pallas_call(
            functools.partial(totals_kernel, place, turn),
            in_specs=[vmem] * (1 + half + len(others)),
            out_specs=[vmem] * (4 + len(shapes)),
            out_shape=data_shapes + shapes,
            compiler_params=params,
            name="totals",
        )(rate, *blocks, *others)

    *data1, other_s, other_g, other_log = totals(1, arrived[half:], [], carry_shapes)
    *data0, own, send = totals(0, arrived[:half], [other_s, other_g, other_log], [f32(*owned), bf16(*coded)])
    got = lax.ppermute(send, "hi", [(0, 1), (1, 0)])

    within = [f32(half, tokens, width), f32(half, ROWS, tokens), f32(half, tokens, STATE), f32(half, tokens, STATE)]
    parts = pl.pallas_call(
        functools.partial(middle_kernel, place),
        in_specs=[vmem] * 3,
        out_specs=[vmem] * 8,
        out_shape=within * 2,
        compiler_params=params,
        cost_estimate=pl.CostEstimate(flops=6_000_000_000, bytes_accessed=20_000_000, transcendentals=2_000_000),
        name="middle",
    )(rate, data0[0], data1[0])

    def finish(turn, data, parts, others, shapes):
        return pl.pallas_call(
            functools.partial(finish_kernel, place, turn),
            in_specs=[vmem] * (9 + len(others)),
            out_specs=[vmem] * (half + len(shapes)),
            out_shape=shapes + [bf16(place.rows_out, LANES)] * half,
            scratch_shapes=[pltpu.VMEM((half, place.rows_out, LANES), BF16)],
            compiler_params=params,
            name="finish",
        )(rate, *data, *parts, *others)

    state, grad, through, *outs0 = finish(0, data0, parts[:4], [own, got], carry_shapes)
    outs1 = finish(1, data1, parts[4:], [state, grad, through], [])
    homes = swap([*outs0, *outs1], range(1, count))

    dx, ddt, db, dc = pl.pallas_call(
        functools.partial(unpack_kernel, place, count, copies),
        in_specs=[vmem] * count,
        out_specs=[hbm] * 4,
        out_shape=[bf16(*x_seq.shape), bf16(HEADS, tokens), bf16(*b_seq.shape), bf16(*c_seq.shape)],
        scratch_shapes=by_partner
        + [pltpu.VMEM(b_seq.shape, BF16), pltpu.VMEM(c_seq.shape, BF16), pltpu.VMEM((HEADS, tokens), BF16)]
        + wides
        + [pltpu.SemaphoreType.DMA((count + 3,))],
        compiler_params=params,
        name="unpack",
    )(*homes)
    return dx, ddt.T, db, dc


def solution(mesh):
    parts, head, ctx = (mesh.shape[name] for name in ("grp", "head", "ctx"))
    split = jax.sharding.Mesh(mesh.devices.reshape(parts, 2, head // 2, ctx), ("grp", "hi", "lo", "ctx"))
    spec = P(("grp", "ctx", "hi", "lo"))
    return jax.shard_map(
        on_device,
        mesh=split,
        in_specs=(spec, spec, spec, P(), spec, spec),
        out_specs=(spec, spec, spec, spec),
        check_vma=False,
    )
```

time: 95.9 us -> 86.2 us (0.90)
  blocking collectives: 23.7 us -> 0 us
  starting transfers between devices: 7.92 us -> 17.6 us
  waiting for transfers between devices: 39.1 us -> 43.4 us
    ppermute x1 -> x15, waiting for transfers between devices: 7.12 us -> 43.4 us  [the longest x14 36.8 us: swap(): lax.ppermute(block, ('lo', 'ctx'), [(i, i ^ turn) for i in range(count)])]
    all_to_all x1 -> x0, waiting for transfers between devices: 31.9 us -> none  [swap(): lax.all_to_all(value, ('ctx', 'lo'), split_axis=0, concat_axis=0, tiled=T...]
    all_to_all x1 -> x0, blocking collectives: 23.7 us -> none  [swap(): lax.all_to_all(value, ('ctx', 'lo'), split_axis=0, concat_axis=0, tiled=T...]
    ppermute x1 -> x15, starting transfers between devices: 2.65 us -> 17.6 us  [the longest x14 14.9 us: swap(): lax.ppermute(block, ('lo', 'ctx'), [(i, i ^ turn) for i in range(count)])]
    all_to_all x1 -> x0, starting transfers between devices: 5.27 us -> none  [swap(): lax.all_to_all(value, ('ctx', 'lo'), split_axis=0, concat_axis=0, tiled=T...]
    pallas_call x5 -> x7, Pallas kernels: 23.9 us -> 23.4 us  [the longest x1 11.8 us: on_device(): pl.pallas_call(functools.partial(middle_kernel, place), in_specs=[vmem] *...]
  transfers between devices with their start and end apart: 2 -> 15, of which waited for: 2 -> 11; matrix products, arithmetic and copies ran while one was open for 0% -> 0% of each run, Pallas kernels for 12% -> 18%
where the time goes in v5:
time: 86.2 us; the launch traced here: 85.4 us
  waiting for transfers between devices  43.4 us (50%)
  Pallas kernels  23.4 us (27%)
  starting transfers between devices  17.6 us (20%)
  between operations  0.87 us (1%)
    ppermute x14, waiting for transfers between devices, swap(): lax.ppermute(block, ('lo', 'ctx'), [(i, i ^ turn) for i in range(count)])  36.8 us
    ppermute x14, starting transfers between devices, swap(): lax.ppermute(block, ('lo', 'ctx'), [(i, i ^ turn) for i in range(count)])  14.9 us
    pallas_call x1, Pallas kernels, on_device(): pl.pallas_call(functools.partial(middle_kernel, place), in_specs=[vmem] *...  11.8 us
    ppermute x1, waiting for transfers between devices, on_device(): got = lax.ppermute(send, 'hi', [(0, 1), (1, 0)])  6.61 us
    pallas_call x2, Pallas kernels, finish(): pl.pallas_call(functools.partial(finish_kernel, place, turn), in_specs=[v...  4.47 us
    pallas_call x1, Pallas kernels, on_device(): pl.pallas_call(functools.partial(pack_kernel, place, count, copies), in_s...  2.9 us
    pallas_call x2, Pallas kernels, totals(): pl.pallas_call(functools.partial(totals_kernel, place, turn), in_specs=[v...  2.76 us
    ppermute x1, starting transfers between devices, on_device(): got = lax.ppermute(send, 'hi', [(0, 1), (1, 0)])  2.65 us
  transfers between devices with their start and end apart: 15, of which 11 were waited for; matrix products, arithmetic and copies ran while one was open for 0% of the time, Pallas kernels for 18%

profile of v5, /device:TPU:0, one launch (start us, length us, event | category | flops | bytes accessed | tf_op | source)
XLA Modules:
  0.0 85.4 jit_solution(11507952993802348163)
XLA Ops:
  0.6 2.9 %pack.1 = (bf16[1296,128]{1,0:T(8,128)(2,1)}, bf16[1296,128]{1,0:T(8,128)(2,1)}, bf16[1296,128]{1,0:T(8,128)(2,1)}, bf16[1296,128]{1,0:T(8,128)(2,1)}, bf16[1296...) custom-call(bf16[128,8,128]{2,1,0:T(8,128)(2,1)} %refs_0_.1, ...), custom_call_target="tpu_custom_call" | custom-call | tf_op jit(solution)/shard_map/pack/pallas_call | solution.py:481
  3.6 0.5 collective-permute-start.1
  4.1 2.6 %collective-permute-start.3 = (bf16[1296,128]{1,0:T(8,128)(2,1)}, bf16[1296,128]{1,0:T(8,128)(2,1)S(1)}, u32[]{:S(2)}, u32[]{:S(2)}) collective-permute-start(bf16[1296,128]{1,0:T(8,128)(2,1)} %get-tuple-element.58), channel_id=1, source_target_pairs={{0,3},{1,2},{2,1},{3,0},{4,7},{5,6},{6,5},{7,4},{8,11},{9,10},{10,... | collective-permute-start | bytes 995336 | tf_op jit(solution)/shard_map/ppermute | solution.py:461
  6.8 1.4 %collective-permute-start.5 = (bf16[1296,128]{1,0:T(8,128)(2,1)}, bf16[1296,128]{1,0:T(8,128)(2,1)S(1)}, u32[]{:S(2)}, u32[]{:S(2)}) collective-permute-start(bf16[1296,128]{1,0:T(8,128)(2,1)} %get-tuple-element.60), channel_id=1, source_target_pairs={{0,5},{1,4},{2,7},{3,6},{4,1},{5,0},{6,3},{7,2},{8,13},{9,12},{10,... | collective-permute-start | bytes 995336 | tf_op jit(solution)/shard_map/ppermute | solution.py:461
  8.2 1.7 %collective-permute-start.6 = (bf16[1296,128]{1,0:T(8,128)(2,1)}, bf16[1296,128]{1,0:T(8,128)(2,1)S(1)}, u32[]{:S(2)}, u32[]{:S(2)}) collective-permute-start(bf16[1296,128]{1,0:T(8,128)(2,1)} %get-tuple-element.61), channel_id=1, source_target_pairs={{0,7},{1,6},{2,5},{3,4},{4,3},{5,2},{6,1},{7,0},{8,15},{9,14},{10,... | collective-permute-start | bytes 995336 | tf_op jit(solution)/shard_map/ppermute | solution.py:461
  9.9 1.6 %collective-permute-start.2 = (bf16[1296,128]{1,0:T(8,128)(2,1)}, bf16[1296,128]{1,0:T(8,128)(2,1)S(1)}, u32[]{:S(2)}, u32[]{:S(2)}) collective-permute-start(bf16[1296,128]{1,0:T(8,128)(2,1)} %get-tuple-element.56), channel_id=1, source_target_pairs={{0,4},{1,5},{2,6},{3,7},{4,0},{5,1},{6,2},{7,3},{8,12},{9,13},{10,... | collective-permute-start | bytes 995336 | tf_op jit(solution)/shard_map/ppermute | solution.py:461
  11.5 3.7 %collective-permute-done.3.refs_1_ = bf16[1296,128]{1,0:T(8,128)(2,1)S(1)} collective-permute-done((bf16[1296,128]{1,0:T(8,128)(2,1)}, bf16[1296,128]{1,0:T(8,128)(2,1)S(1)}, u32[]{:S(2)}, u32[]{:S(2)}) %collective-permute-start.3) | collective-permute-done | bytes 331808 | tf_op jit(solution)/shard_map/ppermute | solution.py:461
  15.2 2.2 %collective-permute-start.4 = (bf16[1296,128]{1,0:T(8,128)(2,1)}, bf16[1296,128]{1,0:T(8,128)(2,1)S(1)}, u32[]{:S(2)}, u32[]{:S(2)}) collective-permute-start(bf16[1296,128]{1,0:T(8,128)(2,1)} %get-tuple-element.59), channel_id=1, source_target_pairs={{0,6},{1,7},{2,4},{3,5},{4,2},{5,3},{6,0},{7,1},{8,14},{9,15},{10,... | collective-permute-start | bytes 995336 | tf_op jit(solution)/shard_map/ppermute | solution.py:461
  17.4 0.1 exponential_negate_fusion
  17.5 8.1 %collective-permute-done.6.refs_3_ = bf16[1296,128]{1,0:T(8,128)(2,1)S(1)} collective-permute-done((bf16[1296,128]{1,0:T(8,128)(2,1)}, bf16[1296,128]{1,0:T(8,128)(2,1)S(1)}, u32[]{:S(2)}, u32[]{:S(2)}) %collective-permute-start.6) | collective-permute-done | bytes 331808 | tf_op jit(solution)/shard_map/ppermute | solution.py:461
  25.7 1.3 %totals.2 = (bf16[4,1296,128]{2,1,0:T(8,128)(2,1)S(1)}, f32[4,8,128]{2,1,0:T(8,128)S(1)}, bf16[2,512,512]{2,1,0:T(8,128)(2,1)S(1)}, bf16[2,512,512]{2,1,0:T(8,12...) custom-call(f32[8,128]{1,0:T(8,128)S(1)} %broadcast_in_dim.2.rate_ref, ...), custom_call_target="tpu_custom_call" | custom-call | tf_op jit(solution)/shard_map/totals/pallas_call | solution.py:500
  26.9 2.6 %collective-permute-done.refs_1_ = bf16[1296,128]{1,0:T(8,128)(2,1)S(1)} collective-permute-done((bf16[1296,128]{1,0:T(8,128)(2,1)}, bf16[1296,128]{1,0:T(8,128)(2,1)S(1)}, u32[]{:S(2)}, u32[]{:S(2)}) %collective-permute-start) | collective-permute-done | bytes 331808 | tf_op jit(solution)/shard_map/ppermute | solution.py:461
  29.5 2.4 %collective-permute-done.2.refs_2_ = bf16[1296,128]{1,0:T(8,128)(2,1)S(1)} collective-permute-done((bf16[1296,128]{1,0:T(8,128)(2,1)}, bf16[1296,128]{1,0:T(8,128)(2,1)S(1)}, u32[]{:S(2)}, u32[]{:S(2)}) %collective-permute-start.2) | collective-permute-done | bytes 331808 | tf_op jit(solution)/shard_map/ppermute | solution.py:461
  31.9 8.0 %collective-permute-done.4.refs_3_ = bf16[1296,128]{1,0:T(8,128)(2,1)S(1)} collective-permute-done((bf16[1296,128]{1,0:T(8,128)(2,1)}, bf16[1296,128]{1,0:T(8,128)(2,1)S(1)}, u32[]{:S(2)}, u32[]{:S(2)}) %collective-permute-start.4) | collective-permute-done | bytes 331808 | tf_op jit(solution)/shard_map/ppermute | solution.py:461
  39.9 1.5 %totals.3 = (bf16[4,1296,128]{2,1,0:T(8,128)(2,1)S(1)}, f32[4,8,128]{2,1,0:T(8,128)S(1)}, bf16[2,512,512]{2,1,0:T(8,128)(2,1)S(1)}, bf16[2,512,512]{2,1,0:T(8,12...) custom-call(f32[8,128]{1,0:T(8,128)S(1)} %broadcast_in_dim.2.rate_ref, bf16[1296,128]{1,0:T(8,128)(2,1)S(1)} %copy-done, ...), custom_call_target="tpu_custom_call" | custom-call | tf_op jit(solution)/shard_map/totals/pallas_call | solution.py:500
  41.4 2.7 %collective-permute-start.7 = (bf16[400,512]{1,0:T(8,128)(2,1)S(1)}, bf16[400,512]{1,0:T(8,128)(2,1)S(1)}, u32[]{:S(2)}, u32[]{:S(2)}) collective-permute-start(bf16[400,512]{1,0:T(8,128)(2,1)S(1)} %get-tuple-element.75), channel_id=1, source_target_pairs={{0,8},{8,0},{1,9},{9,1},{2,10},{10,2},{3,11},{11,3},{4,12},{12,4},... | collective-permute-start | bytes 1228808 | tf_op jit(solution)/shard_map/ppermute | solution.py:511
  44.0 11.8 %middle.1 = (f32[4,128,512]{2,1,0:T(8,128)S(1)}, f32[4,8,128]{2,1,0:T(8,128)S(1)}, f32[4,128,128]{2,1,0:T(8,128)S(1)}, f32[4,128,128]{2,1,0:T(8,128)S(1)}, f32[4...) custom-call(f32[8,128]{1,0:T(8,128)S(1)} %broadcast_in_dim.2.rate_ref, ...), custom_call_target="tpu_custom_call" | custom-call | flops 6000000000 | bytes 20000000 | tf_op jit(solution)/shard_map/middle/pallas_call | solution.py:514
  55.9 6.6 %collective-permute-done.7.refs_1_ = bf16[400,512]{1,0:T(8,128)(2,1)S(1)} collective-permute-done((bf16[400,512]{1,0:T(8,128)(2,1)S(1)}, bf16[400,512]{1,0:T(8,128)(2,1)S(1)}, u32[]{:S(2)}, u32[]{:S(2)}) %collective-permute-start.7) | collective-permute-done | bytes 409632 | tf_op jit(solution)/shard_map/ppermute | solution.py:511
  62.5 2.4 %finish.2 = (f32[128,512]{1,0:T(8,128)S(1)}, f32[128,512]{1,0:T(8,128)S(1)}, f32[8,512]{1,0:T(8,128)S(1)}, bf16[784,128]{1,0:T(8,128)(2,1)S(1)}, bf16[784,128]{1...) custom-call(f32[8,128]{1,0:T(8,128)S(1)} %broadcast_in_dim.2.rate_ref, ...), custom_call_target="tpu_custom_call" | custom-call | tf_op jit(solution)/shard_map/finish/pallas_call | solution.py:525
  64.9 0.5 collective-permute-start.8
  65.4 0.8 collective-permute-start.9
  66.2 2.3 %collective-permute-start.10 = (bf16[784,128]{1,0:T(8,128)(2,1)S(1)}, bf16[784,128]{1,0:T(8,128)(2,1)S(1)}, u32[]{:S(2)}, u32[]{:S(2)}) collective-permute-start(bf16[784,128]{1,0:T(8,128)(2,1)S(1)} %get-tuple-element.79), channel_id=1, source_target_pairs={{0,6},{1,7},{2,4},{3,5},{4,2},{5,3},{6,0},{7,1},{8,14},{9,15},{10,... | collective-permute-start | bytes 602120 | tf_op jit(solution)/shard_map/ppermute | solution.py:461
  68.5 2.0 %finish.3 = (bf16[784,128]{1,0:T(8,128)(2,1)S(1)}, bf16[784,128]{1,0:T(8,128)(2,1)S(1)}, bf16[784,128]{1,0:T(8,128)(2,1)S(1)}, bf16[784,128]{1,0:T(8,128)(2,1)S(1)}) custom-call(f32[8,128]{1,0:T(8,128)S(1)} %broadcast_in_dim.2.rate_ref, bf16[4,1296,128]{2,1,0:T(8,128)(2,1)S(1)} %get-tuple-element.69.refs_1_.buf, f32[4,8,128]{2,1,0:T(8,128)S(1)} %get-tuple-element.80.u_rows, ...), custom_call_target="tpu_custom_call" | custom-call | tf_op jit(solution)/shard_map/finish/pallas_call | solution.py:525
  70.5 0.1 collective-permute-start.11
  70.6 0.6 collective-permute-start.12
  71.2 0.8 collective-permute-done.8.refs_1_
  72.0 1.4 %collective-permute-done.9.refs_2_ = bf16[784,128]{1,0:T(8,128)(2,1)S(1)} collective-permute-done((bf16[784,128]{1,0:T(8,128)(2,1)S(1)}, bf16[784,128]{1,0:T(8,128)(2,1)S(1)}, u32[]{:S(2)}, u32[]{:S(2)}) %collective-permute-start.9) | collective-permute-done | bytes 200736 | tf_op jit(solution)/shard_map/ppermute | solution.py:461
  73.4 0.6 collective-permute-start.14
  73.9 3.8 %collective-permute-done.10.refs_3_ = bf16[784,128]{1,0:T(8,128)(2,1)S(1)} collective-permute-done((bf16[784,128]{1,0:T(8,128)(2,1)S(1)}, bf16[784,128]{1,0:T(8,128)(2,1)S(1)}, u32[]{:S(2)}, u32[]{:S(2)}) %collective-permute-start.10) | collective-permute-done | bytes 200736 | tf_op jit(solution)/shard_map/ppermute | solution.py:461
  77.8 2.9 %collective-permute-done.12.refs_5_ = bf16[784,128]{1,0:T(8,128)(2,1)S(1)} collective-permute-done((bf16[784,128]{1,0:T(8,128)(2,1)S(1)}, bf16[784,128]{1,0:T(8,128)(2,1)S(1)}, u32[]{:S(2)}, u32[]{:S(2)}) %collective-permute-start.12) | collective-permute-done | bytes 200736 | tf_op jit(solution)/shard_map/ppermute | solution.py:461
  80.7 3.1 %collective-permute-done.14.refs_7_ = bf16[784,128]{1,0:T(8,128)(2,1)S(1)} collective-permute-done((bf16[784,128]{1,0:T(8,128)(2,1)S(1)}, bf16[784,128]{1,0:T(8,128)(2,1)S(1)}, u32[]{:S(2)}, u32[]{:S(2)}) %collective-permute-start.14) | collective-permute-done | bytes 200736 | tf_op jit(solution)/shard_map/ppermute | solution.py:461
  83.8 1.4 %unpack.1 = (bf16[128,4096]{1,0:T(8,128)(2,1)}, bf16[64,128]{1,0:T(8,128)(2,1)}, bf16[128,8,128]{2,1,0:T(8,128)(2,1)}, bf16[128,8,128]{2,1,0:T(8,128)(2,1)}) custom-call(bf16[784,128]{1,0:T(8,128)(2,1)S(1)} %get-tuple-element.76.refs_0_, bf16[784,128]{1,0:T(8,128)(2,1)S(1)} %collective-permute-done.8.refs_1_, ...), custom_call_target="tpu_custom_call" | custom-call | tf_op jit(solution)/shard_map/unpack/pallas_call | solution.py:539
  (11 shorter events, 0.1 us)
Async XLA Ops:
  0.6 16.8 %copy-start.1 = (f32[64]{0:T(128)S(1)}, f32[64]{0:T(128)}, u32[]{:S(2)}) copy-start(f32[64]{0:T(128)} %param.9) | copy-start | bytes 772
  3.5 36.3 %copy-start = (bf16[1296,128]{1,0:T(8,128)(2,1)S(1)}, bf16[1296,128]{1,0:T(8,128)(2,1)}, u32[]{:S(2)}) copy-start(bf16[1296,128]{1,0:T(8,128)(2,1)} %get-tuple-element.52.refs_0_) | copy-start | bytes 995332
  3.6 6.4 %collective-permute-start.1 = (bf16[1296,128]{1,0:T(8,128)(2,1)}, bf16[1296,128]{1,0:T(8,128)(2,1)S(1)}, u32[]{:S(2)}, u32[]{:S(2)}) collective-permute-start(bf16[1296,128]{1,0:T(8,128)(2,1)} %get-tuple-element.55), channel_id=1, source_target_pairs={{0,1},{1,0},{2,3},{3,2},{4,5},{5,4},{6,7},{7,6},{8,9},{9,8},{10,11... | collective-permute-start | bytes 995336 | tf_op jit(solution)/shard_map/ppermute | solution.py:461
  4.1 11.1 %collective-permute-start.3 = (bf16[1296,128]{1,0:T(8,128)(2,1)}, bf16[1296,128]{1,0:T(8,128)(2,1)S(1)}, u32[]{:S(2)}, u32[]{:S(2)}) collective-permute-start(bf16[1296,128]{1,0:T(8,128)(2,1)} %get-tuple-element.58), channel_id=1, source_target_pairs={{0,3},{1,2},{2,1},{3,0},{4,7},{5,6},{6,5},{7,4},{8,11},{9,10},{10,... | collective-permute-start | bytes 995336 | tf_op jit(solution)/shard_map/ppermute | solution.py:461
  6.7 22.8 %collective-permute-start = (bf16[1296,128]{1,0:T(8,128)(2,1)}, bf16[1296,128]{1,0:T(8,128)(2,1)S(1)}, u32[]{:S(2)}, u32[]{:S(2)}) collective-permute-start(bf16[1296,128]{1,0:T(8,128)(2,1)} %get-tuple-element.53), channel_id=1, source_target_pairs={{0,2},{1,3},{2,0},{3,1},{4,6},{5,7},{6,4},{7,5},{8,10},{9,11},{10,... | collective-permute-start | bytes 995336 | tf_op jit(solution)/shard_map/ppermute | solution.py:461
  6.8 10.7 %collective-permute-start.5 = (bf16[1296,128]{1,0:T(8,128)(2,1)}, bf16[1296,128]{1,0:T(8,128)(2,1)S(1)}, u32[]{:S(2)}, u32[]{:S(2)}) collective-permute-start(bf16[1296,128]{1,0:T(8,128)(2,1)} %get-tuple-element.60), channel_id=1, source_target_pairs={{0,5},{1,4},{2,7},{3,6},{4,1},{5,0},{6,3},{7,2},{8,13},{9,12},{10,... | collective-permute-start | bytes 995336 | tf_op jit(solution)/shard_map/ppermute | solution.py:461
  8.2 17.4 %collective-permute-start.6 = (bf16[1296,128]{1,0:T(8,128)(2,1)}, bf16[1296,128]{1,0:T(8,128)(2,1)S(1)}, u32[]{:S(2)}, u32[]{:S(2)}) collective-permute-start(bf16[1296,128]{1,0:T(8,128)(2,1)} %get-tuple-element.61), channel_id=1, source_target_pairs={{0,7},{1,6},{2,5},{3,4},{4,3},{5,2},{6,1},{7,0},{8,15},{9,14},{10,... | collective-permute-start | bytes 995336 | tf_op jit(solution)/shard_map/ppermute | solution.py:461
  9.9 21.9 %collective-permute-start.2 = (bf16[1296,128]{1,0:T(8,128)(2,1)}, bf16[1296,128]{1,0:T(8,128)(2,1)S(1)}, u32[]{:S(2)}, u32[]{:S(2)}) collective-permute-start(bf16[1296,128]{1,0:T(8,128)(2,1)} %get-tuple-element.56), channel_id=1, source_target_pairs={{0,4},{1,5},{2,6},{3,7},{4,0},{5,1},{6,2},{7,3},{8,12},{9,13},{10,... | collective-permute-start | bytes 995336 | tf_op jit(solution)/shard_map/ppermute | solution.py:461
  15.2 24.7 %collective-permute-start.4 = (bf16[1296,128]{1,0:T(8,128)(2,1)}, bf16[1296,128]{1,0:T(8,128)(2,1)S(1)}, u32[]{:S(2)}, u32[]{:S(2)}) collective-permute-start(bf16[1296,128]{1,0:T(8,128)(2,1)} %get-tuple-element.59), channel_id=1, source_target_pairs={{0,6},{1,7},{2,4},{3,5},{4,2},{5,3},{6,0},{7,1},{8,14},{9,15},{10,... | collective-permute-start | bytes 995336 | tf_op jit(solution)/shard_map/ppermute | solution.py:461
  41.4 21.1 %collective-permute-start.7 = (bf16[400,512]{1,0:T(8,128)(2,1)S(1)}, bf16[400,512]{1,0:T(8,128)(2,1)S(1)}, u32[]{:S(2)}, u32[]{:S(2)}) collective-permute-start(bf16[400,512]{1,0:T(8,128)(2,1)S(1)} %get-tuple-element.75), channel_id=1, source_target_pairs={{0,8},{8,0},{1,9},{9,1},{2,10},{10,2},{3,11},{11,3},{4,12},{12,4},... | collective-permute-start | bytes 1228808 | tf_op jit(solution)/shard_map/ppermute | solution.py:511
  64.9 7.1 %collective-permute-start.8 = (bf16[784,128]{1,0:T(8,128)(2,1)S(1)}, bf16[784,128]{1,0:T(8,128)(2,1)S(1)}, u32[]{:S(2)}, u32[]{:S(2)}) collective-permute-start(bf16[784,128]{1,0:T(8,128)(2,1)S(1)} %get-tuple-element.77), channel_id=1, source_target_pairs={{0,2},{1,3},{2,0},{3,1},{4,6},{5,7},{6,4},{7,5},{8,10},{9,11},{10,... | collective-permute-start | bytes 602120 | tf_op jit(solution)/shard_map/ppermute | solution.py:461
  65.4 7.9 %collective-permute-start.9 = (bf16[784,128]{1,0:T(8,128)(2,1)S(1)}, bf16[784,128]{1,0:T(8,128)(2,1)S(1)}, u32[]{:S(2)}, u32[]{:S(2)}) collective-permute-start(bf16[784,128]{1,0:T(8,128)(2,1)S(1)} %get-tuple-element.78), channel_id=1, source_target_pairs={{0,4},{1,5},{2,6},{3,7},{4,0},{5,1},{6,2},{7,3},{8,12},{9,13},{10,... | collective-permute-start | bytes 602120 | tf_op jit(solution)/shard_map/ppermute | solution.py:461
  66.2 11.6 %collective-permute-start.10 = (bf16[784,128]{1,0:T(8,128)(2,1)S(1)}, bf16[784,128]{1,0:T(8,128)(2,1)S(1)}, u32[]{:S(2)}, u32[]{:S(2)}) collective-permute-start(bf16[784,128]{1,0:T(8,128)(2,1)S(1)} %get-tuple-element.79), channel_id=1, source_target_pairs={{0,6},{1,7},{2,4},{3,5},{4,2},{5,3},{6,0},{7,1},{8,14},{9,15},{10,... | collective-permute-start | bytes 602120 | tf_op jit(solution)/shard_map/ppermute | solution.py:461
  70.5 7.2 %collective-permute-start.11 = (bf16[784,128]{1,0:T(8,128)(2,1)S(1)}, bf16[784,128]{1,0:T(8,128)(2,1)S(1)}, u32[]{:S(2)}, u32[]{:S(2)}) collective-permute-start(bf16[784,128]{1,0:T(8,128)(2,1)S(1)} %get-tuple-element.90), channel_id=1, source_target_pairs={{0,1},{1,0},{2,3},{3,2},{4,5},{5,4},{6,7},{7,6},{8,9},{9,8},{10,11... | collective-permute-start | bytes 602120 | tf_op jit(solution)/shard_map/ppermute | solution.py:461
  70.6 10.1 %collective-permute-start.12 = (bf16[784,128]{1,0:T(8,128)(2,1)S(1)}, bf16[784,128]{1,0:T(8,128)(2,1)S(1)}, u32[]{:S(2)}, u32[]{:S(2)}) collective-permute-start(bf16[784,128]{1,0:T(8,128)(2,1)S(1)} %get-tuple-element.91), channel_id=1, source_target_pairs={{0,3},{1,2},{2,1},{3,0},{4,7},{5,6},{6,5},{7,4},{8,11},{9,10},{10,... | collective-permute-start | bytes 602120 | tf_op jit(solution)/shard_map/ppermute | solution.py:461
  72.0 8.7 %collective-permute-start.13 = (bf16[784,128]{1,0:T(8,128)(2,1)S(1)}, bf16[784,128]{1,0:T(8,128)(2,1)S(1)}, u32[]{:S(2)}, u32[]{:S(2)}) collective-permute-start(bf16[784,128]{1,0:T(8,128)(2,1)S(1)} %get-tuple-element.93), channel_id=1, source_target_pairs={{0,5},{1,4},{2,7},{3,6},{4,1},{5,0},{6,3},{7,2},{8,13},{9,12},{10,... | collective-permute-start | bytes 602120 | tf_op jit(solution)/shard_map/ppermute | solution.py:461
  73.4 10.5 %collective-permute-start.14 = (bf16[784,128]{1,0:T(8,128)(2,1)S(1)}, bf16[784,128]{1,0:T(8,128)(2,1)S(1)}, u32[]{:S(2)}, u32[]{:S(2)}) collective-permute-start(bf16[784,128]{1,0:T(8,128)(2,1)S(1)} %get-tuple-element.95), channel_id=1, source_target_pairs={{0,7},{1,6},{2,5},{3,4},{4,3},{5,2},{6,1},{7,0},{8,15},{9,14},{10,... | collective-permute-start | bytes 602120 | tf_op jit(solution)/shard_map/ppermute | solution.py:461

commit v6 on v5

--- a/solution.py
+++ b/solution.py
@@ -232,6 +232,15 @@
     return jnp.where(code < 0.0, -size, size)
 
 
+def encode_into(send_ref, value, logs):
+    top = jnp.maximum(jnp.max(jnp.abs(value), axis=0, keepdims=True), 1e-30)
+    scale = (top * 1.01).astype(BF16).astype(F32)
+    send_ref[:STATE] = encode(value, scale)
+    notes = [scale] + [part.astype(F32) for log in logs for part in split2(log[:1])]
+    notes += [jnp.zeros((TILE - len(notes), value.shape[1]), F32)]
+    send_ref[STATE:] = cat(notes, 0).astype(BF16)
+
+
 def totals_kernel(place, turn, rate_ref, *refs):
     blocks, refs = refs[: place.half], refs[place.half :]
     others, refs = ([], refs) if turn else (refs[:3], refs[3:])
@@ -257,24 +266,21 @@
     total_s = dot(b_turned, u_parts[0]) + dot(b_turned, u_parts[1])
     total_g = dot(c_turned, v_parts[0]) + dot(c_turned, v_parts[1])
     log = jnp.broadcast_to(start_wide[tokens - 1 :, :], (ROWS, width))
+    front, early = lax.axis_index("hi") == 0, lax.axis_index("ctx") == 0
+    middle = jnp.where(front, total_s, total_g)
     if turn:
+        encode_into(refs[3], jnp.where(early, total_g, total_s), [])
+        encode_into(refs[4], middle, [])
         for ref, value in zip(refs, (total_s, total_g, log)):
             ref[...] = value
         return
-    own_ref, send_ref = refs
-    front, early = lax.axis_index("hi") == 0, lax.axis_index("ctx") == 0
+    own_ref, send_ref, middle_ref = refs
     other_s, other_g, other_log = (ref[...] for ref in others)
     logs = [jnp.where(early, log, other_log), jnp.where(early, other_log, log)]
-    middle = jnp.where(front, jnp.where(early, other_s, total_s), jnp.where(early, total_g, other_g))
-    values = [jnp.where(early, total_s, other_s), middle, jnp.where(early, other_g, total_g)]
-    tops = [jnp.maximum(jnp.max(jnp.abs(value), axis=0, keepdims=True), 1e-30) for value in values]
-    scales = [(top * 1.01).astype(BF16).astype(F32) for top in tops]
-    for i, (value, scale) in enumerate(zip(values, scales)):
-        send_ref[i * STATE : (i + 1) * STATE] = encode(value, scale)
-    notes = scales + [part.astype(F32) for log in logs for part in split2(log[:1])]
-    send_ref[3 * STATE :] = cat(notes + [jnp.zeros((TILE - len(notes), width), F32)], 0).astype(BF16)
-    own_ref[:STATE] = values[0]
-    own_ref[STATE : 2 * STATE] = values[2]
+    encode_into(send_ref, jnp.where(early, total_s, total_g), logs)
+    encode_into(middle_ref, middle, [])
+    own_ref[:STATE] = jnp.where(early, total_s, other_s)
+    own_ref[STATE : 2 * STATE] = jnp.where(early, other_g, total_g)
     own_ref[2 * STATE :] = cat(logs, 0)
 
 
@@ -291,13 +297,8 @@
     return total
 
 
-def middle_kernel(place, rate_ref, *refs):
-    for turn in range(2):
-        middle_segment(place, rate_ref[...], refs[turn], *refs[2 + 4 * turn : 6 + 4 * turn])
-
-
-def middle_segment(place, rate, buf, dx_ref, ddt_ref, db_ref, dc_ref):
-    tokens, width = place.tokens, place.width
+def middle_kernel(place, rate_ref, buf, dx_ref, ddt_ref, db_ref, dc_ref):
+    rate, tokens, width = rate_ref[...], place.tokens, place.width
     chunks = [buf.at[i] for i in range(place.half)]
     dts = [place.dt(chunk) for chunk in chunks]
     cums = cumulate(cat([dt * rate for dt in dts], 0), False)
@@ -373,12 +374,16 @@
         ddt_ref[i] = along / jnp.where(dts[i] > 0.0, dts[i], 1.0) + rate * dlog
 
 
-def carried_in(own, got, seg, front):
-    notes = got[3 * STATE :].astype(F32)
+def carried_in(own, first, first_middle, second, second_middle, seg, front):
     sent0, sent2, logs = own[:STATE], own[STATE : 2 * STATE], (own[2 * STATE : 2 * STATE + 1], own[2 * STATE + ROWS : 2 * STATE + ROWS + 1])
-    got0, got1, got2 = (decode(got[i * STATE : (i + 1) * STATE], notes[i : i + 1]) for i in range(3))
+    early = lax.axis_index("ctx") == 0
+    crossed, late = (decode(part[:STATE], part[STATE:].astype(F32)[:1]) for part in (first, second))
+    got0, got2 = jnp.where(early, late, crossed), jnp.where(early, crossed, late)
+    middle = jnp.where(front == early, second_middle[...].astype(F32), first_middle[...].astype(F32))
+    got1 = decode(middle[:STATE], middle[STATE : STATE + 1])
+    notes = second[STATE:].astype(F32)
     mine = jnp.where(front, logs[1], logs[0])
-    other = jnp.where(front, notes[3:4] + notes[4:5], notes[5:6] + notes[6:7])
+    other = jnp.where(front, notes[1:2] + notes[2:3], notes[3:4] + notes[4:5])
     far = got1 + other * (jnp.where(front, sent2, sent0) + mine * jnp.where(front, got2, got0))
     near = jnp.where(front, got0, got2) + other * jnp.where(front, sent0, sent2)
     none = jnp.zeros_like(far)
@@ -390,8 +395,8 @@
 def finish_kernel(place, turn, rate_ref, buf, u_rows, u_parts, v_parts, dx_in, ddt_in, db_in, dc_in, *refs):
     rate, tokens, width = rate_ref[...], place.tokens, place.width
     if turn == 0:
-        (own, got), *refs = refs[:2], *refs[2:]
-        (state, grad, through), rest = carried_in(own, got, lax.axis_index("ctx"), lax.axis_index("hi") == 0)
+        got, refs = refs[:5], refs[5:]
+        (state, grad, through), rest = carried_in(*got, lax.axis_index("ctx"), lax.axis_index("hi") == 0)
         for ref, value in zip(refs, rest):
             ref[...] = jnp.broadcast_to(value, ref.shape)
     else:
@@ -490,9 +495,9 @@
         compiler_params=pltpu.CompilerParams(vmem_limit_bytes=58 * 1024 * 1024),
         name="pack",
     )(*seqs)
-    arrived = swap(sent, [*range(half, count), *range(1, half)])
-
-    owned, coded = (2 * STATE + 2 * ROWS, width), (3 * STATE + TILE, width)
+    arrived = swap(sent, [*range(half + 1, count), half, *range(1, half)])
+
+    owned, coded = (2 * STATE + 2 * ROWS, width), (STATE + TILE, width)
     data_shapes = [bf16(half, place.rows_in, LANES), f32(half, ROWS, tokens)] + [bf16(2, half * tokens, width)] * 2
     carry_shapes = [f32(STATE, width), f32(STATE, width), f32(ROWS, width)]
 
@@ -506,20 +511,28 @@
             name="totals",
         )(rate, *blocks, *others)
 
-    *data1, other_s, other_g, other_log = totals(1, arrived[half:], [], carry_shapes)
-    *data0, own, send = totals(0, arrived[:half], [other_s, other_g, other_log], [f32(*owned), bf16(*coded)])
-    got = lax.ppermute(send, "hi", [(0, 1), (1, 0)])
+    def cross(send, middle, early):
+        pairs = [(0, 2), (3, 1)] if early else [(1, 3), (2, 0)]
+        return lax.ppermute(send, "hi", [(0, 1), (1, 0)]), lax.ppermute(middle, ("hi", "ctx"), pairs)
+
+    sends = [bf16(*coded)] * 2
+    *data1, other_s, other_g, other_log, send, middle_send = totals(1, arrived[half:], [], carry_shapes + sends)
+    first_send = send
+    first, first_middle = cross(send, middle_send, True)
+    *data0, own, send, middle_send = totals(0, [after(block, first_send) for block in arrived[:half]], [other_s, other_g, other_log], [f32(*owned)] + sends)
+    second, second_middle = cross(send, middle_send, False)
 
     within = [f32(half, tokens, width), f32(half, ROWS, tokens), f32(half, tokens, STATE), f32(half, tokens, STATE)]
-    parts = pl.pallas_call(
-        functools.partial(middle_kernel, place),
-        in_specs=[vmem] * 3,
-        out_specs=[vmem] * 8,
-        out_shape=within * 2,
-        compiler_params=params,
-        cost_estimate=pl.CostEstimate(flops=6_000_000_000, bytes_accessed=20_000_000, transcendentals=2_000_000),
-        name="middle",
-    )(rate, data0[0], data1[0])
+    def middle(data):
+        return pl.pallas_call(
+            functools.partial(middle_kernel, place),
+            in_specs=[vmem] * 2,
+            out_specs=[vmem] * 4,
+            out_shape=within,
+            compiler_params=params,
+            cost_estimate=pl.CostEstimate(flops=3_000_000_000, bytes_accessed=10_000_000, transcendentals=1_000_000),
+            name="middle",
+        )(rate, data[0])
 
     def finish(turn, data, parts, others, shapes):
         return pl.pallas_call(
@@ -532,9 +545,11 @@
             name="finish",
         )(rate, *data, *parts, *others)
 
-    state, grad, through, *outs0 = finish(0, data0, parts[:4], [own, got], carry_shapes)
-    outs1 = finish(1, data1, parts[4:], [state, grad, through], [])
-    homes = swap([*outs0, *outs1], range(1, count))
+    parts1, parts0 = middle(data1), middle(data0)
+    second = after(second, parts1[0])
+    state, grad, through, *outs0 = finish(0, data0, parts0, [own, first, first_middle, second, second_middle], carry_shapes)
+    outs1 = finish(1, data1, parts1, [state, grad, through], [])
+    homes = swap([*outs0, *outs1], [*range(1, half), *range(half + 1, count), half])
 
     dx, ddt, db, dc = pl.pallas_call(
         functools.partial(unpack_kernel, place, count, copies),

time: 86.2 us -> 79.8 us (0.926)
  waiting for transfers between devices: 43.4 us -> 28.2 us
  starting transfers between devices: 17.6 us -> 27.2 us
  Pallas kernels: 23.4 us -> 22.5 us
    ppermute x14, waiting for transfers between devices: 36.8 us -> 24.1 us  [swap(): lax.ppermute(block, ('lo', 'ctx'), [(i, i ^ turn) for i in range(count)])]
    ppermute x1 -> x4, starting transfers between devices: 2.65 us -> 11.2 us  [the longest x2 6.73 us: cross(): lax.ppermute(middle, ('hi', 'ctx'), pairs)]
    ppermute x1 -> x4, waiting for transfers between devices: 6.61 us -> 4.04 us  [the longest x2 2.46 us: cross(): lax.ppermute(send, 'hi', [(0, 1), (1, 0)])]
    pallas_call x1 -> x2, Pallas kernels: 11.8 us -> 10.7 us  [middle(): pl.pallas_call(functools.partial(middle_kernel, place), in_specs=[vmem] *...]
    ppermute x14, starting transfers between devices: 14.9 us -> 16.1 us  [swap(): lax.ppermute(block, ('lo', 'ctx'), [(i, i ^ turn) for i in range(count)])]
  transfers between devices with their start and end apart: 15 -> 18, of which waited for: 11 -> 10; matrix products, arithmetic and copies ran while one was open for 0% -> 0% of each run, Pallas kernels for 18% -> 20%
where the time goes in v6:
time: 79.8 us; the launch traced here: 78.9 us
  waiting for transfers between devices  28.2 us (35%)
  starting transfers between devices  27.2 us (34%)
  Pallas kernels  22.5 us (28%)
  between operations  0.89 us (1%)
    ppermute x14, waiting for transfers between devices, swap(): lax.ppermute(block, ('lo', 'ctx'), [(i, i ^ turn) for i in range(count)])  24.1 us
    ppermute x14, starting transfers between devices, swap(): lax.ppermute(block, ('lo', 'ctx'), [(i, i ^ turn) for i in range(count)])  16.1 us
    pallas_call x2, Pallas kernels, middle(): pl.pallas_call(functools.partial(middle_kernel, place), in_specs=[vmem] *...  10.7 us
    ppermute x2, starting transfers between devices, cross(): lax.ppermute(middle, ('hi', 'ctx'), pairs)  6.73 us
    pallas_call x2, Pallas kernels, finish(): pl.pallas_call(functools.partial(finish_kernel, place, turn), in_specs=[v...  4.58 us
    ppermute x2, starting transfers between devices, cross(): lax.ppermute(send, 'hi', [(0, 1), (1, 0)])  4.42 us
    pallas_call x2, Pallas kernels, totals(): pl.pallas_call(functools.partial(totals_kernel, place, turn), in_specs=[v...  2.91 us
    pallas_call x1, Pallas kernels, on_device(): pl.pallas_call(functools.partial(pack_kernel, place, count, copies), in_s...  2.91 us
  transfers between devices with their start and end apart: 18, of which 10 were waited for; matrix products, arithmetic and copies ran while one was open for 0% of the time, Pallas kernels for 20%

profile of v6, /device:TPU:0, one launch (start us, length us, event | category | flops | bytes accessed | tf_op | source)
XLA Modules:
  0.0 78.9 jit_solution(2903867797098259147)
XLA Ops:
  0.6 2.9 %pack.1 = (bf16[1296,128]{1,0:T(8,128)(2,1)}, bf16[1296,128]{1,0:T(8,128)(2,1)}, bf16[1296,128]{1,0:T(8,128)(2,1)}, bf16[1296,128]{1,0:T(8,128)(2,1)}, bf16[1296...) custom-call(bf16[128,8,128]{2,1,0:T(8,128)(2,1)} %refs_0_.1, ...), custom_call_target="tpu_custom_call" | custom-call | tf_op jit(solution)/shard_map/pack/pallas_call | solution.py:486
  3.6 2.5 %collective-permute-start.1 = (bf16[1296,128]{1,0:T(8,128)(2,1)}, bf16[1296,128]{1,0:T(8,128)(2,1)S(1)}, u32[]{:S(2)}, u32[]{:S(2)}) collective-permute-start(bf16[1296,128]{1,0:T(8,128)(2,1)} %get-tuple-element.62), channel_id=1, source_target_pairs={{0,3},{1,2},{2,1},{3,0},{4,7},{5,6},{6,5},{7,4},{8,11},{9,10},{10,... | collective-permute-start | bytes 995336 | tf_op jit(solution)/shard_map/ppermute | solution.py:466
  6.0 1.9 %collective-permute-start.2 = (bf16[1296,128]{1,0:T(8,128)(2,1)}, bf16[1296,128]{1,0:T(8,128)(2,1)S(1)}, u32[]{:S(2)}, u32[]{:S(2)}) collective-permute-start(bf16[1296,128]{1,0:T(8,128)(2,1)} %get-tuple-element.63), channel_id=1, source_target_pairs={{0,5},{1,4},{2,7},{3,6},{4,1},{5,0},{6,3},{7,2},{8,13},{9,12},{10,... | collective-permute-start | bytes 995336 | tf_op jit(solution)/shard_map/ppermute | solution.py:466
  7.9 2.0 %collective-permute-start.4 = (bf16[1296,128]{1,0:T(8,128)(2,1)}, bf16[1296,128]{1,0:T(8,128)(2,1)S(1)}, u32[]{:S(2)}, u32[]{:S(2)}) collective-permute-start(bf16[1296,128]{1,0:T(8,128)(2,1)} %get-tuple-element.67), channel_id=1, source_target_pairs={{0,2},{1,3},{2,0},{3,1},{4,6},{5,7},{6,4},{7,5},{8,10},{9,11},{10,... | collective-permute-start | bytes 995336 | tf_op jit(solution)/shard_map/ppermute | solution.py:466
  9.9 4.6 %collective-permute-done.1.refs_1_ = bf16[1296,128]{1,0:T(8,128)(2,1)S(1)} collective-permute-done((bf16[1296,128]{1,0:T(8,128)(2,1)}, bf16[1296,128]{1,0:T(8,128)(2,1)S(1)}, u32[]{:S(2)}, u32[]{:S(2)}) %collective-permute-start.1) | collective-permute-done | bytes 331808 | tf_op jit(solution)/shard_map/ppermute | solution.py:466
  14.5 2.3 %collective-permute-start.5 = (bf16[1296,128]{1,0:T(8,128)(2,1)}, bf16[1296,128]{1,0:T(8,128)(2,1)S(1)}, u32[]{:S(2)}, u32[]{:S(2)}) collective-permute-start(bf16[1296,128]{1,0:T(8,128)(2,1)} %get-tuple-element.70), channel_id=1, source_target_pairs={{0,4},{1,5},{2,6},{3,7},{4,0},{5,1},{6,2},{7,3},{8,12},{9,13},{10,... | collective-permute-start | bytes 995336 | tf_op jit(solution)/shard_map/ppermute | solution.py:466
  16.9 1.5 %collective-permute-start.6 = (bf16[1296,128]{1,0:T(8,128)(2,1)}, bf16[1296,128]{1,0:T(8,128)(2,1)S(1)}, u32[]{:S(2)}, u32[]{:S(2)}) collective-permute-start(bf16[1296,128]{1,0:T(8,128)(2,1)} %get-tuple-element.73), channel_id=1, source_target_pairs={{0,6},{1,7},{2,4},{3,5},{4,2},{5,3},{6,0},{7,1},{8,14},{9,15},{10,... | collective-permute-start | bytes 995336 | tf_op jit(solution)/shard_map/ppermute | solution.py:466
  18.4 5.1 %collective-permute-done.3.refs_3_ = bf16[1296,128]{1,0:T(8,128)(2,1)S(1)} collective-permute-done((bf16[1296,128]{1,0:T(8,128)(2,1)}, bf16[1296,128]{1,0:T(8,128)(2,1)S(1)}, u32[]{:S(2)}, u32[]{:S(2)}) %collective-permute-start.3) | collective-permute-done | bytes 331808 | tf_op jit(solution)/shard_map/ppermute | solution.py:466
  23.6 1.4 %totals.2 = (bf16[4,1296,128]{2,1,0:T(8,128)(2,1)S(1)}, f32[4,8,128]{2,1,0:T(8,128)S(1)}, bf16[2,512,512]{2,1,0:T(8,128)(2,1)S(1)}, bf16[2,512,512]{2,1,0:T(8,12...) custom-call(f32[8,128]{1,0:T(8,128)S(1)} %broadcast_in_dim.2.rate_re, ...), custom_call_target="tpu_custom_call" | custom-call | tf_op jit(solution)/shard_map/totals/pallas_call | solution.py:505
  25.0 2.7 %collective-permute-start.7 = (bf16[144,512]{1,0:T(8,128)(2,1)S(1)}, bf16[144,512]{1,0:T(8,128)(2,1)S(1)}, u32[]{:S(2)}, u32[]{:S(2)}) collective-permute-start(bf16[144,512]{1,0:T(8,128)(2,1)S(1)} %get-tuple-element.65), channel_id=1, source_target_pairs={{0,8},{8,0},{1,9},{9,1},{2,10},{10,2},{3,11},{11,3},{4,12},{12,4},... | collective-permute-start | bytes 442376 | tf_op jit(solution)/shard_map/ppermute | solution.py:516
  27.7 1.1 %collective-permute-done.4.refs_1_ = bf16[1296,128]{1,0:T(8,128)(2,1)S(1)} collective-permute-done((bf16[1296,128]{1,0:T(8,128)(2,1)}, bf16[1296,128]{1,0:T(8,128)(2,1)S(1)}, u32[]{:S(2)}, u32[]{:S(2)}) %collective-permute-start.4) | collective-permute-done | bytes 331808 | tf_op jit(solution)/shard_map/ppermute | solution.py:466
  28.8 5.3 %collective-permute-start.8 = (bf16[144,512]{1,0:T(8,128)(2,1)S(1)}, bf16[144,512]{1,0:T(8,128)(2,1)S(1)}, u32[]{:S(2)}, u32[]{:S(2)}) collective-permute-start(bf16[144,512]{1,0:T(8,128)(2,1)S(1)} %get-tuple-element.87), channel_id=1, source_target_pairs={{0,8},{9,1},{2,10},{11,3},{4,12},{13,5},{6,14},{15,7},{16,24},{25,... | collective-permute-start | bytes 442376 | tf_op jit(solution)/shard_map/ppermute | solution.py:516
  34.1 5.3 %middle.3 = (f32[4,128,512]{2,1,0:T(8,128)S(1)}, f32[4,8,128]{2,1,0:T(8,128)S(1)}, f32[4,128,128]{2,1,0:T(8,128)S(1)}, f32[4,128,128]{2,1,0:T(8,128)S(1)}) custom-call(f32[8,128]{1,0:T(8,128)S(1)} %broadcast_in_dim.2.rate_ref, bf16[4,1296,128]{2,1,0:T(8,128)(2,1)S(1)} %get-tuple-element.89.buf), custom_call_target="tpu_custom_call" | custom-call | flops 3000000000 | bytes 10000000 | tf_op jit(solution)/shard_map/middle/pallas_call | solution.py:527
  39.4 3.1 %collective-permute-done.6.refs_3_ = bf16[1296,128]{1,0:T(8,128)(2,1)S(1)} collective-permute-done((bf16[1296,128]{1,0:T(8,128)(2,1)}, bf16[1296,128]{1,0:T(8,128)(2,1)S(1)}, u32[]{:S(2)}, u32[]{:S(2)}) %collective-permute-start.6) | collective-permute-done | bytes 331808 | tf_op jit(solution)/shard_map/ppermute | solution.py:466
  42.5 1.5 %totals.3 = (bf16[4,1296,128]{2,1,0:T(8,128)(2,1)S(1)}, f32[4,8,128]{2,1,0:T(8,128)S(1)}, bf16[2,512,512]{2,1,0:T(8,128)(2,1)S(1)}, bf16[2,512,512]{2,1,0:T(8,12...) custom-call(f32[8,128]{1,0:T(8,128)S(1)} %broadcast_in_dim.2.rate_ref, ...), custom_call_target="tpu_custom_call" | custom-call | tf_op jit(solution)/shard_map/totals/pallas_call | solution.py:505
  44.0 1.8 %collective-permute-start.9 = (bf16[144,512]{1,0:T(8,128)(2,1)S(1)}, bf16[144,512]{1,0:T(8,128)(2,1)S(1)}, u32[]{:S(2)}, u32[]{:S(2)}) collective-permute-start(bf16[144,512]{1,0:T(8,128)(2,1)S(1)} %get-tuple-element.88), channel_id=1, source_target_pairs={{0,8},{8,0},{1,9},{9,1},{2,10},{10,2},{3,11},{11,3},{4,12},{12,4},... | collective-permute-start | bytes 442376 | tf_op jit(solution)/shard_map/ppermute | solution.py:516
  45.8 1.5 %collective-permute-start.10 = (bf16[144,512]{1,0:T(8,128)(2,1)S(1)}, bf16[144,512]{1,0:T(8,128)(2,1)S(1)}, u32[]{:S(2)}, u32[]{:S(2)}) collective-permute-start(bf16[144,512]{1,0:T(8,128)(2,1)S(1)} %get-tuple-element.92), channel_id=1, source_target_pairs={{1,9},{8,0},{3,11},{10,2},{5,13},{12,4},{7,15},{14,6},{17,25},{24,... | collective-permute-start | bytes 442376 | tf_op jit(solution)/shard_map/ppermute | solution.py:516
  47.3 5.3 %middle.2 = (f32[4,128,512]{2,1,0:T(8,128)S(1)}, f32[4,8,128]{2,1,0:T(8,128)S(1)}, f32[4,128,128]{2,1,0:T(8,128)S(1)}, f32[4,128,128]{2,1,0:T(8,128)S(1)}) custom-call(f32[8,128]{1,0:T(8,128)S(1)} %broadcast_in_dim.2.rate_ref, bf16[4,1296,128]{2,1,0:T(8,128)(2,1)S(1)} %get-tuple-element.78.buf), custom_call_target="tpu_custom_call" | custom-call | flops 3000000000 | bytes 10000000 | tf_op jit(solution)/shard_map/middle/pallas_call | solution.py:527
  52.6 2.5 %collective-permute-done.9.refs_3_ = bf16[144,512]{1,0:T(8,128)(2,1)S(1)} collective-permute-done((bf16[144,512]{1,0:T(8,128)(2,1)S(1)}, bf16[144,512]{1,0:T(8,128)(2,1)S(1)}, u32[]{:S(2)}, u32[]{:S(2)}) %collective-permute-start.9) | collective-permute-done | bytes 147488 | tf_op jit(solution)/shard_map/ppermute | solution.py:516
  55.1 1.6 %collective-permute-done.10.refs_4_ = bf16[144,512]{1,0:T(8,128)(2,1)S(1)} collective-permute-done((bf16[144,512]{1,0:T(8,128)(2,1)S(1)}, bf16[144,512]{1,0:T(8,128)(2,1)S(1)}, u32[]{:S(2)}, u32[]{:S(2)}) %collective-permute-start.10) | collective-permute-done | bytes 147488 | tf_op jit(solution)/shard_map/ppermute | solution.py:516
  56.6 2.5 %finish.2 = (f32[128,512]{1,0:T(8,128)S(1)}, f32[128,512]{1,0:T(8,128)S(1)}, f32[8,512]{1,0:T(8,128)S(1)}, bf16[784,128]{1,0:T(8,128)(2,1)S(1)}, bf16[784,128]{1...) custom-call(f32[8,128]{1,0:T(8,128)S(1)} %broadcast_in_dim.2.rate_ref, ...), custom_call_target="tpu_custom_call" | custom-call | tf_op jit(solution)/shard_map/finish/pallas_call | solution.py:538
  59.2 1.4 %collective-permute-start.11 = (bf16[784,128]{1,0:T(8,128)(2,1)S(1)}, bf16[784,128]{1,0:T(8,128)(2,1)S(1)}, u32[]{:S(2)}, u32[]{:S(2)}) collective-permute-start(bf16[784,128]{1,0:T(8,128)(2,1)S(1)} %get-tuple-element.94), channel_id=1, source_target_pairs={{0,2},{1,3},{2,0},{3,1},{4,6},{5,7},{6,4},{7,5},{8,10},{9,11},{10,... | collective-permute-start | bytes 602120 | tf_op jit(solution)/shard_map/ppermute | solution.py:466
  60.6 2.2 %collective-permute-start.13 = (bf16[784,128]{1,0:T(8,128)(2,1)S(1)}, bf16[784,128]{1,0:T(8,128)(2,1)S(1)}, u32[]{:S(2)}, u32[]{:S(2)}) collective-permute-start(bf16[784,128]{1,0:T(8,128)(2,1)S(1)} %get-tuple-element.96), channel_id=1, source_target_pairs={{0,6},{1,7},{2,4},{3,5},{4,2},{5,3},{6,0},{7,1},{8,14},{9,15},{10,... | collective-permute-start | bytes 602120 | tf_op jit(solution)/shard_map/ppermute | solution.py:466
  62.7 2.0 %finish.3 = (bf16[784,128]{1,0:T(8,128)(2,1)S(1)}, bf16[784,128]{1,0:T(8,128)(2,1)S(1)}, bf16[784,128]{1,0:T(8,128)(2,1)S(1)}, bf16[784,128]{1,0:T(8,128)(2,1)S(1)}) custom-call(f32[8,128]{1,0:T(8,128)S(1)} %broadcast_in_dim.2.rate_ref, bf16[4,1296,128]{2,1,0:T(8,128)(2,1)S(1)} %get-tuple-element.89.buf, f32[4,8,128]{2,1,0:T(8,128)S(1)} %get-tuple-element.97.u_rows, ...), custom_call_target="tpu_custom_call" | custom-call | tf_op jit(solution)/shard_map/finish/pallas_call | solution.py:538
  64.9 1.1 %collective-permute-start.16 = (bf16[784,128]{1,0:T(8,128)(2,1)S(1)}, bf16[784,128]{1,0:T(8,128)(2,1)S(1)}, u32[]{:S(2)}, u32[]{:S(2)}) collective-permute-start(bf16[784,128]{1,0:T(8,128)(2,1)S(1)} %get-tuple-element.109), channel_id=1, source_target_pairs={{0,5},{1,4},{2,7},{3,6},{4,1},{5,0},{6,3},{7,2},{8,13},{9,12},{10,... | collective-permute-start | bytes 602120 | tf_op jit(solution)/shard_map/ppermute | solution.py:466
  66.0 1.0 %collective-permute-done.11.refs_1_ = bf16[784,128]{1,0:T(8,128)(2,1)S(1)} collective-permute-done((bf16[784,128]{1,0:T(8,128)(2,1)S(1)}, bf16[784,128]{1,0:T(8,128)(2,1)S(1)}, u32[]{:S(2)}, u32[]{:S(2)}) %collective-permute-start.11) | collective-permute-done | bytes 200736 | tf_op jit(solution)/shard_map/ppermute | solution.py:466
  67.0 0.5 collective-permute-start.17
  67.5 0.7 collective-permute-start.14
  68.2 3.2 %collective-permute-done.13.refs_3_ = bf16[784,128]{1,0:T(8,128)(2,1)S(1)} collective-permute-done((bf16[784,128]{1,0:T(8,128)(2,1)S(1)}, bf16[784,128]{1,0:T(8,128)(2,1)S(1)}, u32[]{:S(2)}, u32[]{:S(2)}) %collective-permute-start.13) | collective-permute-done | bytes 200736 | tf_op jit(solution)/shard_map/ppermute | solution.py:466
  71.4 3.9 %collective-permute-done.15.refs_5_ = bf16[784,128]{1,0:T(8,128)(2,1)S(1)} collective-permute-done((bf16[784,128]{1,0:T(8,128)(2,1)S(1)}, bf16[784,128]{1,0:T(8,128)(2,1)S(1)}, u32[]{:S(2)}, u32[]{:S(2)}) %collective-permute-start.15) | collective-permute-done | bytes 200736 | tf_op jit(solution)/shard_map/ppermute | solution.py:466
  75.3 2.1 %collective-permute-done.17.refs_7_ = bf16[784,128]{1,0:T(8,128)(2,1)S(1)} collective-permute-done((bf16[784,128]{1,0:T(8,128)(2,1)S(1)}, bf16[784,128]{1,0:T(8,128)(2,1)S(1)}, u32[]{:S(2)}, u32[]{:S(2)}) %collective-permute-start.17) | collective-permute-done | bytes 200736 | tf_op jit(solution)/shard_map/ppermute | solution.py:466
  77.4 1.4 %unpack.1 = (bf16[128,4096]{1,0:T(8,128)(2,1)}, bf16[64,128]{1,0:T(8,128)(2,1)}, bf16[128,8,128]{2,1,0:T(8,128)(2,1)}, bf16[128,8,128]{2,1,0:T(8,128)(2,1)}) custom-call(bf16[784,128]{1,0:T(8,128)(2,1)S(1)} %get-tuple-element.93.refs_0_, bf16[784,128]{1,0:T(8,128)(2,1)S(1)} %collective-permute-done.11.refs_1_, ...), custom_call_target="tpu_custom_call" | custom-call | tf_op jit(solution)/shard_map/unpack/pallas_call | solution.py:554
  (18 shorter events, 0.3 us)
Async XLA Ops:
  0.6 17.7 %copy-start.1 = (f32[64]{0:T(128)S(1)}, f32[64]{0:T(128)}, u32[]{:S(2)}) copy-start(f32[64]{0:T(128)} %param.9) | copy-start | bytes 772
  3.6 11.0 %collective-permute-start.1 = (bf16[1296,128]{1,0:T(8,128)(2,1)}, bf16[1296,128]{1,0:T(8,128)(2,1)S(1)}, u32[]{:S(2)}, u32[]{:S(2)}) collective-permute-start(bf16[1296,128]{1,0:T(8,128)(2,1)} %get-tuple-element.62), channel_id=1, source_target_pairs={{0,3},{1,2},{2,1},{3,0},{4,7},{5,6},{6,5},{7,4},{8,11},{9,10},{10,... | collective-permute-start | bytes 995336 | tf_op jit(solution)/shard_map/ppermute | solution.py:466
  6.0 10.9 %collective-permute-start.2 = (bf16[1296,128]{1,0:T(8,128)(2,1)}, bf16[1296,128]{1,0:T(8,128)(2,1)S(1)}, u32[]{:S(2)}, u32[]{:S(2)}) collective-permute-start(bf16[1296,128]{1,0:T(8,128)(2,1)} %get-tuple-element.63), channel_id=1, source_target_pairs={{0,5},{1,4},{2,7},{3,6},{4,1},{5,0},{6,3},{7,2},{8,13},{9,12},{10,... | collective-permute-start | bytes 995336 | tf_op jit(solution)/shard_map/ppermute | solution.py:466
  7.9 10.6 %collective-permute-start = (bf16[1296,128]{1,0:T(8,128)(2,1)}, bf16[1296,128]{1,0:T(8,128)(2,1)S(1)}, u32[]{:S(2)}, u32[]{:S(2)}) collective-permute-start(bf16[1296,128]{1,0:T(8,128)(2,1)} %get-tuple-element.61), channel_id=1, source_target_pairs={{0,1},{1,0},{2,3},{3,2},{4,5},{5,4},{6,7},{7,6},{8,9},{9,8},{10,11... | collective-permute-start | bytes 995336 | tf_op jit(solution)/shard_map/ppermute | solution.py:466
  7.9 15.6 %collective-permute-start.3 = (bf16[1296,128]{1,0:T(8,128)(2,1)}, bf16[1296,128]{1,0:T(8,128)(2,1)S(1)}, u32[]{:S(2)}, u32[]{:S(2)}) collective-permute-start(bf16[1296,128]{1,0:T(8,128)(2,1)} %get-tuple-element.64), channel_id=1, source_target_pairs={{0,7},{1,6},{2,5},{3,4},{4,3},{5,2},{6,1},{7,0},{8,15},{9,14},{10,... | collective-permute-start | bytes 995336 | tf_op jit(solution)/shard_map/ppermute | solution.py:466
  7.9 20.9 %collective-permute-start.4 = (bf16[1296,128]{1,0:T(8,128)(2,1)}, bf16[1296,128]{1,0:T(8,128)(2,1)S(1)}, u32[]{:S(2)}, u32[]{:S(2)}) collective-permute-start(bf16[1296,128]{1,0:T(8,128)(2,1)} %get-tuple-element.67), channel_id=1, source_target_pairs={{0,2},{1,3},{2,0},{3,1},{4,6},{5,7},{6,4},{7,5},{8,10},{9,11},{10,... | collective-permute-start | bytes 995336 | tf_op jit(solution)/shard_map/ppermute | solution.py:466
  14.5 28.0 %collective-permute-start.5 = (bf16[1296,128]{1,0:T(8,128)(2,1)}, bf16[1296,128]{1,0:T(8,128)(2,1)S(1)}, u32[]{:S(2)}, u32[]{:S(2)}) collective-permute-start(bf16[1296,128]{1,0:T(8,128)(2,1)} %get-tuple-element.70), channel_id=1, source_target_pairs={{0,4},{1,5},{2,6},{3,7},{4,0},{5,1},{6,2},{7,3},{8,12},{9,13},{10,... | collective-permute-start | bytes 995336 | tf_op jit(solution)/shard_map/ppermute | solution.py:466
  16.9 25.7 %collective-permute-start.6 = (bf16[1296,128]{1,0:T(8,128)(2,1)}, bf16[1296,128]{1,0:T(8,128)(2,1)S(1)}, u32[]{:S(2)}, u32[]{:S(2)}) collective-permute-start(bf16[1296,128]{1,0:T(8,128)(2,1)} %get-tuple-element.73), channel_id=1, source_target_pairs={{0,6},{1,7},{2,4},{3,5},{4,2},{5,3},{6,0},{7,1},{8,14},{9,15},{10,... | collective-permute-start | bytes 995336 | tf_op jit(solution)/shard_map/ppermute | solution.py:466
  25.0 30.0 %collective-permute-start.7 = (bf16[144,512]{1,0:T(8,128)(2,1)S(1)}, bf16[144,512]{1,0:T(8,128)(2,1)S(1)}, u32[]{:S(2)}, u32[]{:S(2)}) collective-permute-start(bf16[144,512]{1,0:T(8,128)(2,1)S(1)} %get-tuple-element.65), channel_id=1, source_target_pairs={{0,8},{8,0},{1,9},{9,1},{2,10},{10,2},{3,11},{11,3},{4,12},{12,4},... | collective-permute-start | bytes 442376 | tf_op jit(solution)/shard_map/ppermute | solution.py:516
  28.8 26.2 %collective-permute-start.8 = (bf16[144,512]{1,0:T(8,128)(2,1)S(1)}, bf16[144,512]{1,0:T(8,128)(2,1)S(1)}, u32[]{:S(2)}, u32[]{:S(2)}) collective-permute-start(bf16[144,512]{1,0:T(8,128)(2,1)S(1)} %get-tuple-element.87), channel_id=1, source_target_pairs={{0,8},{9,1},{2,10},{11,3},{4,12},{13,5},{6,14},{15,7},{16,24},{25,... | collective-permute-start | bytes 442376 | tf_op jit(solution)/shard_map/ppermute | solution.py:516
  34.1 8.4 %copy-start = (bf16[1296,128]{1,0:T(8,128)(2,1)S(1)}, bf16[1296,128]{1,0:T(8,128)(2,1)}, u32[]{:S(2)}) copy-start(bf16[1296,128]{1,0:T(8,128)(2,1)} %get-tuple-element.66.refs_0_) | copy-start | bytes 995332
  44.0 11.0 %collective-permute-start.9 = (bf16[144,512]{1,0:T(8,128)(2,1)S(1)}, bf16[144,512]{1,0:T(8,128)(2,1)S(1)}, u32[]{:S(2)}, u32[]{:S(2)}) collective-permute-start(bf16[144,512]{1,0:T(8,128)(2,1)S(1)} %get-tuple-element.88), channel_id=1, source_target_pairs={{0,8},{8,0},{1,9},{9,1},{2,10},{10,2},{3,11},{11,3},{4,12},{12,4},... | collective-permute-start | bytes 442376 | tf_op jit(solution)/shard_map/ppermute | solution.py:516
  45.8 10.8 %collective-permute-start.10 = (bf16[144,512]{1,0:T(8,128)(2,1)S(1)}, bf16[144,512]{1,0:T(8,128)(2,1)S(1)}, u32[]{:S(2)}, u32[]{:S(2)}) collective-permute-start(bf16[144,512]{1,0:T(8,128)(2,1)S(1)} %get-tuple-element.92), channel_id=1, source_target_pairs={{1,9},{8,0},{3,11},{10,2},{5,13},{12,4},{7,15},{14,6},{17,25},{24,... | collective-permute-start | bytes 442376 | tf_op jit(solution)/shard_map/ppermute | solution.py:516
  59.2 7.8 %collective-permute-start.11 = (bf16[784,128]{1,0:T(8,128)(2,1)S(1)}, bf16[784,128]{1,0:T(8,128)(2,1)S(1)}, u32[]{:S(2)}, u32[]{:S(2)}) collective-permute-start(bf16[784,128]{1,0:T(8,128)(2,1)S(1)} %get-tuple-element.94), channel_id=1, source_target_pairs={{0,2},{1,3},{2,0},{3,1},{4,6},{5,7},{6,4},{7,5},{8,10},{9,11},{10,... | collective-permute-start | bytes 602120 | tf_op jit(solution)/shard_map/ppermute | solution.py:466
  60.6 6.9 %collective-permute-start.12 = (bf16[784,128]{1,0:T(8,128)(2,1)S(1)}, bf16[784,128]{1,0:T(8,128)(2,1)S(1)}, u32[]{:S(2)}, u32[]{:S(2)}) collective-permute-start(bf16[784,128]{1,0:T(8,128)(2,1)S(1)} %get-tuple-element.95), channel_id=1, source_target_pairs={{0,4},{1,5},{2,6},{3,7},{4,0},{5,1},{6,2},{7,3},{8,12},{9,13},{10,... | collective-permute-start | bytes 602120 | tf_op jit(solution)/shard_map/ppermute | solution.py:466
  60.6 10.8 %collective-permute-start.13 = (bf16[784,128]{1,0:T(8,128)(2,1)S(1)}, bf16[784,128]{1,0:T(8,128)(2,1)S(1)}, u32[]{:S(2)}, u32[]{:S(2)}) collective-permute-start(bf16[784,128]{1,0:T(8,128)(2,1)S(1)} %get-tuple-element.96), channel_id=1, source_target_pairs={{0,6},{1,7},{2,4},{3,5},{4,2},{5,3},{6,0},{7,1},{8,14},{9,15},{10,... | collective-permute-start | bytes 602120 | tf_op jit(solution)/shard_map/ppermute | solution.py:466
  64.8 10.5 %collective-permute-start.15 = (bf16[784,128]{1,0:T(8,128)(2,1)S(1)}, bf16[784,128]{1,0:T(8,128)(2,1)S(1)}, u32[]{:S(2)}, u32[]{:S(2)}) collective-permute-start(bf16[784,128]{1,0:T(8,128)(2,1)S(1)} %get-tuple-element.108), channel_id=1, source_target_pairs={{0,3},{1,2},{2,1},{3,0},{4,7},{5,6},{6,5},{7,4},{8,11},{9,10},{10,... | collective-permute-start | bytes 602120 | tf_op jit(solution)/shard_map/ppermute | solution.py:466
  64.9 10.4 %collective-permute-start.16 = (bf16[784,128]{1,0:T(8,128)(2,1)S(1)}, bf16[784,128]{1,0:T(8,128)(2,1)S(1)}, u32[]{:S(2)}, u32[]{:S(2)}) collective-permute-start(bf16[784,128]{1,0:T(8,128)(2,1)S(1)} %get-tuple-element.109), channel_id=1, source_target_pairs={{0,5},{1,4},{2,7},{3,6},{4,1},{5,0},{6,3},{7,2},{8,13},{9,12},{10,... | collective-permute-start | bytes 602120 | tf_op jit(solution)/shard_map/ppermute | solution.py:466
  67.0 10.4 %collective-permute-start.17 = (bf16[784,128]{1,0:T(8,128)(2,1)S(1)}, bf16[784,128]{1,0:T(8,128)(2,1)S(1)}, u32[]{:S(2)}, u32[]{:S(2)}) collective-permute-start(bf16[784,128]{1,0:T(8,128)(2,1)S(1)} %get-tuple-element.111), channel_id=1, source_target_pairs={{0,7},{1,6},{2,5},{3,4},{4,3},{5,2},{6,1},{7,0},{8,15},{9,14},{10,... | collective-permute-start | bytes 602120 | tf_op jit(solution)/shard_map/ppermute | solution.py:466
  67.5 9.9 %collective-permute-start.14 = (bf16[784,128]{1,0:T(8,128)(2,1)S(1)}, bf16[784,128]{1,0:T(8,128)(2,1)S(1)}, u32[]{:S(2)}, u32[]{:S(2)}) collective-permute-start(bf16[784,128]{1,0:T(8,128)(2,1)S(1)} %get-tuple-element.107), channel_id=1, source_target_pairs={{0,1},{1,0},{2,3},{3,2},{4,5},{5,4},{6,7},{7,6},{8,9},{9,8},{10,11... | collective-permute-start | bytes 602120 | tf_op jit(solution)/shard_map/ppermute | solution.py:466

commit v7 on v6

--- a/solution.py
+++ b/solution.py
@@ -456,15 +456,14 @@
     def after(value, *others):
         return lax.optimization_barrier((value, *others))[0]
 
-    def swap(blocks, order):
-        got, under_way = {0: blocks[0]}, []
-        for k in order:
+    def swap(blocks, order, done):
+        got = {0: blocks[0]}
+        for i, k in enumerate(order):
             turn = (k % half) * 2 + k // half
             block = blocks[k]
-            if len(under_way) >= IN_FLIGHT:
-                block = after(block, under_way[-IN_FLIGHT])
-            got[k] = lax.ppermute(block, ("lo", "ctx"), [(i, i ^ turn) for i in range(count)])
-            under_way.append(got[k])
+            if i >= IN_FLIGHT:
+                block = after(block, got[done[i - IN_FLIGHT]])
+            got[k] = lax.ppermute(block, ("lo", "ctx"), [(j, j ^ turn) for j in range(count)])
         return [got[k] for k in range(count)]
 
     rates = -jnp.exp(lax.dynamic_slice_in_dim(a_log, lax.axis_index(("ctx", "lo")) * heads, heads))
@@ -495,7 +494,9 @@
         compiler_params=pltpu.CompilerParams(vmem_limit_bytes=58 * 1024 * 1024),
         name="pack",
     )(*seqs)
-    arrived = swap(sent, [*range(half + 1, count), half, *range(1, half)])
+    own_turns = [*range(half // 2, half), *range(1, half // 2)]
+    other_turns = [half + k for k in own_turns]
+    arrived = swap(sent, [*other_turns[:3], half, *other_turns[3:], *own_turns], [half, *other_turns, *own_turns])
 
     owned, coded = (2 * STATE + 2 * ROWS, width), (STATE + TILE, width)
     data_shapes = [bf16(half, place.rows_in, LANES), f32(half, ROWS, tokens)] + [bf16(2, half * tokens, width)] * 2
@@ -549,7 +550,8 @@
     second = after(second, parts1[0])
     state, grad, through, *outs0 = finish(0, data0, parts0, [own, first, first_middle, second, second_middle], carry_shapes)
     outs1 = finish(1, data1, parts1, [state, grad, through], [])
-    homes = swap([*outs0, *outs1], [*range(1, half), *range(half + 1, count), half])
+    turns = [*range(1, half), *range(half + 1, count), half]
+    homes = swap([*outs0, *outs1], turns, turns)
 
     dx, ddt, db, dc = pl.pallas_call(
         functools.partial(unpack_kernel, place, count, copies),

time: 79.8 us -> 78.2 us (0.980)
  starting transfers between devices: 27.2 us -> 22.9 us
  waiting for transfers between devices: 28.2 us -> 31.1 us
    ppermute x14, waiting for transfers between devices: 24.1 us -> 26.1 us  [swap(): lax.ppermute(block, ('lo', 'ctx'), [(j, j ^ turn) for j in range(count)])]
    ppermute x2, starting transfers between devices: 4.42 us -> 2.72 us  [cross(): lax.ppermute(send, 'hi', [(0, 1), (1, 0)])]
    ppermute x14, starting transfers between devices: 16.1 us -> 14.6 us  [swap(): lax.ppermute(block, ('lo', 'ctx'), [(j, j ^ turn) for j in range(count)])]
    ppermute x2, starting transfers between devices: 6.73 us -> 5.6 us  [cross(): lax.ppermute(middle, ('hi', 'ctx'), pairs)]
    ppermute x2, waiting for transfers between devices: 2.46 us -> 3.48 us  [cross(): lax.ppermute(send, 'hi', [(0, 1), (1, 0)])]
  transfers between devices with their start and end apart: 18 -> 18, of which waited for: 10 -> 9; matrix products, arithmetic and copies ran while one was open for 0% -> 0% of each run, Pallas kernels for 20% -> 20%
where the time goes in v7:
time: 78.2 us; the launch traced here: 77.6 us
  waiting for transfers between devices  31.1 us (40%)
  starting transfers between devices  22.9 us (29%)
  Pallas kernels  22.5 us (29%)
  between operations  0.9 us (1%)
    ppermute x14, waiting for transfers between devices, swap(): lax.ppermute(block, ('lo', 'ctx'), [(j, j ^ turn) for j in range(count)])  26.1 us
    ppermute x14, starting transfers between devices, swap(): lax.ppermute(block, ('lo', 'ctx'), [(j, j ^ turn) for j in range(count)])  14.6 us
    pallas_call x2, Pallas kernels, middle(): pl.pallas_call(functools.partial(middle_kernel, place), in_specs=[vmem] *...  10.7 us
    ppermute x2, starting transfers between devices, cross(): lax.ppermute(middle, ('hi', 'ctx'), pairs)  5.6 us
    pallas_call x2, Pallas kernels, finish(): pl.pallas_call(functools.partial(finish_kernel, place, turn), in_specs=[v...  4.58 us
    ppermute x2, waiting for transfers between devices, cross(): lax.ppermute(send, 'hi', [(0, 1), (1, 0)])  3.48 us
    pallas_call x2, Pallas kernels, totals(): pl.pallas_call(functools.partial(totals_kernel, place, turn), in_specs=[v...  2.92 us
    pallas_call x1, Pallas kernels, on_device(): pl.pallas_call(functools.partial(pack_kernel, place, count, copies), in_s...  2.91 us
  transfers between devices with their start and end apart: 18, of which 9 were waited for; matrix products, arithmetic and copies ran while one was open for 0% of the time, Pallas kernels for 20%

profile of v7, /device:TPU:0, one launch (start us, length us, event | category | flops | bytes accessed | tf_op | source)
XLA Modules:
  0.0 77.6 jit_solution(13517233954291082494)
XLA Ops:
  0.6 2.9 %pack.1 = (bf16[1296,128]{1,0:T(8,128)(2,1)}, bf16[1296,128]{1,0:T(8,128)(2,1)}, bf16[1296,128]{1,0:T(8,128)(2,1)}, bf16[1296,128]{1,0:T(8,128)(2,1)}, bf16[1296...) custom-call(bf16[128,8,128]{2,1,0:T(8,128)(2,1)} %refs_0_.1, ...), custom_call_target="tpu_custom_call" | custom-call | tf_op jit(solution)/shard_map/pack/pallas_call | solution.py:485
  3.6 0.5 collective-permute-start
  4.1 2.7 %collective-permute-start.2 = (bf16[1296,128]{1,0:T(8,128)(2,1)}, bf16[1296,128]{1,0:T(8,128)(2,1)S(1)}, u32[]{:S(2)}, u32[]{:S(2)}) collective-permute-start(bf16[1296,128]{1,0:T(8,128)(2,1)} %get-tuple-element.63), channel_id=1, source_target_pairs={{0,5},{1,4},{2,7},{3,6},{4,1},{5,0},{6,3},{7,2},{8,13},{9,12},{10,... | collective-permute-start | bytes 995336 | tf_op jit(solution)/shard_map/ppermute | solution.py:466
  6.8 1.2 %collective-permute-start.1 = (bf16[1296,128]{1,0:T(8,128)(2,1)}, bf16[1296,128]{1,0:T(8,128)(2,1)S(1)}, u32[]{:S(2)}, u32[]{:S(2)}) collective-permute-start(bf16[1296,128]{1,0:T(8,128)(2,1)} %get-tuple-element.62), channel_id=1, source_target_pairs={{0,3},{1,2},{2,1},{3,0},{4,7},{5,6},{6,5},{7,4},{8,11},{9,10},{10,... | collective-permute-start | bytes 995336 | tf_op jit(solution)/shard_map/ppermute | solution.py:466
  8.0 2.0 %collective-permute-start.5 = (bf16[1296,128]{1,0:T(8,128)(2,1)}, bf16[1296,128]{1,0:T(8,128)(2,1)S(1)}, u32[]{:S(2)}, u32[]{:S(2)}) collective-permute-start(bf16[1296,128]{1,0:T(8,128)(2,1)} %get-tuple-element.70), channel_id=1, source_target_pairs={{0,4},{1,5},{2,6},{3,7},{4,0},{5,1},{6,2},{7,3},{8,12},{9,13},{10,... | collective-permute-start | bytes 995336 | tf_op jit(solution)/shard_map/ppermute | solution.py:466
  10.0 1.4 %collective-permute-start.6 = (bf16[1296,128]{1,0:T(8,128)(2,1)}, bf16[1296,128]{1,0:T(8,128)(2,1)S(1)}, u32[]{:S(2)}, u32[]{:S(2)}) collective-permute-start(bf16[1296,128]{1,0:T(8,128)(2,1)} %get-tuple-element.73), channel_id=1, source_target_pairs={{0,6},{1,7},{2,4},{3,5},{4,2},{5,3},{6,0},{7,1},{8,14},{9,15},{10,... | collective-permute-start | bytes 995336 | tf_op jit(solution)/shard_map/ppermute | solution.py:466
  11.4 3.8 %collective-permute-done.2.refs_2_ = bf16[1296,128]{1,0:T(8,128)(2,1)S(1)} collective-permute-done((bf16[1296,128]{1,0:T(8,128)(2,1)}, bf16[1296,128]{1,0:T(8,128)(2,1)S(1)}, u32[]{:S(2)}, u32[]{:S(2)}) %collective-permute-start.2) | collective-permute-done | bytes 331808 | tf_op jit(solution)/shard_map/ppermute | solution.py:466
  15.2 1.5 %collective-permute-start.4 = (bf16[1296,128]{1,0:T(8,128)(2,1)}, bf16[1296,128]{1,0:T(8,128)(2,1)S(1)}, u32[]{:S(2)}, u32[]{:S(2)}) collective-permute-start(bf16[1296,128]{1,0:T(8,128)(2,1)} %get-tuple-element.68), channel_id=1, source_target_pairs={{0,2},{1,3},{2,0},{3,1},{4,6},{5,7},{6,4},{7,5},{8,10},{9,11},{10,... | collective-permute-start | bytes 995336 | tf_op jit(solution)/shard_map/ppermute | solution.py:466
  16.8 0.1 exponential_negate_fusion
  16.8 6.9 %collective-permute-done.1.refs_1_ = bf16[1296,128]{1,0:T(8,128)(2,1)S(1)} collective-permute-done((bf16[1296,128]{1,0:T(8,128)(2,1)}, bf16[1296,128]{1,0:T(8,128)(2,1)S(1)}, u32[]{:S(2)}, u32[]{:S(2)}) %collective-permute-start.1) | collective-permute-done | bytes 331808 | tf_op jit(solution)/shard_map/ppermute | solution.py:466
  23.8 1.4 %totals.2 = (bf16[4,1296,128]{2,1,0:T(8,128)(2,1)S(1)}, f32[4,8,128]{2,1,0:T(8,128)S(1)}, bf16[2,512,512]{2,1,0:T(8,128)(2,1)S(1)}, bf16[2,512,512]{2,1,0:T(8,12...) custom-call(f32[8,128]{1,0:T(8,128)S(1)} %broadcast_in_dim.2.rate_re, ...), custom_call_target="tpu_custom_call" | custom-call | tf_op jit(solution)/shard_map/totals/pallas_call | solution.py:506
  25.3 2.7 %collective-permute-start.7 = (bf16[144,512]{1,0:T(8,128)(2,1)S(1)}, bf16[144,512]{1,0:T(8,128)(2,1)S(1)}, u32[]{:S(2)}, u32[]{:S(2)}) collective-permute-start(bf16[144,512]{1,0:T(8,128)(2,1)S(1)} %get-tuple-element.65), channel_id=1, source_target_pairs={{0,8},{8,0},{1,9},{9,1},{2,10},{10,2},{3,11},{11,3},{4,12},{12,4},... | collective-permute-start | bytes 442376 | tf_op jit(solution)/shard_map/ppermute | solution.py:517
  27.9 5.1 %collective-permute-done.5.refs_2_ = bf16[1296,128]{1,0:T(8,128)(2,1)S(1)} collective-permute-done((bf16[1296,128]{1,0:T(8,128)(2,1)}, bf16[1296,128]{1,0:T(8,128)(2,1)S(1)}, u32[]{:S(2)}, u32[]{:S(2)}) %collective-permute-start.5) | collective-permute-done | bytes 331808 | tf_op jit(solution)/shard_map/ppermute | solution.py:466
  33.0 4.1 %collective-permute-start.8 = (bf16[144,512]{1,0:T(8,128)(2,1)S(1)}, bf16[144,512]{1,0:T(8,128)(2,1)S(1)}, u32[]{:S(2)}, u32[]{:S(2)}) collective-permute-start(bf16[144,512]{1,0:T(8,128)(2,1)S(1)} %get-tuple-element.87), channel_id=1, source_target_pairs={{0,8},{9,1},{2,10},{11,3},{4,12},{13,5},{6,14},{15,7},{16,24},{25,... | collective-permute-start | bytes 442376 | tf_op jit(solution)/shard_map/ppermute | solution.py:517
  37.2 5.3 %middle.3 = (f32[4,128,512]{2,1,0:T(8,128)S(1)}, f32[4,8,128]{2,1,0:T(8,128)S(1)}, f32[4,128,128]{2,1,0:T(8,128)S(1)}, f32[4,128,128]{2,1,0:T(8,128)S(1)}) custom-call(f32[8,128]{1,0:T(8,128)S(1)} %broadcast_in_dim.2.rate_ref, bf16[4,1296,128]{2,1,0:T(8,128)(2,1)S(1)} %get-tuple-element.89.buf), custom_call_target="tpu_custom_call" | custom-call | flops 3000000000 | bytes 10000000 | tf_op jit(solution)/shard_map/middle/pallas_call | solution.py:528
  42.5 1.5 %totals.3 = (bf16[4,1296,128]{2,1,0:T(8,128)(2,1)S(1)}, f32[4,8,128]{2,1,0:T(8,128)S(1)}, bf16[2,512,512]{2,1,0:T(8,128)(2,1)S(1)}, bf16[2,512,512]{2,1,0:T(8,12...) custom-call(f32[8,128]{1,0:T(8,128)S(1)} %broadcast_in_dim.2.rate_ref, ...), custom_call_target="tpu_custom_call" | custom-call | tf_op jit(solution)/shard_map/totals/pallas_call | solution.py:506
  44.0 0.1 collective-permute-start.9
  44.1 1.5 %collective-permute-start.10 = (bf16[144,512]{1,0:T(8,128)(2,1)S(1)}, bf16[144,512]{1,0:T(8,128)(2,1)S(1)}, u32[]{:S(2)}, u32[]{:S(2)}) collective-permute-start(bf16[144,512]{1,0:T(8,128)(2,1)S(1)} %get-tuple-element.92), channel_id=1, source_target_pairs={{1,9},{8,0},{3,11},{10,2},{5,13},{12,4},{7,15},{14,6},{17,25},{24,... | collective-permute-start | bytes 442376 | tf_op jit(solution)/shard_map/ppermute | solution.py:517
  45.6 5.3 %middle.2 = (f32[4,128,512]{2,1,0:T(8,128)S(1)}, f32[4,8,128]{2,1,0:T(8,128)S(1)}, f32[4,128,128]{2,1,0:T(8,128)S(1)}, f32[4,128,128]{2,1,0:T(8,128)S(1)}) custom-call(f32[8,128]{1,0:T(8,128)S(1)} %broadcast_in_dim.2.rate_ref, bf16[4,1296,128]{2,1,0:T(8,128)(2,1)S(1)} %get-tuple-element.78.buf), custom_call_target="tpu_custom_call" | custom-call | flops 3000000000 | bytes 10000000 | tf_op jit(solution)/shard_map/middle/pallas_call | solution.py:528
  50.9 3.5 %collective-permute-done.9.refs_3_ = bf16[144,512]{1,0:T(8,128)(2,1)S(1)} collective-permute-done((bf16[144,512]{1,0:T(8,128)(2,1)S(1)}, bf16[144,512]{1,0:T(8,128)(2,1)S(1)}, u32[]{:S(2)}, u32[]{:S(2)}) %collective-permute-start.9) | collective-permute-done | bytes 147488 | tf_op jit(solution)/shard_map/ppermute | solution.py:517
  54.4 1.6 %collective-permute-done.10.refs_4_ = bf16[144,512]{1,0:T(8,128)(2,1)S(1)} collective-permute-done((bf16[144,512]{1,0:T(8,128)(2,1)S(1)}, bf16[144,512]{1,0:T(8,128)(2,1)S(1)}, u32[]{:S(2)}, u32[]{:S(2)}) %collective-permute-start.10) | collective-permute-done | bytes 147488 | tf_op jit(solution)/shard_map/ppermute | solution.py:517
  56.0 2.5 %finish.2 = (f32[128,512]{1,0:T(8,128)S(1)}, f32[128,512]{1,0:T(8,128)S(1)}, f32[8,512]{1,0:T(8,128)S(1)}, bf16[784,128]{1,0:T(8,128)(2,1)S(1)}, bf16[784,128]{1...) custom-call(f32[8,128]{1,0:T(8,128)S(1)} %broadcast_in_dim.2.rate_ref, ...), custom_call_target="tpu_custom_call" | custom-call | tf_op jit(solution)/shard_map/finish/pallas_call | solution.py:539
  58.5 0.7 collective-permute-start.11
  59.2 2.8 %collective-permute-start.13 = (bf16[784,128]{1,0:T(8,128)(2,1)S(1)}, bf16[784,128]{1,0:T(8,128)(2,1)S(1)}, u32[]{:S(2)}, u32[]{:S(2)}) collective-permute-start(bf16[784,128]{1,0:T(8,128)(2,1)S(1)} %get-tuple-element.96), channel_id=1, source_target_pairs={{0,6},{1,7},{2,4},{3,5},{4,2},{5,3},{6,0},{7,1},{8,14},{9,15},{10,... | collective-permute-start | bytes 602120 | tf_op jit(solution)/shard_map/ppermute | solution.py:466
  62.1 2.0 %finish.3 = (bf16[784,128]{1,0:T(8,128)(2,1)S(1)}, bf16[784,128]{1,0:T(8,128)(2,1)S(1)}, bf16[784,128]{1,0:T(8,128)(2,1)S(1)}, bf16[784,128]{1,0:T(8,128)(2,1)S(1)}) custom-call(f32[8,128]{1,0:T(8,128)S(1)} %broadcast_in_dim.2.rate_ref, bf16[4,1296,128]{2,1,0:T(8,128)(2,1)S(1)} %get-tuple-element.89.buf, f32[4,8,128]{2,1,0:T(8,128)S(1)} %get-tuple-element.97.u_rows, ...), custom_call_target="tpu_custom_call" | custom-call | tf_op jit(solution)/shard_map/finish/pallas_call | solution.py:539
  64.2 0.4 collective-permute-start.16
  64.6 1.7 %collective-permute-done.11.refs_1_ = bf16[784,128]{1,0:T(8,128)(2,1)S(1)} collective-permute-done((bf16[784,128]{1,0:T(8,128)(2,1)S(1)}, bf16[784,128]{1,0:T(8,128)(2,1)S(1)}, u32[]{:S(2)}, u32[]{:S(2)}) %collective-permute-start.11) | collective-permute-done | bytes 200736 | tf_op jit(solution)/shard_map/ppermute | solution.py:466
  66.3 1.2 %collective-permute-start.14 = (bf16[784,128]{1,0:T(8,128)(2,1)S(1)}, bf16[784,128]{1,0:T(8,128)(2,1)S(1)}, u32[]{:S(2)}, u32[]{:S(2)}) collective-permute-start(bf16[784,128]{1,0:T(8,128)(2,1)S(1)} %get-tuple-element.107), channel_id=1, source_target_pairs={{0,1},{1,0},{2,3},{3,2},{4,5},{5,4},{6,7},{7,6},{8,9},{9,8},{10,11... | collective-permute-start | bytes 602120 | tf_op jit(solution)/shard_map/ppermute | solution.py:466
  67.5 2.0 %collective-permute-done.13.refs_3_ = bf16[784,128]{1,0:T(8,128)(2,1)S(1)} collective-permute-done((bf16[784,128]{1,0:T(8,128)(2,1)S(1)}, bf16[784,128]{1,0:T(8,128)(2,1)S(1)}, u32[]{:S(2)}, u32[]{:S(2)}) %collective-permute-start.13) | collective-permute-done | bytes 200736 | tf_op jit(solution)/shard_map/ppermute | solution.py:466
  69.5 4.3 %collective-permute-done.15.refs_5_ = bf16[784,128]{1,0:T(8,128)(2,1)S(1)} collective-permute-done((bf16[784,128]{1,0:T(8,128)(2,1)S(1)}, bf16[784,128]{1,0:T(8,128)(2,1)S(1)}, u32[]{:S(2)}, u32[]{:S(2)}) %collective-permute-start.15) | collective-permute-done | bytes 200736 | tf_op jit(solution)/shard_map/ppermute | solution.py:466
  73.8 2.2 %collective-permute-done.17.refs_7_ = bf16[784,128]{1,0:T(8,128)(2,1)S(1)} collective-permute-done((bf16[784,128]{1,0:T(8,128)(2,1)S(1)}, bf16[784,128]{1,0:T(8,128)(2,1)S(1)}, u32[]{:S(2)}, u32[]{:S(2)}) %collective-permute-start.17) | collective-permute-done | bytes 200736 | tf_op jit(solution)/shard_map/ppermute | solution.py:466
  76.0 1.4 %unpack.1 = (bf16[128,4096]{1,0:T(8,128)(2,1)}, bf16[64,128]{1,0:T(8,128)(2,1)}, bf16[128,8,128]{2,1,0:T(8,128)(2,1)}, bf16[128,8,128]{2,1,0:T(8,128)(2,1)}) custom-call(bf16[784,128]{1,0:T(8,128)(2,1)S(1)} %get-tuple-element.93.refs_0_, bf16[784,128]{1,0:T(8,128)(2,1)S(1)} %collective-permute-done.11.refs_1_, ...), custom_call_target="tpu_custom_call" | custom-call | tf_op jit(solution)/shard_map/unpack/pallas_call | solution.py:556
  (18 shorter events, 0.2 us)
Async XLA Ops:
  0.6 16.1 %copy-start.1 = (f32[64]{0:T(128)S(1)}, f32[64]{0:T(128)}, u32[]{:S(2)}) copy-start(f32[64]{0:T(128)} %param.9) | copy-start | bytes 772
  3.6 6.4 %collective-permute-start = (bf16[1296,128]{1,0:T(8,128)(2,1)}, bf16[1296,128]{1,0:T(8,128)(2,1)S(1)}, u32[]{:S(2)}, u32[]{:S(2)}) collective-permute-start(bf16[1296,128]{1,0:T(8,128)(2,1)} %get-tuple-element.61), channel_id=1, source_target_pairs={{0,1},{1,0},{2,3},{3,2},{4,5},{5,4},{6,7},{7,6},{8,9},{9,8},{10,11... | collective-permute-start | bytes 995336 | tf_op jit(solution)/shard_map/ppermute | solution.py:466
  4.1 11.2 %collective-permute-start.2 = (bf16[1296,128]{1,0:T(8,128)(2,1)}, bf16[1296,128]{1,0:T(8,128)(2,1)S(1)}, u32[]{:S(2)}, u32[]{:S(2)}) collective-permute-start(bf16[1296,128]{1,0:T(8,128)(2,1)} %get-tuple-element.63), channel_id=1, source_target_pairs={{0,5},{1,4},{2,7},{3,6},{4,1},{5,0},{6,3},{7,2},{8,13},{9,12},{10,... | collective-permute-start | bytes 995336 | tf_op jit(solution)/shard_map/ppermute | solution.py:466
  6.8 17.0 %collective-permute-start.1 = (bf16[1296,128]{1,0:T(8,128)(2,1)}, bf16[1296,128]{1,0:T(8,128)(2,1)S(1)}, u32[]{:S(2)}, u32[]{:S(2)}) collective-permute-start(bf16[1296,128]{1,0:T(8,128)(2,1)} %get-tuple-element.62), channel_id=1, source_target_pairs={{0,3},{1,2},{2,1},{3,0},{4,7},{5,6},{6,5},{7,4},{8,11},{9,10},{10,... | collective-permute-start | bytes 995336 | tf_op jit(solution)/shard_map/ppermute | solution.py:466
  8.0 15.8 %collective-permute-start.3 = (bf16[1296,128]{1,0:T(8,128)(2,1)}, bf16[1296,128]{1,0:T(8,128)(2,1)S(1)}, u32[]{:S(2)}, u32[]{:S(2)}) collective-permute-start(bf16[1296,128]{1,0:T(8,128)(2,1)} %get-tuple-element.64), channel_id=1, source_target_pairs={{0,7},{1,6},{2,5},{3,4},{4,3},{5,2},{6,1},{7,0},{8,15},{9,14},{10,... | collective-permute-start | bytes 995336 | tf_op jit(solution)/shard_map/ppermute | solution.py:466
  8.0 25.0 %collective-permute-start.5 = (bf16[1296,128]{1,0:T(8,128)(2,1)}, bf16[1296,128]{1,0:T(8,128)(2,1)S(1)}, u32[]{:S(2)}, u32[]{:S(2)}) collective-permute-start(bf16[1296,128]{1,0:T(8,128)(2,1)} %get-tuple-element.70), channel_id=1, source_target_pairs={{0,4},{1,5},{2,6},{3,7},{4,0},{5,1},{6,2},{7,3},{8,12},{9,13},{10,... | collective-permute-start | bytes 995336 | tf_op jit(solution)/shard_map/ppermute | solution.py:466
  10.0 32.5 %collective-permute-start.6 = (bf16[1296,128]{1,0:T(8,128)(2,1)}, bf16[1296,128]{1,0:T(8,128)(2,1)S(1)}, u32[]{:S(2)}, u32[]{:S(2)}) collective-permute-start(bf16[1296,128]{1,0:T(8,128)(2,1)} %get-tuple-element.73), channel_id=1, source_target_pairs={{0,6},{1,7},{2,4},{3,5},{4,2},{5,3},{6,0},{7,1},{8,14},{9,15},{10,... | collective-permute-start | bytes 995336 | tf_op jit(solution)/shard_map/ppermute | solution.py:466
  15.2 27.3 %collective-permute-start.4 = (bf16[1296,128]{1,0:T(8,128)(2,1)}, bf16[1296,128]{1,0:T(8,128)(2,1)S(1)}, u32[]{:S(2)}, u32[]{:S(2)}) collective-permute-start(bf16[1296,128]{1,0:T(8,128)(2,1)} %get-tuple-element.68), channel_id=1, source_target_pairs={{0,2},{1,3},{2,0},{3,1},{4,6},{5,7},{6,4},{7,5},{8,10},{9,11},{10,... | collective-permute-start | bytes 995336 | tf_op jit(solution)/shard_map/ppermute | solution.py:466
  25.3 29.1 %collective-permute-start.7 = (bf16[144,512]{1,0:T(8,128)(2,1)S(1)}, bf16[144,512]{1,0:T(8,128)(2,1)S(1)}, u32[]{:S(2)}, u32[]{:S(2)}) collective-permute-start(bf16[144,512]{1,0:T(8,128)(2,1)S(1)} %get-tuple-element.65), channel_id=1, source_target_pairs={{0,8},{8,0},{1,9},{9,1},{2,10},{10,2},{3,11},{11,3},{4,12},{12,4},... | collective-permute-start | bytes 442376 | tf_op jit(solution)/shard_map/ppermute | solution.py:517
  33.0 21.4 %collective-permute-start.8 = (bf16[144,512]{1,0:T(8,128)(2,1)S(1)}, bf16[144,512]{1,0:T(8,128)(2,1)S(1)}, u32[]{:S(2)}, u32[]{:S(2)}) collective-permute-start(bf16[144,512]{1,0:T(8,128)(2,1)S(1)} %get-tuple-element.87), channel_id=1, source_target_pairs={{0,8},{9,1},{2,10},{11,3},{4,12},{13,5},{6,14},{15,7},{16,24},{25,... | collective-permute-start | bytes 442376 | tf_op jit(solution)/shard_map/ppermute | solution.py:517
  37.2 5.4 %copy-start = (bf16[1296,128]{1,0:T(8,128)(2,1)S(1)}, bf16[1296,128]{1,0:T(8,128)(2,1)}, u32[]{:S(2)}) copy-start(bf16[1296,128]{1,0:T(8,128)(2,1)} %get-tuple-element.66.refs_0_) | copy-start | bytes 995332
  44.0 10.4 %collective-permute-start.9 = (bf16[144,512]{1,0:T(8,128)(2,1)S(1)}, bf16[144,512]{1,0:T(8,128)(2,1)S(1)}, u32[]{:S(2)}, u32[]{:S(2)}) collective-permute-start(bf16[144,512]{1,0:T(8,128)(2,1)S(1)} %get-tuple-element.88), channel_id=1, source_target_pairs={{0,8},{8,0},{1,9},{9,1},{2,10},{10,2},{3,11},{11,3},{4,12},{12,4},... | collective-permute-start | bytes 442376 | tf_op jit(solution)/shard_map/ppermute | solution.py:517
  44.1 11.9 %collective-permute-start.10 = (bf16[144,512]{1,0:T(8,128)(2,1)S(1)}, bf16[144,512]{1,0:T(8,128)(2,1)S(1)}, u32[]{:S(2)}, u32[]{:S(2)}) collective-permute-start(bf16[144,512]{1,0:T(8,128)(2,1)S(1)} %get-tuple-element.92), channel_id=1, source_target_pairs={{1,9},{8,0},{3,11},{10,2},{5,13},{12,4},{7,15},{14,6},{17,25},{24,... | collective-permute-start | bytes 442376 | tf_op jit(solution)/shard_map/ppermute | solution.py:517
  58.5 7.8 %collective-permute-start.11 = (bf16[784,128]{1,0:T(8,128)(2,1)S(1)}, bf16[784,128]{1,0:T(8,128)(2,1)S(1)}, u32[]{:S(2)}, u32[]{:S(2)}) collective-permute-start(bf16[784,128]{1,0:T(8,128)(2,1)S(1)} %get-tuple-element.94), channel_id=1, source_target_pairs={{0,2},{1,3},{2,0},{3,1},{4,6},{5,7},{6,4},{7,5},{8,10},{9,11},{10,... | collective-permute-start | bytes 602120 | tf_op jit(solution)/shard_map/ppermute | solution.py:466
  59.2 7.1 %collective-permute-start.12 = (bf16[784,128]{1,0:T(8,128)(2,1)S(1)}, bf16[784,128]{1,0:T(8,128)(2,1)S(1)}, u32[]{:S(2)}, u32[]{:S(2)}) collective-permute-start(bf16[784,128]{1,0:T(8,128)(2,1)S(1)} %get-tuple-element.95), channel_id=1, source_target_pairs={{0,4},{1,5},{2,6},{3,7},{4,0},{5,1},{6,2},{7,3},{8,12},{9,13},{10,... | collective-permute-start | bytes 602120 | tf_op jit(solution)/shard_map/ppermute | solution.py:466
  59.2 10.3 %collective-permute-start.13 = (bf16[784,128]{1,0:T(8,128)(2,1)S(1)}, bf16[784,128]{1,0:T(8,128)(2,1)S(1)}, u32[]{:S(2)}, u32[]{:S(2)}) collective-permute-start(bf16[784,128]{1,0:T(8,128)(2,1)S(1)} %get-tuple-element.96), channel_id=1, source_target_pairs={{0,6},{1,7},{2,4},{3,5},{4,2},{5,3},{6,0},{7,1},{8,14},{9,15},{10,... | collective-permute-start | bytes 602120 | tf_op jit(solution)/shard_map/ppermute | solution.py:466
  64.1 9.7 %collective-permute-start.15 = (bf16[784,128]{1,0:T(8,128)(2,1)S(1)}, bf16[784,128]{1,0:T(8,128)(2,1)S(1)}, u32[]{:S(2)}, u32[]{:S(2)}) collective-permute-start(bf16[784,128]{1,0:T(8,128)(2,1)S(1)} %get-tuple-element.108), channel_id=1, source_target_pairs={{0,3},{1,2},{2,1},{3,0},{4,7},{5,6},{6,5},{7,4},{8,11},{9,10},{10,... | collective-permute-start | bytes 602120 | tf_op jit(solution)/shard_map/ppermute | solution.py:466
  64.2 9.6 %collective-permute-start.16 = (bf16[784,128]{1,0:T(8,128)(2,1)S(1)}, bf16[784,128]{1,0:T(8,128)(2,1)S(1)}, u32[]{:S(2)}, u32[]{:S(2)}) collective-permute-start(bf16[784,128]{1,0:T(8,128)(2,1)S(1)} %get-tuple-element.109), channel_id=1, source_target_pairs={{0,5},{1,4},{2,7},{3,6},{4,1},{5,0},{6,3},{7,2},{8,13},{9,12},{10,... | collective-permute-start | bytes 602120 | tf_op jit(solution)/shard_map/ppermute | solution.py:466
  66.3 9.7 %collective-permute-start.17 = (bf16[784,128]{1,0:T(8,128)(2,1)S(1)}, bf16[784,128]{1,0:T(8,128)(2,1)S(1)}, u32[]{:S(2)}, u32[]{:S(2)}) collective-permute-start(bf16[784,128]{1,0:T(8,128)(2,1)S(1)} %get-tuple-element.111), channel_id=1, source_target_pairs={{0,7},{1,6},{2,5},{3,4},{4,3},{5,2},{6,1},{7,0},{8,15},{9,14},{10,... | collective-permute-start | bytes 602120 | tf_op jit(solution)/shard_map/ppermute | solution.py:466
  66.3 9.7 %collective-permute-start.14 = (bf16[784,128]{1,0:T(8,128)(2,1)S(1)}, bf16[784,128]{1,0:T(8,128)(2,1)S(1)}, u32[]{:S(2)}, u32[]{:S(2)}) collective-permute-start(bf16[784,128]{1,0:T(8,128)(2,1)S(1)} %get-tuple-element.107), channel_id=1, source_target_pairs={{0,1},{1,0},{2,3},{3,2},{4,5},{5,4},{6,7},{7,6},{8,9},{9,8},{10,11... | collective-permute-start | bytes 602120 | tf_op jit(solution)/shard_map/ppermute | solution.py:466

commit v8 on v7

--- a/solution.py
+++ b/solution.py
@@ -228,7 +228,7 @@
 
 def decode(code, scale):
     code = code.astype(F32)
-    size = (jnp.log(jnp.abs(code)) * LOG2E + CODE_SPAN / 2) * (scale / CODE_SPAN)
+    size = jnp.log(jnp.abs(code)) * (scale * (LOG2E / CODE_SPAN)) + scale / 2
     return jnp.where(code < 0.0, -size, size)
 
 
@@ -244,7 +244,7 @@
 def totals_kernel(place, turn, rate_ref, *refs):
     blocks, refs = refs[: place.half], refs[place.half :]
     others, refs = ([], refs) if turn else (refs[:3], refs[3:])
-    buf, u_rows, u_parts, v_parts, *refs = refs
+    buf, u_rows, v_rows, u_parts, v_parts, *refs = refs
     width, tokens = place.width, place.tokens
     for k, block in enumerate(blocks):
         lo = lax.axis_index("lo") ^ k
@@ -258,7 +258,8 @@
         rows = slice(i * tokens, (i + 1) * tokens)
         hi, lo = split2(spread_rows(u_rows[i], width) * cat(place.x(chunk), 1).astype(F32))
         u_parts[0, rows], u_parts[1, rows] = hi, lo
-        start_wide = spread_rows(jnp.exp(starts[i]), width)
+        v_rows[i] = jnp.exp(starts[i])
+        start_wide = spread_rows(v_rows[i], width)
         hi, lo = split2(start_wide * cat(place.dy(chunk), 1).astype(F32))
         v_parts[0, rows], v_parts[1, rows] = hi, lo
     b_turned = jnp.transpose(cat([place.b(chunk) for chunk in chunks], 0).astype(F32)).astype(BF16)
@@ -392,7 +393,7 @@
     return [[jnp.where(here == 0, pair[0], pair[1]) for pair in (states, grads, logs)] for here in (seg, 1 - seg)]
 
 
-def finish_kernel(place, turn, rate_ref, buf, u_rows, u_parts, v_parts, dx_in, ddt_in, db_in, dc_in, *refs):
+def finish_kernel(place, turn, rate_ref, buf, u_rows, v_rows, u_parts, v_parts, dx_in, ddt_in, db_in, dc_in, *refs):
     rate, tokens, width = rate_ref[...], place.tokens, place.width
     if turn == 0:
         got, refs = refs[:5], refs[5:]
@@ -410,9 +411,8 @@
     b_all, c_all = cat([place.b(chunk) for chunk in chunks], 0), cat([place.c(chunk) for chunk in chunks], 0)
     b_grad = dot(cat([b_all, b_all], 1), cat([g_hi, g_lo], 0))
     c_state = dot(cat([c_all, c_all], 1), cat([s_hi, s_lo], 0))
-    v_hi, v_lo = v_parts[0], v_parts[1]
     db = head_products((u_parts[0], u_parts[1]), (g_hi, g_lo))
-    dc = head_products((v_hi, v_lo), (s_hi, s_lo))
+    dc = head_products((v_parts[0], v_parts[1]), (s_hi, s_lo))
     ins = []
     for i, chunk in enumerate(chunks):
         rows = slice(i * tokens, (i + 1) * tokens)
@@ -425,8 +425,9 @@
         out[i, first : first + tokens, :] = (db_in[i] + db[rows]).astype(BF16)
         out[i, first + tokens : first + 2 * tokens, :] = (dc_in[i] + dc[rows]).astype(BF16)
     ins = head_sums(cat(ins, 0), width)
-    laters = head_sums((v_hi.astype(F32) + v_lo.astype(F32)) * c_state, width)
+    laters = head_sums(cat([cat(place.dy(chunk), 1) for chunk in chunks], 0).astype(F32) * c_state, width)
     ins, laters = ([sums[:, i * tokens : (i + 1) * tokens] for i in range(place.half)] for sums in (ins, laters))
+    laters = [v_rows[i] * later for i, later in enumerate(laters)]
     over = cumulate(cat([one - other for one, other in zip(ins, laters)], 0), True)
     rest = corner
     for later in laters:
@@ -499,14 +500,14 @@
     arrived = swap(sent, [*other_turns[:3], half, *other_turns[3:], *own_turns], [half, *other_turns, *own_turns])
 
     owned, coded = (2 * STATE + 2 * ROWS, width), (STATE + TILE, width)
-    data_shapes = [bf16(half, place.rows_in, LANES), f32(half, ROWS, tokens)] + [bf16(2, half * tokens, width)] * 2
+    data_shapes = [bf16(half, place.rows_in, LANES)] + [f32(half, ROWS, tokens)] * 2 + [bf16(2, half * tokens, width)] * 2
     carry_shapes = [f32(STATE, width), f32(STATE, width), f32(ROWS, width)]
 
     def totals(turn, blocks, others, shapes):
         return pl.pallas_call(
             functools.partial(totals_kernel, place, turn),
             in_specs=[vmem] * (1 + half + len(others)),
-            out_specs=[vmem] * (4 + len(shapes)),
+            out_specs=[vmem] * (5 + len(shapes)),
             out_shape=data_shapes + shapes,
             compiler_params=params,
             name="totals",
@@ -538,7 +539,7 @@
     def finish(turn, data, parts, others, shapes):
         return pl.pallas_call(
             functools.partial(finish_kernel, place, turn),
-            in_specs=[vmem] * (9 + len(others)),
+            in_specs=[vmem] * (10 + len(others)),
             out_specs=[vmem] * (half + len(shapes)),
             out_shape=shapes + [bf16(place.rows_out, LANES)] * half,
             scratch_shapes=[pltpu.VMEM((half, place.rows_out, LANES), BF16)],

time: 78.2 us -> 78.1 us (level)
  no operation moved by 1% of the time
where the time goes in v8:
time: 78.1 us; the launch traced here: 77.4 us
  waiting for transfers between devices  31.2 us (40%)
  starting transfers between devices  22.9 us (29%)
  Pallas kernels  22.3 us (29%)
  between operations  0.9 us (1%)
    ppermute x14, waiting for transfers between devices, swap(): lax.ppermute(block, ('lo', 'ctx'), [(j, j ^ turn) for j in range(count)])  26.1 us
    ppermute x14, starting transfers between devices, swap(): lax.ppermute(block, ('lo', 'ctx'), [(j, j ^ turn) for j in range(count)])  14.6 us
    pallas_call x2, Pallas kernels, middle(): pl.pallas_call(functools.partial(middle_kernel, place), in_specs=[vmem] *...  10.7 us
    ppermute x2, starting transfers between devices, cross(): lax.ppermute(middle, ('hi', 'ctx'), pairs)  5.6 us
    pallas_call x2, Pallas kernels, finish(): pl.pallas_call(functools.partial(finish_kernel, place, turn), in_specs=[v...  4.44 us
    ppermute x2, waiting for transfers between devices, cross(): lax.ppermute(send, 'hi', [(0, 1), (1, 0)])  3.48 us
    pallas_call x2, Pallas kernels, totals(): pl.pallas_call(functools.partial(totals_kernel, place, turn), in_specs=[v...  2.91 us
    pallas_call x1, Pallas kernels, on_device(): pl.pallas_call(functools.partial(pack_kernel, place, count, copies), in_s...  2.91 us
  transfers between devices with their start and end apart: 18, of which 9 were waited for; matrix products, arithmetic and copies ran while one was open for 0% of the time, Pallas kernels for 20%

profile of v8, /device:TPU:0, one launch (start us, length us, event | category | flops | bytes accessed | tf_op | source)
XLA Modules:
  0.0 77.4 jit_solution(13702480971493148460)
XLA Ops:
  0.6 2.9 %pack.1 = (bf16[1296,128]{1,0:T(8,128)(2,1)}, bf16[1296,128]{1,0:T(8,128)(2,1)}, bf16[1296,128]{1,0:T(8,128)(2,1)}, bf16[1296,128]{1,0:T(8,128)(2,1)}, bf16[1296...) custom-call(bf16[128,8,128]{2,1,0:T(8,128)(2,1)} %refs_0_.1, ...), custom_call_target="tpu_custom_call" | custom-call | tf_op jit(solution)/shard_map/pack/pallas_call | solution.py:486
  3.6 0.5 collective-permute-start
  4.1 2.7 %collective-permute-start.2 = (bf16[1296,128]{1,0:T(8,128)(2,1)}, bf16[1296,128]{1,0:T(8,128)(2,1)S(1)}, u32[]{:S(2)}, u32[]{:S(2)}) collective-permute-start(bf16[1296,128]{1,0:T(8,128)(2,1)} %get-tuple-element.65), channel_id=1, source_target_pairs={{0,5},{1,4},{2,7},{3,6},{4,1},{5,0},{6,3},{7,2},{8,13},{9,12},{10,... | collective-permute-start | bytes 995336 | tf_op jit(solution)/shard_map/ppermute | solution.py:467
  6.8 1.2 %collective-permute-start.1 = (bf16[1296,128]{1,0:T(8,128)(2,1)}, bf16[1296,128]{1,0:T(8,128)(2,1)S(1)}, u32[]{:S(2)}, u32[]{:S(2)}) collective-permute-start(bf16[1296,128]{1,0:T(8,128)(2,1)} %get-tuple-element.64), channel_id=1, source_target_pairs={{0,3},{1,2},{2,1},{3,0},{4,7},{5,6},{6,5},{7,4},{8,11},{9,10},{10,... | collective-permute-start | bytes 995336 | tf_op jit(solution)/shard_map/ppermute | solution.py:467
  8.0 2.0 %collective-permute-start.5 = (bf16[1296,128]{1,0:T(8,128)(2,1)}, bf16[1296,128]{1,0:T(8,128)(2,1)S(1)}, u32[]{:S(2)}, u32[]{:S(2)}) collective-permute-start(bf16[1296,128]{1,0:T(8,128)(2,1)} %get-tuple-element.72), channel_id=1, source_target_pairs={{0,4},{1,5},{2,6},{3,7},{4,0},{5,1},{6,2},{7,3},{8,12},{9,13},{10,... | collective-permute-start | bytes 995336 | tf_op jit(solution)/shard_map/ppermute | solution.py:467
  10.0 1.4 %collective-permute-start.6 = (bf16[1296,128]{1,0:T(8,128)(2,1)}, bf16[1296,128]{1,0:T(8,128)(2,1)S(1)}, u32[]{:S(2)}, u32[]{:S(2)}) collective-permute-start(bf16[1296,128]{1,0:T(8,128)(2,1)} %get-tuple-element.75), channel_id=1, source_target_pairs={{0,6},{1,7},{2,4},{3,5},{4,2},{5,3},{6,0},{7,1},{8,14},{9,15},{10,... | collective-permute-start | bytes 995336 | tf_op jit(solution)/shard_map/ppermute | solution.py:467
  11.4 3.8 %collective-permute-done.2.refs_2_ = bf16[1296,128]{1,0:T(8,128)(2,1)S(1)} collective-permute-done((bf16[1296,128]{1,0:T(8,128)(2,1)}, bf16[1296,128]{1,0:T(8,128)(2,1)S(1)}, u32[]{:S(2)}, u32[]{:S(2)}) %collective-permute-start.2) | collective-permute-done | bytes 331808 | tf_op jit(solution)/shard_map/ppermute | solution.py:467
  15.2 1.5 %collective-permute-start.4 = (bf16[1296,128]{1,0:T(8,128)(2,1)}, bf16[1296,128]{1,0:T(8,128)(2,1)S(1)}, u32[]{:S(2)}, u32[]{:S(2)}) collective-permute-start(bf16[1296,128]{1,0:T(8,128)(2,1)} %get-tuple-element.70), channel_id=1, source_target_pairs={{0,2},{1,3},{2,0},{3,1},{4,6},{5,7},{6,4},{7,5},{8,10},{9,11},{10,... | collective-permute-start | bytes 995336 | tf_op jit(solution)/shard_map/ppermute | solution.py:467
  16.8 0.1 exponential_negate_fusion
  16.8 6.9 %collective-permute-done.1.refs_1_ = bf16[1296,128]{1,0:T(8,128)(2,1)S(1)} collective-permute-done((bf16[1296,128]{1,0:T(8,128)(2,1)}, bf16[1296,128]{1,0:T(8,128)(2,1)S(1)}, u32[]{:S(2)}, u32[]{:S(2)}) %collective-permute-start.1) | collective-permute-done | bytes 331808 | tf_op jit(solution)/shard_map/ppermute | solution.py:467
  23.8 1.4 %totals.2 = (bf16[4,1296,128]{2,1,0:T(8,128)(2,1)S(1)}, f32[4,8,128]{2,1,0:T(8,128)S(1)}, f32[4,8,128]{2,1,0:T(8,128)S(1)}, bf16[2,512,512]{2,1,0:T(8,128)(2,1)S...) custom-call(f32[8,128]{1,0:T(8,128)S(1)} %broadcast_in_dim.2.rate_re, ...), custom_call_target="tpu_custom_call" | custom-call | tf_op jit(solution)/shard_map/totals/pallas_call | solution.py:507
  25.3 2.7 %collective-permute-start.7 = (bf16[144,512]{1,0:T(8,128)(2,1)S(1)}, bf16[144,512]{1,0:T(8,128)(2,1)S(1)}, u32[]{:S(2)}, u32[]{:S(2)}) collective-permute-start(bf16[144,512]{1,0:T(8,128)(2,1)S(1)} %get-tuple-element.67), channel_id=1, source_target_pairs={{0,8},{8,0},{1,9},{9,1},{2,10},{10,2},{3,11},{11,3},{4,12},{12,4},... | collective-permute-start | bytes 442376 | tf_op jit(solution)/shard_map/ppermute | solution.py:518
  27.9 5.1 %collective-permute-done.5.refs_2_ = bf16[1296,128]{1,0:T(8,128)(2,1)S(1)} collective-permute-done((bf16[1296,128]{1,0:T(8,128)(2,1)}, bf16[1296,128]{1,0:T(8,128)(2,1)S(1)}, u32[]{:S(2)}, u32[]{:S(2)}) %collective-permute-start.5) | collective-permute-done | bytes 331808 | tf_op jit(solution)/shard_map/ppermute | solution.py:467
  33.0 4.1 %collective-permute-start.8 = (bf16[144,512]{1,0:T(8,128)(2,1)S(1)}, bf16[144,512]{1,0:T(8,128)(2,1)S(1)}, u32[]{:S(2)}, u32[]{:S(2)}) collective-permute-start(bf16[144,512]{1,0:T(8,128)(2,1)S(1)} %get-tuple-element.90), channel_id=1, source_target_pairs={{0,8},{9,1},{2,10},{11,3},{4,12},{13,5},{6,14},{15,7},{16,24},{25,... | collective-permute-start | bytes 442376 | tf_op jit(solution)/shard_map/ppermute | solution.py:518
  37.2 5.3 %middle.3 = (f32[4,128,512]{2,1,0:T(8,128)S(1)}, f32[4,8,128]{2,1,0:T(8,128)S(1)}, f32[4,128,128]{2,1,0:T(8,128)S(1)}, f32[4,128,128]{2,1,0:T(8,128)S(1)}) custom-call(f32[8,128]{1,0:T(8,128)S(1)} %broadcast_in_dim.2.rate_ref, bf16[4,1296,128]{2,1,0:T(8,128)(2,1)S(1)} %get-tuple-element.92.buf), custom_call_target="tpu_custom_call" | custom-call | flops 3000000000 | bytes 10000000 | tf_op jit(solution)/shard_map/middle/pallas_call | solution.py:529
  42.5 1.5 %totals.3 = (bf16[4,1296,128]{2,1,0:T(8,128)(2,1)S(1)}, f32[4,8,128]{2,1,0:T(8,128)S(1)}, f32[4,8,128]{2,1,0:T(8,128)S(1)}, bf16[2,512,512]{2,1,0:T(8,128)(2,1)S...) custom-call(f32[8,128]{1,0:T(8,128)S(1)} %broadcast_in_dim.2.rate_re, ...), custom_call_target="tpu_custom_call" | custom-call | tf_op jit(solution)/shard_map/totals/pallas_call | solution.py:507
  44.0 0.1 collective-permute-start.9
  44.1 1.5 %collective-permute-start.10 = (bf16[144,512]{1,0:T(8,128)(2,1)S(1)}, bf16[144,512]{1,0:T(8,128)(2,1)S(1)}, u32[]{:S(2)}, u32[]{:S(2)}) collective-permute-start(bf16[144,512]{1,0:T(8,128)(2,1)S(1)} %get-tuple-element.95), channel_id=1, source_target_pairs={{1,9},{8,0},{3,11},{10,2},{5,13},{12,4},{7,15},{14,6},{17,25},{24,... | collective-permute-start | bytes 442376 | tf_op jit(solution)/shard_map/ppermute | solution.py:518
  45.6 5.3 %middle.2 = (f32[4,128,512]{2,1,0:T(8,128)S(1)}, f32[4,8,128]{2,1,0:T(8,128)S(1)}, f32[4,128,128]{2,1,0:T(8,128)S(1)}, f32[4,128,128]{2,1,0:T(8,128)S(1)}) custom-call(f32[8,128]{1,0:T(8,128)S(1)} %broadcast_in_dim.2.rate_ref, bf16[4,1296,128]{2,1,0:T(8,128)(2,1)S(1)} %get-tuple-element.80.buf), custom_call_target="tpu_custom_call" | custom-call | flops 3000000000 | bytes 10000000 | tf_op jit(solution)/shard_map/middle/pallas_call | solution.py:529
  50.9 3.5 %collective-permute-done.9.refs_3_ = bf16[144,512]{1,0:T(8,128)(2,1)S(1)} collective-permute-done((bf16[144,512]{1,0:T(8,128)(2,1)S(1)}, bf16[144,512]{1,0:T(8,128)(2,1)S(1)}, u32[]{:S(2)}, u32[]{:S(2)}) %collective-permute-start.9) | collective-permute-done | bytes 147488 | tf_op jit(solution)/shard_map/ppermute | solution.py:518
  54.4 1.6 %collective-permute-done.10.refs_4_ = bf16[144,512]{1,0:T(8,128)(2,1)S(1)} collective-permute-done((bf16[144,512]{1,0:T(8,128)(2,1)S(1)}, bf16[144,512]{1,0:T(8,128)(2,1)S(1)}, u32[]{:S(2)}, u32[]{:S(2)}) %collective-permute-start.10) | collective-permute-done | bytes 147488 | tf_op jit(solution)/shard_map/ppermute | solution.py:518
  56.0 2.4 %finish.2 = (f32[128,512]{1,0:T(8,128)S(1)}, f32[128,512]{1,0:T(8,128)S(1)}, f32[8,512]{1,0:T(8,128)S(1)}, bf16[784,128]{1,0:T(8,128)(2,1)S(1)}, bf16[784,128]{1...) custom-call(f32[8,128]{1,0:T(8,128)S(1)} %broadcast_in_dim.2.rate_ref, ...), custom_call_target="tpu_custom_call" | custom-call | tf_op jit(solution)/shard_map/finish/pallas_call | solution.py:540
  58.4 0.7 collective-permute-start.11
  59.1 2.8 %collective-permute-start.13 = (bf16[784,128]{1,0:T(8,128)(2,1)S(1)}, bf16[784,128]{1,0:T(8,128)(2,1)S(1)}, u32[]{:S(2)}, u32[]{:S(2)}) collective-permute-start(bf16[784,128]{1,0:T(8,128)(2,1)S(1)} %get-tuple-element.99), channel_id=1, source_target_pairs={{0,6},{1,7},{2,4},{3,5},{4,2},{5,3},{6,0},{7,1},{8,14},{9,15},{10,... | collective-permute-start | bytes 602120 | tf_op jit(solution)/shard_map/ppermute | solution.py:467
  62.0 2.0 %finish.3 = (bf16[784,128]{1,0:T(8,128)(2,1)S(1)}, bf16[784,128]{1,0:T(8,128)(2,1)S(1)}, bf16[784,128]{1,0:T(8,128)(2,1)S(1)}, bf16[784,128]{1,0:T(8,128)(2,1)S(1)}) custom-call(f32[8,128]{1,0:T(8,128)S(1)} %broadcast_in_dim.2.rate_ref, bf16[4,1296,128]{2,1,0:T(8,128)(2,1)S(1)} %get-tuple-element.92.buf, f32[4,8,128]{2,1,0:T(8,128)S(1)} %get-tuple-element.100.u_rows, ...), custom_call_target="tpu_custom_call" | custom-call | tf_op jit(solution)/shard_map/finish/pallas_call | solution.py:540
  64.1 0.4 collective-permute-start.16
  64.5 1.7 %collective-permute-done.11.refs_1_ = bf16[784,128]{1,0:T(8,128)(2,1)S(1)} collective-permute-done((bf16[784,128]{1,0:T(8,128)(2,1)S(1)}, bf16[784,128]{1,0:T(8,128)(2,1)S(1)}, u32[]{:S(2)}, u32[]{:S(2)}) %collective-permute-start.11) | collective-permute-done | bytes 200736 | tf_op jit(solution)/shard_map/ppermute | solution.py:467
  66.2 1.2 %collective-permute-start.14 = (bf16[784,128]{1,0:T(8,128)(2,1)S(1)}, bf16[784,128]{1,0:T(8,128)(2,1)S(1)}, u32[]{:S(2)}, u32[]{:S(2)}) collective-permute-start(bf16[784,128]{1,0:T(8,128)(2,1)S(1)} %get-tuple-element.111), channel_id=1, source_target_pairs={{0,1},{1,0},{2,3},{3,2},{4,5},{5,4},{6,7},{7,6},{8,9},{9,8},{10,11... | collective-permute-start | bytes 602120 | tf_op jit(solution)/shard_map/ppermute | solution.py:467
  67.4 2.1 %collective-permute-done.13.refs_3_ = bf16[784,128]{1,0:T(8,128)(2,1)S(1)} collective-permute-done((bf16[784,128]{1,0:T(8,128)(2,1)S(1)}, bf16[784,128]{1,0:T(8,128)(2,1)S(1)}, u32[]{:S(2)}, u32[]{:S(2)}) %collective-permute-start.13) | collective-permute-done | bytes 200736 | tf_op jit(solution)/shard_map/ppermute | solution.py:467
  69.4 4.3 %collective-permute-done.15.refs_5_ = bf16[784,128]{1,0:T(8,128)(2,1)S(1)} collective-permute-done((bf16[784,128]{1,0:T(8,128)(2,1)S(1)}, bf16[784,128]{1,0:T(8,128)(2,1)S(1)}, u32[]{:S(2)}, u32[]{:S(2)}) %collective-permute-start.15) | collective-permute-done | bytes 200736 | tf_op jit(solution)/shard_map/ppermute | solution.py:467
  73.7 2.1 %collective-permute-done.17.refs_7_ = bf16[784,128]{1,0:T(8,128)(2,1)S(1)} collective-permute-done((bf16[784,128]{1,0:T(8,128)(2,1)S(1)}, bf16[784,128]{1,0:T(8,128)(2,1)S(1)}, u32[]{:S(2)}, u32[]{:S(2)}) %collective-permute-start.17) | collective-permute-done | bytes 200736 | tf_op jit(solution)/shard_map/ppermute | solution.py:467
  75.9 1.4 %unpack.1 = (bf16[128,4096]{1,0:T(8,128)(2,1)}, bf16[64,128]{1,0:T(8,128)(2,1)}, bf16[128,8,128]{2,1,0:T(8,128)(2,1)}, bf16[128,8,128]{2,1,0:T(8,128)(2,1)}) custom-call(bf16[784,128]{1,0:T(8,128)(2,1)S(1)} %get-tuple-element.96.refs_0_, bf16[784,128]{1,0:T(8,128)(2,1)S(1)} %collective-permute-done.11.refs_1_, ...), custom_call_target="tpu_custom_call" | custom-call | tf_op jit(solution)/shard_map/unpack/pallas_call | solution.py:557
  (18 shorter events, 0.2 us)
Async XLA Ops:
  0.6 16.1 %copy-start.1 = (f32[64]{0:T(128)S(1)}, f32[64]{0:T(128)}, u32[]{:S(2)}) copy-start(f32[64]{0:T(128)} %param.9) | copy-start | bytes 772
  3.6 6.4 %collective-permute-start = (bf16[1296,128]{1,0:T(8,128)(2,1)}, bf16[1296,128]{1,0:T(8,128)(2,1)S(1)}, u32[]{:S(2)}, u32[]{:S(2)}) collective-permute-start(bf16[1296,128]{1,0:T(8,128)(2,1)} %get-tuple-element.63), channel_id=1, source_target_pairs={{0,1},{1,0},{2,3},{3,2},{4,5},{5,4},{6,7},{7,6},{8,9},{9,8},{10,11... | collective-permute-start | bytes 995336 | tf_op jit(solution)/shard_map/ppermute | solution.py:467
  4.1 11.2 %collective-permute-start.2 = (bf16[1296,128]{1,0:T(8,128)(2,1)}, bf16[1296,128]{1,0:T(8,128)(2,1)S(1)}, u32[]{:S(2)}, u32[]{:S(2)}) collective-permute-start(bf16[1296,128]{1,0:T(8,128)(2,1)} %get-tuple-element.65), channel_id=1, source_target_pairs={{0,5},{1,4},{2,7},{3,6},{4,1},{5,0},{6,3},{7,2},{8,13},{9,12},{10,... | collective-permute-start | bytes 995336 | tf_op jit(solution)/shard_map/ppermute | solution.py:467
  6.8 17.0 %collective-permute-start.1 = (bf16[1296,128]{1,0:T(8,128)(2,1)}, bf16[1296,128]{1,0:T(8,128)(2,1)S(1)}, u32[]{:S(2)}, u32[]{:S(2)}) collective-permute-start(bf16[1296,128]{1,0:T(8,128)(2,1)} %get-tuple-element.64), channel_id=1, source_target_pairs={{0,3},{1,2},{2,1},{3,0},{4,7},{5,6},{6,5},{7,4},{8,11},{9,10},{10,... | collective-permute-start | bytes 995336 | tf_op jit(solution)/shard_map/ppermute | solution.py:467
  8.0 15.8 %collective-permute-start.3 = (bf16[1296,128]{1,0:T(8,128)(2,1)}, bf16[1296,128]{1,0:T(8,128)(2,1)S(1)}, u32[]{:S(2)}, u32[]{:S(2)}) collective-permute-start(bf16[1296,128]{1,0:T(8,128)(2,1)} %get-tuple-element.66), channel_id=1, source_target_pairs={{0,7},{1,6},{2,5},{3,4},{4,3},{5,2},{6,1},{7,0},{8,15},{9,14},{10,... | collective-permute-start | bytes 995336 | tf_op jit(solution)/shard_map/ppermute | solution.py:467
  8.0 25.0 %collective-permute-start.5 = (bf16[1296,128]{1,0:T(8,128)(2,1)}, bf16[1296,128]{1,0:T(8,128)(2,1)S(1)}, u32[]{:S(2)}, u32[]{:S(2)}) collective-permute-start(bf16[1296,128]{1,0:T(8,128)(2,1)} %get-tuple-element.72), channel_id=1, source_target_pairs={{0,4},{1,5},{2,6},{3,7},{4,0},{5,1},{6,2},{7,3},{8,12},{9,13},{10,... | collective-permute-start | bytes 995336 | tf_op jit(solution)/shard_map/ppermute | solution.py:467
  10.0 32.5 %collective-permute-start.6 = (bf16[1296,128]{1,0:T(8,128)(2,1)}, bf16[1296,128]{1,0:T(8,128)(2,1)S(1)}, u32[]{:S(2)}, u32[]{:S(2)}) collective-permute-start(bf16[1296,128]{1,0:T(8,128)(2,1)} %get-tuple-element.75), channel_id=1, source_target_pairs={{0,6},{1,7},{2,4},{3,5},{4,2},{5,3},{6,0},{7,1},{8,14},{9,15},{10,... | collective-permute-start | bytes 995336 | tf_op jit(solution)/shard_map/ppermute | solution.py:467
  15.2 27.3 %collective-permute-start.4 = (bf16[1296,128]{1,0:T(8,128)(2,1)}, bf16[1296,128]{1,0:T(8,128)(2,1)S(1)}, u32[]{:S(2)}, u32[]{:S(2)}) collective-permute-start(bf16[1296,128]{1,0:T(8,128)(2,1)} %get-tuple-element.70), channel_id=1, source_target_pairs={{0,2},{1,3},{2,0},{3,1},{4,6},{5,7},{6,4},{7,5},{8,10},{9,11},{10,... | collective-permute-start | bytes 995336 | tf_op jit(solution)/shard_map/ppermute | solution.py:467
  25.3 29.1 %collective-permute-start.7 = (bf16[144,512]{1,0:T(8,128)(2,1)S(1)}, bf16[144,512]{1,0:T(8,128)(2,1)S(1)}, u32[]{:S(2)}, u32[]{:S(2)}) collective-permute-start(bf16[144,512]{1,0:T(8,128)(2,1)S(1)} %get-tuple-element.67), channel_id=1, source_target_pairs={{0,8},{8,0},{1,9},{9,1},{2,10},{10,2},{3,11},{11,3},{4,12},{12,4},... | collective-permute-start | bytes 442376 | tf_op jit(solution)/shard_map/ppermute | solution.py:518
  33.0 21.4 %collective-permute-start.8 = (bf16[144,512]{1,0:T(8,128)(2,1)S(1)}, bf16[144,512]{1,0:T(8,128)(2,1)S(1)}, u32[]{:S(2)}, u32[]{:S(2)}) collective-permute-start(bf16[144,512]{1,0:T(8,128)(2,1)S(1)} %get-tuple-element.90), channel_id=1, source_target_pairs={{0,8},{9,1},{2,10},{11,3},{4,12},{13,5},{6,14},{15,7},{16,24},{25,... | collective-permute-start | bytes 442376 | tf_op jit(solution)/shard_map/ppermute | solution.py:518
  37.2 5.4 %copy-start = (bf16[1296,128]{1,0:T(8,128)(2,1)S(1)}, bf16[1296,128]{1,0:T(8,128)(2,1)}, u32[]{:S(2)}) copy-start(bf16[1296,128]{1,0:T(8,128)(2,1)} %get-tuple-element.68.refs_0_) | copy-start | bytes 995332
  44.0 10.4 %collective-permute-start.9 = (bf16[144,512]{1,0:T(8,128)(2,1)S(1)}, bf16[144,512]{1,0:T(8,128)(2,1)S(1)}, u32[]{:S(2)}, u32[]{:S(2)}) collective-permute-start(bf16[144,512]{1,0:T(8,128)(2,1)S(1)} %get-tuple-element.91), channel_id=1, source_target_pairs={{0,8},{8,0},{1,9},{9,1},{2,10},{10,2},{3,11},{11,3},{4,12},{12,4},... | collective-permute-start | bytes 442376 | tf_op jit(solution)/shard_map/ppermute | solution.py:518
  44.1 11.9 %collective-permute-start.10 = (bf16[144,512]{1,0:T(8,128)(2,1)S(1)}, bf16[144,512]{1,0:T(8,128)(2,1)S(1)}, u32[]{:S(2)}, u32[]{:S(2)}) collective-permute-start(bf16[144,512]{1,0:T(8,128)(2,1)S(1)} %get-tuple-element.95), channel_id=1, source_target_pairs={{1,9},{8,0},{3,11},{10,2},{5,13},{12,4},{7,15},{14,6},{17,25},{24,... | collective-permute-start | bytes 442376 | tf_op jit(solution)/shard_map/ppermute | solution.py:518
  58.4 7.8 %collective-permute-start.11 = (bf16[784,128]{1,0:T(8,128)(2,1)S(1)}, bf16[784,128]{1,0:T(8,128)(2,1)S(1)}, u32[]{:S(2)}, u32[]{:S(2)}) collective-permute-start(bf16[784,128]{1,0:T(8,128)(2,1)S(1)} %get-tuple-element.97), channel_id=1, source_target_pairs={{0,2},{1,3},{2,0},{3,1},{4,6},{5,7},{6,4},{7,5},{8,10},{9,11},{10,... | collective-permute-start | bytes 602120 | tf_op jit(solution)/shard_map/ppermute | solution.py:467
  59.1 7.1 %collective-permute-start.12 = (bf16[784,128]{1,0:T(8,128)(2,1)S(1)}, bf16[784,128]{1,0:T(8,128)(2,1)S(1)}, u32[]{:S(2)}, u32[]{:S(2)}) collective-permute-start(bf16[784,128]{1,0:T(8,128)(2,1)S(1)} %get-tuple-element.98), channel_id=1, source_target_pairs={{0,4},{1,5},{2,6},{3,7},{4,0},{5,1},{6,2},{7,3},{8,12},{9,13},{10,... | collective-permute-start | bytes 602120 | tf_op jit(solution)/shard_map/ppermute | solution.py:467
  59.1 10.3 %collective-permute-start.13 = (bf16[784,128]{1,0:T(8,128)(2,1)S(1)}, bf16[784,128]{1,0:T(8,128)(2,1)S(1)}, u32[]{:S(2)}, u32[]{:S(2)}) collective-permute-start(bf16[784,128]{1,0:T(8,128)(2,1)S(1)} %get-tuple-element.99), channel_id=1, source_target_pairs={{0,6},{1,7},{2,4},{3,5},{4,2},{5,3},{6,0},{7,1},{8,14},{9,15},{10,... | collective-permute-start | bytes 602120 | tf_op jit(solution)/shard_map/ppermute | solution.py:467
  64.0 9.8 %collective-permute-start.15 = (bf16[784,128]{1,0:T(8,128)(2,1)S(1)}, bf16[784,128]{1,0:T(8,128)(2,1)S(1)}, u32[]{:S(2)}, u32[]{:S(2)}) collective-permute-start(bf16[784,128]{1,0:T(8,128)(2,1)S(1)} %get-tuple-element.112), channel_id=1, source_target_pairs={{0,3},{1,2},{2,1},{3,0},{4,7},{5,6},{6,5},{7,4},{8,11},{9,10},{10,... | collective-permute-start | bytes 602120 | tf_op jit(solution)/shard_map/ppermute | solution.py:467
  64.1 9.7 %collective-permute-start.16 = (bf16[784,128]{1,0:T(8,128)(2,1)S(1)}, bf16[784,128]{1,0:T(8,128)(2,1)S(1)}, u32[]{:S(2)}, u32[]{:S(2)}) collective-permute-start(bf16[784,128]{1,0:T(8,128)(2,1)S(1)} %get-tuple-element.113), channel_id=1, source_target_pairs={{0,5},{1,4},{2,7},{3,6},{4,1},{5,0},{6,3},{7,2},{8,13},{9,12},{10,... | collective-permute-start | bytes 602120 | tf_op jit(solution)/shard_map/ppermute | solution.py:467
  66.2 9.7 %collective-permute-start.17 = (bf16[784,128]{1,0:T(8,128)(2,1)S(1)}, bf16[784,128]{1,0:T(8,128)(2,1)S(1)}, u32[]{:S(2)}, u32[]{:S(2)}) collective-permute-start(bf16[784,128]{1,0:T(8,128)(2,1)S(1)} %get-tuple-element.115), channel_id=1, source_target_pairs={{0,7},{1,6},{2,5},{3,4},{4,3},{5,2},{6,1},{7,0},{8,15},{9,14},{10,... | collective-permute-start | bytes 602120 | tf_op jit(solution)/shard_map/ppermute | solution.py:467
  66.2 9.7 %collective-permute-start.14 = (bf16[784,128]{1,0:T(8,128)(2,1)S(1)}, bf16[784,128]{1,0:T(8,128)(2,1)S(1)}, u32[]{:S(2)}, u32[]{:S(2)}) collective-permute-start(bf16[784,128]{1,0:T(8,128)(2,1)S(1)} %get-tuple-element.111), channel_id=1, source_target_pairs={{0,1},{1,0},{2,3},{3,2},{4,5},{5,4},{6,7},{7,6},{8,9},{9,8},{10,11... | collective-permute-start | bytes 602120 | tf_op jit(solution)/shard_map/ppermute | solution.py:467
